TPU v7x, 32 devices: a whole 2x2x4 slice. The times are simulated.
32 devices in a mesh: section: 2 (over core), batch: 16 (over z, y, x).
Axes of the slice: x: 2, y: 2, z: 4, core: 2. Of those that a mesh axis runs over, the one named last changes fastest.
Arguments:
- x_q: bfloat16 [32, 32, 768], P('batch'), may hold values from -6 to 6
- x_p: bfloat16 [96, 128, 768], P('batch'), may hold values from -6 to 6
- len_q: int32 [32], P('batch'), may hold values from 4 to 32
- len_p: int32 [96], P('batch'), may hold values from 20 to 128
- cot_q: bfloat16 [32, 32, 768], P('batch'), may hold values from -6 to 6
- cot_p: bfloat16 [96, 128, 768], P('batch'), may hold values from -6 to 6
- positive: int32 [32], replicated, may hold values from 0 to 95, as said below
- micro: int32 [32], replicated, may hold values from 0 to 1, as said below
- w_qkv: bfloat16 [2, 2, 768, 2304], P('section'), may hold values from -0.21875 to 0.21875
- w_out: bfloat16 [2, 2, 768, 768], P('section'), may hold values from -0.875 to 0.875
- w_up: bfloat16 [2, 2, 768, 3072], P('section'), may hold values from -0.21875 to 0.21875
- w_down: bfloat16 [2, 2, 3072, 768], P('section'), may hold values from -0.109375 to 0.109375
- norm_gain: float32 [2, 2, 2, 768], P('section'), may hold values from 0.5 to 1.5
- biases: float32 [2, 2, 6, 768], P('section'), may hold values from -1.8 to 1.8
- b_up: float32 [2, 2, 3072], P('section'), may hold values from -1.8 to 1.8
Outputs:
- hidden_q: bfloat16 [2, 32, 32, 768], P('section', 'batch')
- hidden_p: bfloat16 [2, 96, 128, 768], P('section', 'batch')
- grad_q: float32 [2, 32, 32, 768], P('section', 'batch')
- grad_p: float32 [2, 96, 128, 768], P('section', 'batch')
- query_loss: float32 [32], P('batch')
- g_qkv: float32 [2, 2, 768, 2304], P('section', None, 'batch')
- g_out: float32 [2, 2, 768, 768], P('section', None, 'batch')
- g_up: float32 [2, 2, 768, 3072], P('section', None, 'batch')
- g_down: float32 [2, 2, 3072, 768], P('section', None, 'batch')
- g_gain: float32 [2, 2, 2, 768], P('section', None, None, 'batch')
- g_bias: float32 [2, 2, 6, 768], P('section', None, None, 'batch')
- g_bup: float32 [2, 2, 3072], P('section', None, 'batch')
- g_qbias: float32 [2, 2, 768], P('section', None, 'batch')
Inputs may be any that keep to these rules, and one draw needn't show every extreme that they name: positive[q] is one of 3 q, 3 q + 1, 3 q + 2: a query's own passage and its two hard negatives. Each aligned block of 2 queries (the queries of one index of batch) holds exactly 1 query of each micro-batch.
All inputs are finite; a program needn't handle non-finite values.
Results may differ from a plain program's by a relative error of at most 0.02.
Values may be sent and summed in bfloat16 or wider, within the bound.
No kernel may reach another device: no remote copies, remote signals or barrier semaphores. Data moves between devices by JAX's collectives and lax.ppermute only.
A program may use at most 448 MiB of HBM per device.

v0:
```python
from functools import partial

import jax
import jax.numpy as jnp
from jax import lax
from jax.sharding import PartitionSpec as P

HEADS = 12
HEAD_DIM = 64


NORM_EPS = 1e-05
SQRT_HALF = 0.7071067811865476
ROOT_TAU_INV = 0.3989422804014327
MASK_FILL = -1e30
LOGIT_GAIN = 2.5
PRECISE = lax.Precision.HIGHEST


def passed_along(block, axis, distance):
    devices = range(lax.axis_size(axis))
    route = [(i - distance, i) for i in devices if i - distance in devices]
    return lax.ppermute(block, axis, route)


def outer_sum(left, right):
    return lax.dot_general(
        left, right, (((0,), (0,)), ((), ())), preferred_element_type=jnp.float32
    )


def times_transposed(left, right):
    return lax.dot_general(
        left, right, (((1,), (1,)), ((), ())), preferred_element_type=jnp.float32
    )


def norm_rows(values, scale_gain, shift_bias):
    center = values - jnp.mean(values, axis=-1, keepdims=True)
    inverse = lax.rsqrt(jnp.mean(center * center, axis=-1, keepdims=True) + NORM_EPS)
    normed = center * inverse
    return (normed * scale_gain + shift_bias, normed, inverse)


def norm_back(upstream, normed, inverse, scale_gain):
    scaled = upstream * scale_gain
    return inverse * (
        scaled
        - jnp.mean(scaled, axis=-1, keepdims=True)
        - normed * jnp.mean(scaled * normed, axis=-1, keepdims=True)
    )


def gelu_value(values):
    return 0.5 * values * (1.0 + jax.scipy.special.erf(values * SQRT_HALF))


def gelu_slope(values):
    return (
        0.5 * (1.0 + jax.scipy.special.erf(values * SQRT_HALF))
        + values * jnp.exp(-0.5 * values * values) * ROOT_TAU_INV
    )


def soft_scores(query_rows, key_rows, lengths):
    scores = jnp.einsum(
        "nqhd,nkhd->nhqk", query_rows, key_rows, preferred_element_type=jnp.float32
    ) * HEAD_DIM ** (-0.5)
    valid_keys = jnp.arange(scores.shape[-1])[None, :] < lengths[:, None]
    scores = jnp.where(valid_keys[:, None, None, :], scores, MASK_FILL)
    exponent = jnp.exp(scores - jnp.max(scores, axis=-1, keepdims=True))
    return exponent / jnp.sum(exponent, axis=-1, keepdims=True)


def block_forward(weights, block_rows, lengths):
    w_qkv, w_out, w_up, w_down, norm_gains, biases, b_up = weights
    seq_count, seq_slots, model_width = block_rows.shape
    flat_rows = block_rows.reshape(seq_count * seq_slots, model_width)
    projected = jnp.dot(flat_rows, w_qkv, preferred_element_type=jnp.float32)
    shape_heads = (seq_count, seq_slots, HEADS, HEAD_DIM)
    query_rows = (projected[:, :model_width] + biases[0]).astype(jnp.bfloat16).reshape(shape_heads)
    key_rows = projected[:, model_width : 2 * model_width].astype(jnp.bfloat16).reshape(shape_heads)
    value_rows = (
        (projected[:, 2 * model_width :] + biases[1]).astype(jnp.bfloat16).reshape(shape_heads)
    )
    soft_weights = soft_scores(query_rows, key_rows, lengths)
    mixed_rows = jnp.einsum(
        "nhqk,nkhd->nqhd",
        soft_weights.astype(jnp.bfloat16),
        value_rows,
        preferred_element_type=jnp.float32,
    )
    mixed_rows = mixed_rows.reshape(flat_rows.shape).astype(jnp.bfloat16)
    summed = flat_rows.astype(jnp.float32) + (
        jnp.dot(mixed_rows, w_out, preferred_element_type=jnp.float32) + biases[2]
    )
    first_norm, first_hat, first_inv = norm_rows(summed, norm_gains[0], biases[3])
    first_low = first_norm.astype(jnp.bfloat16)
    hidden = jnp.dot(first_low, w_up, preferred_element_type=jnp.float32) + b_up
    active = gelu_value(hidden).astype(jnp.bfloat16)
    second = first_norm + (jnp.dot(active, w_down, preferred_element_type=jnp.float32) + biases[4])
    output, out_hat, out_inv = norm_rows(second, norm_gains[1], biases[5])
    kept_values = (
        flat_rows,
        query_rows,
        key_rows,
        value_rows,
        soft_weights,
        mixed_rows,
        first_hat,
        first_inv,
        first_low,
        hidden,
        active,
        out_hat,
        out_inv,
    )
    return (output.reshape(block_rows.shape), kept_values)


def block_backward(weights, block_rows, lengths, upstream):
    w_qkv, w_out, w_up, w_down, norm_gains, biases, b_up = weights
    _, kept_values = block_forward(weights, block_rows, lengths)
    (
        flat_rows,
        query_rows,
        key_rows,
        value_rows,
        soft_weights,
        mixed_rows,
        first_hat,
        first_inv,
        first_low,
        hidden,
        active,
        out_hat,
        out_inv,
    ) = kept_values
    model_width = flat_rows.shape[1]
    grad_rows = upstream.reshape(flat_rows.shape)
    d_gain_out = jnp.sum(grad_rows * out_hat, axis=0)
    d_shift_out = jnp.sum(grad_rows, axis=0)
    d_second = norm_back(grad_rows, out_hat, out_inv, norm_gains[1])
    d_branch_ffn = d_second.astype(jnp.bfloat16)
    d_bias_ffn = jnp.sum(d_branch_ffn.astype(jnp.float32), axis=0)
    d_down = outer_sum(active, d_branch_ffn)
    d_hidden = (times_transposed(d_branch_ffn, w_down) * gelu_slope(hidden)).astype(jnp.bfloat16)
    d_bias_up = jnp.sum(d_hidden.astype(jnp.float32), axis=0)
    d_up = outer_sum(first_low, d_hidden)
    d_first = d_second + times_transposed(d_hidden, w_up)
    d_gain_first = jnp.sum(d_first * first_hat, axis=0)
    d_shift_first = jnp.sum(d_first, axis=0)
    d_summed = norm_back(d_first, first_hat, first_inv, norm_gains[0])
    d_branch = d_summed.astype(jnp.bfloat16)
    d_bias_out = jnp.sum(d_branch.astype(jnp.float32), axis=0)
    d_out = outer_sum(mixed_rows, d_branch)
    d_mixed = times_transposed(d_branch, w_out).astype(jnp.bfloat16).reshape(query_rows.shape)
    d_soft = jnp.einsum("nqhd,nkhd->nhqk", d_mixed, value_rows, preferred_element_type=jnp.float32)
    d_value = jnp.einsum(
        "nhqk,nqhd->nkhd",
        soft_weights.astype(jnp.bfloat16),
        d_mixed,
        preferred_element_type=jnp.float32,
    )
    d_scores = (
        soft_weights * (d_soft - jnp.sum(d_soft * soft_weights, axis=-1, keepdims=True))
    ).astype(jnp.bfloat16)
    head_scale = HEAD_DIM ** (-0.5)
    d_query = (
        jnp.einsum("nhqk,nkhd->nqhd", d_scores, key_rows, preferred_element_type=jnp.float32)
        * head_scale
    )
    d_key = (
        jnp.einsum("nhqk,nqhd->nkhd", d_scores, query_rows, preferred_element_type=jnp.float32)
        * head_scale
    )
    d_proj = jnp.concatenate(
        [
            member.astype(jnp.bfloat16).reshape(flat_rows.shape)
            for member in (d_query, d_key, d_value)
        ],
        axis=1,
    )
    d_bias_query = jnp.sum(d_proj[:, :model_width].astype(jnp.float32), axis=0)
    d_bias_value = jnp.sum(d_proj[:, 2 * model_width :].astype(jnp.float32), axis=0)
    d_qkv = outer_sum(flat_rows, d_proj)
    d_input = d_summed + times_transposed(d_proj, w_qkv)
    d_gains = jnp.stack([d_gain_first, d_gain_out])
    d_biases = jnp.stack(
        [d_bias_query, d_bias_value, d_bias_out, d_shift_first, d_bias_ffn, d_shift_out]
    )
    return (
        d_input.reshape(block_rows.shape),
        (d_qkv, d_out, d_up, d_down, d_gains, d_biases, d_bias_up),
    )


def join_rows(pair_rows):
    return jnp.concatenate([member.reshape(-1, member.shape[-1]) for member in pair_rows], 0)


def split_rows(flat_rows, like):
    boundary = like[0].shape[0] * like[0].shape[1]
    return (
        flat_rows[:boundary].reshape(like[0].shape),
        flat_rows[boundary:].reshape(like[1].shape),
    )


def select_section(is_first, early_pair, late_pair):
    return tuple(
        (
            jnp.where(is_first, early_item, late_item)
            for early_item, late_item in zip(early_pair, late_pair)
        )
    )


def take_part(pair_rows):
    return tuple((member for member in pair_rows))


def glue_parts(pieces):
    return tuple(
        (jnp.concatenate([piece[tower_id] for piece in pieces], 0) for tower_id in range(2))
    )


def seed_grad(cotangent, lengths, cls_grad):
    valid_rows = (jnp.arange(cotangent.shape[1])[None, :] < lengths[:, None]).astype(jnp.float32)
    grad_rows = cotangent.astype(jnp.float32) * valid_rows[:, :, None]
    return grad_rows.at[:, 0, :].add(cls_grad)


def forward_work(towers, rows_pair, lengths_pair):
    return tuple(
        (
            block_forward(towers[tower_id], rows_pair[tower_id], lengths_pair[tower_id])[0].astype(
                jnp.bfloat16
            )
            for tower_id in range(2)
        )
    )


def zero_forward(rows_pair):
    return tuple((jnp.zeros(member.shape, jnp.bfloat16) for member in rows_pair))


def backward_work(towers, rows_pair, lengths_pair, incoming):
    outcome = [
        block_backward(
            towers[tower_id], rows_pair[tower_id], lengths_pair[tower_id], incoming[tower_id]
        )
        for tower_id in range(2)
    ]
    row_grads = (outcome[0][0], outcome[1][0])
    step_grads = tuple(
        (
            jnp.stack([outcome[0][1][grad_kind], outcome[1][1][grad_kind]])[None]
            for grad_kind in range(7)
        )
    )
    return (row_grads, step_grads)


def zero_backward(rows_pair, weight_sets):
    return (
        tuple((jnp.zeros(member.shape, jnp.float32) for member in rows_pair)),
        tuple((jnp.zeros(member.shape, jnp.float32) for member in weight_sets)),
    )


def shards(
    x_q,
    x_p,
    len_q,
    len_p,
    cot_q,
    cot_p,
    positive,
    micro,
    w_qkv,
    w_out,
    w_up,
    w_down,
    norm_gain,
    biases,
    b_up,
):
    is_first = lax.axis_index("section") == 0
    batch_index = lax.axis_index("batch")
    batch_size = lax.axis_size("batch")
    weight_sets = (w_qkv, w_out, w_up, w_down, norm_gain, biases, b_up)
    towers = [tuple((member[0, tower_id] for member in weight_sets)) for tower_id in range(2)]
    part_count = 1
    query_count = x_q.shape[0]
    piece_queries = query_count // part_count
    places = jnp.arange(query_count, dtype=jnp.int32)
    triple = jnp.arange(3, dtype=jnp.int32)
    label_grid = micro.reshape(batch_size, query_count)
    order_all = jnp.argsort(label_grid * query_count + places[None, :], axis=1)
    order = lax.dynamic_index_in_dim(order_all, batch_index, 0, keepdims=False)
    inverse = jnp.argsort(order)
    passage_order = (3 * order[:, None] + triple[None, :]).reshape(-1)
    passage_inverse = (3 * inverse[:, None] + triple[None, :]).reshape(-1)
    sorted_labels = jnp.take_along_axis(label_grid, order_all, axis=1)
    global_ids = jnp.arange(batch_size * query_count, dtype=jnp.int32).reshape(
        batch_size, query_count
    )
    offset_grid = positive.reshape(batch_size, query_count) - 3 * global_ids
    sorted_offsets = jnp.take_along_axis(offset_grid, order_all, axis=1)
    inputs = (jnp.take(x_q, order, axis=0), jnp.take(x_p, passage_order, axis=0))
    lengths = (jnp.take(len_q, order, axis=0), jnp.take(len_p, passage_order, axis=0))
    cotangents = (jnp.take(cot_q, order, axis=0), jnp.take(cot_p, passage_order, axis=0))
    early_out = [None] * part_count
    late_in = [None] * part_count
    late_out = [None] * part_count
    out_grad = [None] * part_count
    loss_parts = [None] * part_count
    early_grad = [None] * part_count
    late_grad = [None] * part_count
    outgoing = None
    back_sent = None
    summed_local = None
    reduced = None
    for step_index in range(part_count + 2):
        if step_index <= part_count:
            late_index = max(step_index - 1, 0)
            own_rows = take_part(inputs)
            own_len = take_part(lengths)
            late_len = take_part(lengths)
            arrived = own_rows
            if step_index >= 1:
                arrived = split_rows(passed_along(outgoing, "section", 1), own_rows)
            if step_index == 0:
                result = lax.cond(
                    is_first,
                    partial(forward_work, towers, own_rows, own_len),
                    partial(zero_forward, own_rows),
                )
            else:
                result = lax.cond(
                    is_first,
                    partial(zero_forward, own_rows),
                    partial(forward_work, towers, arrived, late_len),
                )
            outgoing = join_rows(result)
            if step_index < part_count:
                early_out[step_index] = result
            if step_index >= 1:
                late_in[step_index - 1] = arrived
                late_out[step_index - 1] = result
                all_q = lax.all_gather(result[0][:, 0, :], ("section", "batch"), axis=0, tiled=True)
                all_p = lax.all_gather(result[1][:, 0, :], ("section", "batch"), axis=0, tiled=True)
                all_q = all_q[all_q.shape[0] // 2 :]
                all_p = all_p[all_p.shape[0] // 2 :]
                labels = sorted_labels.reshape(-1)
                offsets = sorted_offsets.reshape(-1)
                logit_scale = LOGIT_GAIN * all_q.shape[1] ** (-0.5)
                logits = times_transposed(all_q, all_p) * logit_scale
                same_group = labels[:, None] == jnp.repeat(labels, 3)[None, :]
                logits = jnp.where(same_group, logits, MASK_FILL)
                row_top = jnp.max(logits, axis=-1, keepdims=True)
                exponent = jnp.exp(logits - row_top)
                totals = jnp.sum(exponent, axis=-1, keepdims=True)
                wanted = 3 * jnp.arange(all_q.shape[0], dtype=jnp.int32) + offsets
                target = jnp.arange(all_p.shape[0], dtype=jnp.int32)[None, :] == wanted[:, None]
                loss_all = (
                    row_top[:, 0]
                    + jnp.log(totals[:, 0])
                    - jnp.sum(jnp.where(target, logits, 0.0), axis=-1)
                )
                coefficient = (exponent / totals - target.astype(jnp.float32)) * logit_scale
                d_all_q = jnp.dot(coefficient, all_p.astype(jnp.float32), precision=PRECISE)
                d_all_p = lax.dot_general(
                    coefficient,
                    all_q.astype(jnp.float32),
                    (((0,), (0,)), ((), ())),
                    precision=PRECISE,
                )
                d_cls_q = lax.dynamic_slice_in_dim(
                    d_all_q, batch_index * piece_queries, piece_queries, 0
                )
                d_cls_p = lax.dynamic_slice_in_dim(
                    d_all_p, batch_index * 3 * piece_queries, 3 * piece_queries, 0
                )
                loss_own = lax.dynamic_slice_in_dim(
                    loss_all, batch_index * piece_queries, piece_queries, 0
                )
                loss_own, d_cls_q, d_cls_p = (loss_own, d_cls_q, d_cls_p)
                loss_parts[step_index - 1] = loss_own
                cot_piece = take_part(cotangents)
                len_piece = take_part(lengths)
                out_grad[step_index - 1] = (
                    seed_grad(cot_piece[0], len_piece[0], d_cls_q),
                    seed_grad(cot_piece[1], len_piece[1], d_cls_p),
                )
        if step_index >= 1:
            late_index = min(step_index - 1, part_count - 1)
            late_rows = late_in[late_index]
            late_len = take_part(lengths)
            early_rows = take_part(inputs)
            early_len = take_part(lengths)
            arrived_grad = out_grad[late_index]
            if step_index >= 2:
                arrived_low = split_rows(passed_along(back_sent, "section", -1), early_rows)
                arrived_grad = tuple((member.astype(jnp.float32) for member in arrived_low))
            if step_index == 1:
                outcome = lax.cond(
                    is_first,
                    partial(zero_backward, late_rows, weight_sets),
                    partial(backward_work, towers, late_rows, late_len, out_grad[late_index]),
                )
            else:
                outcome = lax.cond(
                    is_first,
                    partial(backward_work, towers, early_rows, early_len, arrived_grad),
                    partial(zero_backward, early_rows, weight_sets),
                )
            row_grads, step_grads = outcome
            sent_grads = tuple((member.astype(jnp.bfloat16) for member in row_grads))
            back_sent = join_rows(sent_grads)
            if step_index <= part_count:
                late_grad[step_index - 1] = tuple(
                    (member.astype(jnp.float32) for member in sent_grads)
                )
            if step_index >= 2:
                early_grad[step_index - 2] = row_grads
            summed_local = (
                step_grads
                if summed_local is None
                else tuple(
                    (
                        total_item + step_item
                        for total_item, step_item in zip(summed_local, step_grads)
                    )
                )
            )
    reduced = (
        lax.psum_scatter(summed_local[0], "batch", scatter_dimension=2, tiled=True),
        lax.psum_scatter(summed_local[1], "batch", scatter_dimension=2, tiled=True),
        lax.psum_scatter(summed_local[2], "batch", scatter_dimension=2, tiled=True),
        lax.psum_scatter(summed_local[3], "batch", scatter_dimension=2, tiled=True),
        lax.psum_scatter(summed_local[4], "batch", scatter_dimension=3, tiled=True),
        lax.psum_scatter(summed_local[5], "batch", scatter_dimension=3, tiled=True),
        lax.psum_scatter(summed_local[6], "batch", scatter_dimension=2, tiled=True),
    )
    sorted_hidden = glue_parts([select_section(is_first, early_out[0], late_out[0])])
    sorted_grads = glue_parts([select_section(is_first, early_grad[0], late_grad[0])])
    hidden_q = jnp.take(sorted_hidden[0], inverse, axis=0)
    hidden_p = jnp.take(sorted_hidden[1], passage_inverse, axis=0)
    grad_rows_q = jnp.take(sorted_grads[0], inverse, axis=0)
    grad_rows_p = jnp.take(sorted_grads[1], passage_inverse, axis=0)
    loss_own = jnp.take(loss_parts[0], inverse, axis=0)
    query_bias_grad = reduced[5][:, :, 0, :]
    return (
        (hidden_q[None], hidden_p[None], grad_rows_q[None], grad_rows_p[None], loss_own)
        + tuple(reduced)
        + (query_bias_grad,)
    )


def solution(mesh):
    return jax.shard_map(
        shards,
        mesh=mesh,
        in_specs=(
            P("batch", None, None),
            P("batch", None, None),
            P("batch"),
            P("batch"),
            P("batch", None, None),
            P("batch", None, None),
            P(),
            P(),
            P("section", None, None, None),
            P("section", None, None, None),
            P("section", None, None, None),
            P("section", None, None, None),
            P("section", None, None, None),
            P("section", None, None, None),
            P("section", None, None),
        ),
        out_specs=(
            P("section", "batch", None, None),
            P("section", "batch", None, None),
            P("section", "batch", None, None),
            P("section", "batch", None, None),
            P("batch"),
            P("section", None, "batch", None),
            P("section", None, "batch", None),
            P("section", None, "batch", None),
            P("section", None, "batch", None),
            P("section", None, None, "batch"),
            P("section", None, None, "batch"),
            P("section", None, "batch"),
            P("section", None, "batch"),
        ),
        check_vma=False,
    )
```

profile of v0, /device:TPU:0, one launch (start us, length us, event | category | flops | bytes accessed | tf_op | source)
XLA Modules:
  0.0 2141.7 jit_solution(13909919688011162533)
XLA Ops:
  15.2 6.6 slice_bitcast_fusion.4
  24.2 8.2 slice_bitcast_fusion.1
  33.0 8.0 slice_bitcast_fusion
  51.2 69.9 %conditional.4 = (bf16[2,32,768]{2,1,0:T(8,128)(2,1)}, bf16[6,128,768]{2,1,0:T(8,128)(2,1)}, bf16[64,768]{1,0:T(8,128)(2,1)}, bf16[768,768]{1,0:T(8,128)(2,1)S(1)}) conditional(s32[]{:T(128)} %convert_element_type.625, () %tuple.79, (bf16[2,32,768]{2,1,0:T(8,128)(2,1)S(1)}, bf16[768,2304]{1,0:T(8,128)(2,1)S(1)}, f32[6,768]{1,0:T(8,128)S(1)}, ...), branch_computations={%region_1.0_spmd, %region_2.17_spmd} | conditional | flops 12134477824 | bytes 166706080 | solution.py:337
  54.7 5.8 fusion.365
  62.2 4.9 fusion.419
  67.1 2.9 copy-done.22
  70.2 3.3 reshape.1244
  76.2 3.3 reshape.1243
  79.5 4.6 fusion.5
  84.2 3.1 fusion.368
  87.3 3.6 reshape.1242
  91.0 4.1 fusion.17
  99.9 14.4 fusion.370
  134.4 4.5 conditional.5
  139.0 136.3 %all-gather.1 = bf16[192,1,768]{2,1,0:T(2,128)(2,1)S(1)} all-gather(bf16[6,1,768]{2,1,0:T(2,128)(2,1)S(1)} %slice.441), channel_id=3, replica_groups=mesh['section'=2,'batch'=16] {'section','batch'}, dimensions={0}, use_global_device_ids=true | all-gather | bytes 304128 | tf_op jit(solution)/shard_map/all_gather | solution.py:355
  276.3 64.4 %all-gather = bf16[64,1,768]{2,1,0:T(2,128)(2,1)S(1)} all-gather(bf16[2,1,768]{2,1,0:T(2,128)(2,1)S(1)} %slice.439), channel_id=2, replica_groups=mesh['section'=2,'batch'=16] {'section','batch'}, dimensions={0}, use_global_device_ids=true | all-gather | bytes 101376 | tf_op jit(solution)/shard_map/all_gather | solution.py:354
  346.3 35.0 %conditional.6 = (f32[1,2,768,768]{3,2,1,0:T(8,128)}, f32[1,2,768,3072]{3,2,1,0:T(8,128)}, f32[1,2,3072,768]{3,2,1,0:T(8,128)}, f32[1,2,2,768]{3,2,1,0:T(2,128)}...) conditional(s32[]{:T(128)} %convert_element_type.625, ...), branch_computations={%region_32.76_spmd, %region_73.77_spmd} | conditional | flops 36403179520 | bytes 822113152 | solution.py:410
  355.2 8.7 broadcast.1073
  363.9 7.7 broadcast.1074
  374.6 6.0 broadcast.1071.clone
  382.8 210.2 %collective-permute-done.1 = bf16[832,768]{1,0:T(8,128)(2,1)} collective-permute-done((bf16[832,768]{1,0:T(8,128)(2,1)S(1)}, bf16[832,768]{1,0:T(8,128)(2,1)}, u32[]{:S(2)}, u32[]{:S(2)}) %collective-permute-start.1) | collective-permute-done | bytes 1277984 | tf_op jit(solution)/shard_map/ppermute | solution.py:23
  593.1 210.3 %conditional.7 = (f32[2,32,768]{2,1,0:T(8,128)S(1)}, f32[6,128,768]{2,1,0:T(8,128)}, f32[1,2,768,768]{3,2,1,0:T(8,128)}, f32[1,2,768,3072]{3,2,1,0:T(8,128)}, f3...) conditional(s32[]{:T(128)} %convert_element_type.625, () %tuple.83, ...), branch_computations={%region_74.78_spmd, %region_75.119_spmd} | conditional | flops 36401897472 | bytes 793294976 | solution.py:416
  598.8 3.5 convolution_add_fusion.12
  616.9 4.1 convolution_add_fusion.15
  621.6 2.9 fusion.423
  627.5 3.4 reshape.1258
  630.9 4.5 copy.395
  636.0 3.2 reshape.1259
  639.2 3.7 copy.393
  645.2 3.3 reshape.1260
  648.5 3.7 copy.394
  652.2 4.8 fusion.394
  657.0 3.4 fusion.264
  664.4 7.4 multiply_convert_fusion.12
  671.8 4.1 fusion.396
  676.6 3.0 fusion.257
  682.1 10.6 convert_reduce_fusion.10
  692.7 5.1 multiply_reduce_fusion.25
  702.9 4.6 reshape.1261
  707.6 4.9 copy.399
  712.5 4.1 multiply_reduce_fusion.24
  716.7 3.8 multiply_convert_fusion.13
  730.4 4.4 convolution_add_fusion.13
  740.0 4.2 convolution_bitcast_fusion.13
  745.7 7.1 maximum_bitcast_fusion.9
  752.9 4.1 convolution_bitcast_fusion.12
  758.6 6.8 maximum_bitcast_fusion.10
  766.7 4.9 convolution_bitcast_fusion.10
  771.5 4.0 convolution_bitcast_fusion.11
  775.6 10.9 maximum_bitcast_fusion.11
  786.6 15.4 copy.464
  815.6 6.5 add.1106
  822.2 15.5 add.1105
  837.8 19.4 add.1107
  857.3 19.7 add.1108
  890.4 3.4 broadcast_select_fusion.1
  899.7 28.8 %reduce-scatter.22.cloned.1.call-done = f32[48,4]{1,0:T(8,128)} async-done(((f32[768,4]{1,0:T(8,128)}), f32[48,4]{1,0:T(8,128)}) %reduce-scatter.22.cloned.1.call-update) | async-done | bytes 784
  929.9 127.8 %reduce-scatter.26.cloned.1.call-done = f32[192,2]{1,0:T(8,128)} async-done(((f32[3072,2]{1,0:T(8,128)}), f32[192,2]{1,0:T(8,128)}) %reduce-scatter.26.cloned.1.call-update) | async-done | bytes 1552
  1059.2 124.4 %reduce-scatter.24.cloned.1.call-done = f32[48,12]{1,0:T(8,128)} async-done(((f32[768,12]{1,0:T(8,128)}), f32[48,12]{1,0:T(8,128)}) %reduce-scatter.24.cloned.1.call-update) | async-done | bytes 2320
  1185.2 140.0 %reduce-scatter.16.cloned.1.call-done = f32[1,2,48,768]{3,2,1,0:T(8,128)} async-done(((f32[1,2,768,768]{3,2,1,0:T(8,128)}), f32[1,2,48,768]{3,2,1,0:T(8,128)}) %reduce-scatter.16.cloned.1.call-update) | async-done | bytes 294928 | tf_op jit(solution)/shard_map/reduce_scatter | solution.py:442
  1325.2 227.1 %reduce-scatter.14.cloned.1.call-done = f32[1,2,48,2304]{3,2,1,0:T(8,128)} async-done(((f32[1,2,768,2304]{3,2,1,0:T(8,128)}), f32[1,2,48,2304]{3,2,1,0:T(8,128)}) %reduce-scatter.14.cloned.1.call-update) | async-done | bytes 884752 | tf_op jit(solution)/shard_map/reduce_scatter | solution.py:441
  1552.3 291.4 %reduce-scatter.18.cloned.1.call-done = f32[1,2,48,3072]{3,2,1,0:T(8,128)} async-done(((f32[1,2,768,3072]{3,2,1,0:T(8,128)}), f32[1,2,48,3072]{3,2,1,0:T(8,128)}) %reduce-scatter.18.cloned.1.call-update) | async-done | bytes 1179664 | tf_op jit(solution)/shard_map/reduce_scatter | solution.py:443
  1843.7 290.9 %reduce-scatter.20.cloned.1.call-done = f32[1,2,192,768]{3,2,1,0:T(8,128)} async-done(((f32[1,2,3072,768]{3,2,1,0:T(8,128)}), f32[1,2,192,768]{3,2,1,0:T(8,128)}) %reduce-scatter.20.cloned.1.call-update) | async-done | bytes 1179664 | tf_op jit(solution)/shard_map/reduce_scatter | solution.py:444
  (560 shorter events, 162.8 us)
Async XLA Ops:
  7.2 35.0 %copy-start = (bf16[6,128,768]{2,1,0:T(8,128)(2,1)S(1)}, bf16[6,128,768]{2,1,0:T(8,128)(2,1)}, u32[]{:S(2)}) copy-start(bf16[6,128,768]{2,1,0:T(8,128)(2,1)} %param.38) | copy-start | bytes 3538948
  7.2 921.2 %reduce-scatter.22.cloned.1.call-start = ((), (), s32[]{:S(2)}) async-start(), calls=%async_computation.11 | async-start | bytes 417792
  8.8 13.1 copy-start.170
  8.9 12.9 copy-start.206
  15.2 7.3 copy-start.56
  24.2 8.2 copy-start.133
  33.0 8.0 copy-start.2
  54.7 7.5 copy-start.68
  123.2 7.3 collective-permute-start
  127.2 7.2 copy-start.90
  127.2 7.2 copy-start.95
  127.2 7.2 copy-start.98
  127.2 7.2 copy-start.112
  127.3 7.2 copy-start.117
  138.9 207.4 %copy-start.28 = (bf16[6,128,768]{2,1,0:T(8,128)(2,1)}, bf16[6,128,768]{2,1,0:T(8,128)(2,1)S(1)}, u32[]{:S(2)}) copy-start(bf16[6,128,768]{2,1,0:T(8,128)(2,1)S(1)} %get-tuple-element.496) | copy-start | bytes 3538948
  138.9 207.3 %copy-start.91 = (f32[6,768]{1,0:T(8,128)S(1)}, f32[6,768]{1,0:T(8,128)}, u32[]{:S(2)}) copy-start(f32[6,768]{1,0:T(8,128)} %get-tuple-element.792) | copy-start | bytes 55300
  138.9 207.3 %copy-start.113 = (f32[2,768]{1,0:T(2,128)S(1)}, f32[2,768]{1,0:T(2,128)}, u32[]{:S(2)}) copy-start(f32[2,768]{1,0:T(2,128)} %get-tuple-element.777) | copy-start | bytes 18436
  381.3 211.9 %copy-start.84 = (f32[2,32,768]{2,1,0:T(8,128)}, f32[2,32,768]{2,1,0:T(8,128)S(1)}, u32[]{:S(2)}) copy-start(f32[2,32,768]{2,1,0:T(8,128)S(1)} %get-tuple-element.500) | copy-start | bytes 589828
  381.3 211.8 %copy-start.42 = (bf16[2,32,768]{2,1,0:T(8,128)(2,1)S(1)}, bf16[2,32,768]{2,1,0:T(8,128)(2,1)}, u32[]{:S(2)}) copy-start(bf16[2,32,768]{2,1,0:T(8,128)(2,1)} %copy-done.41) | copy-start | bytes 294916
  381.3 211.8 %copy-start.92 = (f32[6,768]{1,0:T(8,128)S(1)}, f32[6,768]{1,0:T(8,128)}, u32[]{:S(2)}) copy-start(f32[6,768]{1,0:T(8,128)} %get-tuple-element.792) | copy-start | bytes 55300
  381.3 211.8 %copy-start.96 = (f32[6,768]{1,0:T(8,128)S(1)}, f32[6,768]{1,0:T(8,128)}, u32[]{:S(2)}) copy-start(f32[6,768]{1,0:T(8,128)} %copy-done.94) | copy-start | bytes 55300
  381.3 211.8 %copy-start.99 = (f32[1,1,3072]{2,1,0:T(1,128)S(1)}, f32[1,1,3072]{2,1,0:T(1,128)}, u32[]{:S(2)}) copy-start(f32[1,1,3072]{2,1,0:T(1,128)} %get-tuple-element.776) | copy-start | bytes 36868
  381.3 211.8 %copy-start.114 = (f32[2,768]{1,0:T(2,128)S(1)}, f32[2,768]{1,0:T(2,128)}, u32[]{:S(2)}) copy-start(f32[2,768]{1,0:T(2,128)} %get-tuple-element.777) | copy-start | bytes 18436
  381.3 211.8 %copy-start.118 = (f32[2,768]{1,0:T(2,128)S(1)}, f32[2,768]{1,0:T(2,128)}, u32[]{:S(2)}) copy-start(f32[2,768]{1,0:T(2,128)} %get-tuple-element.778) | copy-start | bytes 18436
  381.3 211.8 %copy-start.211 = (s32[2]{0:T(128)S(1)}, s32[2]{0:T(128)}, u32[]{:S(2)}) copy-start(s32[2]{0:T(128)} %get-tuple-element.635) | copy-start | bytes 28
  381.4 211.7 %collective-permute-start.1 = (bf16[832,768]{1,0:T(8,128)(2,1)S(1)}, bf16[832,768]{1,0:T(8,128)(2,1)}, u32[]{:S(2)}, u32[]{:S(2)}) collective-permute-start(bf16[832,768]{1,0:T(8,128)(2,1)S(1)} %pad_maximum_fusion.1), channel_id=1, source_target_pairs={{16,0},{17,1},{18,2},{19,3},{20,4},{21,5},{22,6},{23,7},{24,8},{25... | collective-permute-start | bytes 3833864 | tf_op jit(solution)/shard_map/ppermute | solution.py:23
  593.7 8.7 copy-start.104
  598.6 12.6 copy-start.128
  598.8 12.4 copy-start.134
  598.8 10.2 slice-start
  616.9 7.7 copy-start.54
  643.0 9.2 copy-start.34
  663.5 8.3 slice-start.8
  664.4 7.4 slice-start.9
  664.4 7.4 copy-start.192
  682.1 10.6 copy-start.57
  744.2 8.7 slice-start.20
  745.7 7.2 copy-start.58
  745.7 7.2 slice-start.21
  758.5 6.9 copy-start.150
  758.5 7.5 copy-start.124
  758.5 7.5 copy-start.169
  758.5 8.1 copy-start.72
  786.5 15.5 copy-start.127
  786.5 15.6 copy-start.181
  786.5 15.6 copy-start.154
  786.5 15.6 copy-start.195
  786.5 15.7 copy-start.160
  786.5 15.7 copy-start.159
  786.5 15.7 copy-start.177
  786.5 15.8 copy-start.178
  786.6 15.9 copy-start.147
  786.6 15.9 copy-start.146
  786.6 15.9 copy-start.143
  786.6 15.9 copy-start.142
  786.6 16.6 copy-start.86
  806.0 251.7 %reduce-scatter.26.cloned.1.call-start = ((), (), s32[]{:S(2)}) async-start(), calls=%async_computation.13 | async-start | bytes 1671168
  809.6 374.1 %reduce-scatter.24.cloned.1.call-start = ((), (), s32[]{:S(2)}) async-start(), calls=%async_computation.12 | async-start | bytes 417792
  815.5 509.7 %reduce-scatter.16.cloned.1.call-start = ((), (), s32[]{:S(2)}) async-start(), calls=%async_computation.8 | async-start | bytes 5013504 | tf_op jit(solution)/shard_map/reduce_scatter | solution.py:442
  822.1 730.1 %reduce-scatter.14.cloned.1.call-start = ((), (), s32[]{:S(2)}) async-start(), calls=%async_computation.7 | async-start | bytes 15040512 | tf_op jit(solution)/shard_map/reduce_scatter | solution.py:441
  837.7 1006.0 %reduce-scatter.18.cloned.1.call-start = ((), (), s32[]{:S(2)}) async-start(), calls=%async_computation.9 | async-start | bytes 20054016 | tf_op jit(solution)/shard_map/reduce_scatter | solution.py:443
  857.2 1277.3 %reduce-scatter.20.cloned.1.call-start = ((), (), s32[]{:S(2)}) async-start(), calls=%async_computation.10 | async-start | bytes 20054016 | tf_op jit(solution)/shard_map/reduce_scatter | solution.py:444
  896.2 1238.4 %copy-start.1 = (bf16[6,128,768]{2,1,0:T(8,128)(2,1)S(1)}, bf16[6,128,768]{2,1,0:T(8,128)(2,1)}, u32[]{:S(2)}) copy-start(bf16[6,128,768]{2,1,0:T(8,128)(2,1)} %param.38) | copy-start | bytes 3538948
  1184.6 949.9 %copy-start.172 = (f32[1,2,6,48]{3,1,2,0:T(2,128)}, f32[1,2,6,48]{3,1,2,0:T(2,128)S(1)}, u32[]{:S(2)}) copy-start(f32[1,2,6,48]{3,1,2,0:T(2,128)S(1)} %copy.456) | copy-start | bytes 6916
  (88 other events, 284.7 us)
Sparse Core Ops, SparseCore 0:
  806.1 122.3 reduce-scatter.21
  934.0 123.6 reduce-scatter.25
  1063.1 120.5 reduce-scatter.23
  1189.3 135.8 reduce-scatter.15
  1332.4 219.8 reduce-scatter.13
  1558.5 285.1 reduce-scatter.17
  1850.1 284.4 reduce-scatter.19
where the time goes:
time: 2150 us; the launch traced here: 2140 us
  waiting for transfers between devices  1440 us (67%)
  blocking collectives  201 us (9%)
  local copies, waits for them, and re-layouts  182 us (8%)
  other arithmetic  147 us (7%)
  matrix products  140 us (7%)
    reduce_scatter x1, waiting for transfers between devices, shards(): lax.psum_scatter(summed_local[2], 'batch', scatter_dimension=2, tiled=True)  291 us
    reduce_scatter x1, waiting for transfers between devices, shards(): lax.psum_scatter(summed_local[3], 'batch', scatter_dimension=2, tiled=True)  291 us
    unnamed x10, waiting for transfers between devices  281 us
    reduce_scatter x1, waiting for transfers between devices, shards(): lax.psum_scatter(summed_local[0], 'batch', scatter_dimension=2, tiled=True)  227 us
    ppermute x2, waiting for transfers between devices, passed_along(): return lax.ppermute(block, axis, route)  210 us
    reduce_scatter x1, waiting for transfers between devices, shards(): lax.psum_scatter(summed_local[1], 'batch', scatter_dimension=2, tiled=True)  140 us
    all_gather x1, blocking collectives, shards(): lax.all_gather(result[1][:, 0, :], ('section', 'batch'), axis=0, tiled=True)  136 us
    all_gather x1, blocking collectives, shards(): lax.all_gather(result[0][:, 0, :], ('section', 'batch'), axis=0, tiled=True)  64.4 us
  transfers between devices with their start and end apart: 9, of which 8 were waited for; matrix products, arithmetic and copies ran while one was open for 5% of the time, Pallas kernels for 0%

commit v1 on v0

v1 whole, which is shorter than its diff:
```python
from functools import partial

import jax
import jax.numpy as jnp
from jax import lax
from jax.sharding import PartitionSpec as P

HEADS = 12
HEAD_DIM = 64


NORM_EPS = 1e-05
SQRT_HALF = 0.7071067811865476
ROOT_TAU_INV = 0.3989422804014327
MASK_FILL = -1e30
LOGIT_GAIN = 2.5
PRECISE = lax.Precision.HIGHEST


def core_swap(block):
    return lax.ppermute(block, "section", [(0, 1), (1, 0)])


def flip_swap(block, bit):
    size = lax.axis_size("batch")
    return lax.ppermute(block, "batch", [(i, i ^ bit) for i in range(size)])


def outer_sum(left, right):
    return lax.dot_general(
        left, right, (((0,), (0,)), ((), ())), preferred_element_type=jnp.float32
    )


def times_transposed(left, right):
    return lax.dot_general(
        left, right, (((1,), (1,)), ((), ())), preferred_element_type=jnp.float32
    )


def norm_rows(values, scale_gain, shift_bias):
    center = values - jnp.mean(values, axis=-1, keepdims=True)
    inverse = lax.rsqrt(jnp.mean(center * center, axis=-1, keepdims=True) + NORM_EPS)
    normed = center * inverse
    return (normed * scale_gain + shift_bias, normed, inverse)


def norm_back(upstream, normed, inverse, scale_gain):
    scaled = upstream * scale_gain
    return inverse * (
        scaled
        - jnp.mean(scaled, axis=-1, keepdims=True)
        - normed * jnp.mean(scaled * normed, axis=-1, keepdims=True)
    )


def gelu_value(values):
    return 0.5 * values * (1.0 + jax.scipy.special.erf(values * SQRT_HALF))


def gelu_slope(values):
    return (
        0.5 * (1.0 + jax.scipy.special.erf(values * SQRT_HALF))
        + values * jnp.exp(-0.5 * values * values) * ROOT_TAU_INV
    )


def soft_scores(query_rows, key_rows, lengths):
    scores = jnp.einsum(
        "nqhd,nkhd->nhqk", query_rows, key_rows, preferred_element_type=jnp.float32
    ) * HEAD_DIM ** (-0.5)
    valid_keys = jnp.arange(scores.shape[-1])[None, :] < lengths[:, None]
    scores = jnp.where(valid_keys[:, None, None, :], scores, MASK_FILL)
    exponent = jnp.exp(scores - jnp.max(scores, axis=-1, keepdims=True))
    return exponent / jnp.sum(exponent, axis=-1, keepdims=True)


def block_forward(weights, block_rows, lengths):
    w_qkv, w_out, w_up, w_down, norm_gains, biases, b_up = weights
    seq_count, seq_slots, model_width = block_rows.shape
    flat_rows = block_rows.reshape(seq_count * seq_slots, model_width)
    projected = jnp.dot(flat_rows, w_qkv, preferred_element_type=jnp.float32)
    shape_heads = (seq_count, seq_slots, HEADS, HEAD_DIM)
    query_rows = (projected[:, :model_width] + biases[0]).astype(jnp.bfloat16).reshape(shape_heads)
    key_rows = projected[:, model_width : 2 * model_width].astype(jnp.bfloat16).reshape(shape_heads)
    value_rows = (
        (projected[:, 2 * model_width :] + biases[1]).astype(jnp.bfloat16).reshape(shape_heads)
    )
    soft_weights = soft_scores(query_rows, key_rows, lengths)
    mixed_rows = jnp.einsum(
        "nhqk,nkhd->nqhd",
        soft_weights.astype(jnp.bfloat16),
        value_rows,
        preferred_element_type=jnp.float32,
    )
    mixed_rows = mixed_rows.reshape(flat_rows.shape).astype(jnp.bfloat16)
    summed = flat_rows.astype(jnp.float32) + (
        jnp.dot(mixed_rows, w_out, preferred_element_type=jnp.float32) + biases[2]
    )
    first_norm, first_hat, first_inv = norm_rows(summed, norm_gains[0], biases[3])
    first_low = first_norm.astype(jnp.bfloat16)
    hidden = jnp.dot(first_low, w_up, preferred_element_type=jnp.float32) + b_up
    active = gelu_value(hidden).astype(jnp.bfloat16)
    second = first_norm + (jnp.dot(active, w_down, preferred_element_type=jnp.float32) + biases[4])
    output, out_hat, out_inv = norm_rows(second, norm_gains[1], biases[5])
    kept_values = (
        flat_rows,
        query_rows,
        key_rows,
        value_rows,
        soft_weights,
        mixed_rows,
        first_hat,
        first_inv,
        first_low,
        hidden,
        active,
        out_hat,
        out_inv,
    )
    return (output.reshape(block_rows.shape), kept_values)


def block_backward(weights, kept_values, upstream):
    w_qkv, w_out, w_up, w_down, norm_gains, biases, b_up = weights
    (
        flat_rows,
        query_rows,
        key_rows,
        value_rows,
        soft_weights,
        mixed_rows,
        first_hat,
        first_inv,
        first_low,
        hidden,
        active,
        out_hat,
        out_inv,
    ) = kept_values
    grad_rows = upstream.reshape(flat_rows.shape)
    d_gain_out = jnp.sum(grad_rows * out_hat, axis=0)
    d_shift_out = jnp.sum(grad_rows, axis=0)
    d_second = norm_back(grad_rows, out_hat, out_inv, norm_gains[1])
    d_branch_ffn = d_second.astype(jnp.bfloat16)
    d_bias_ffn = jnp.sum(d_branch_ffn.astype(jnp.float32), axis=0)
    d_hidden = (times_transposed(d_branch_ffn, w_down) * gelu_slope(hidden)).astype(jnp.bfloat16)
    d_bias_up = jnp.sum(d_hidden.astype(jnp.float32), axis=0)
    d_first = d_second + times_transposed(d_hidden, w_up)
    d_gain_first = jnp.sum(d_first * first_hat, axis=0)
    d_shift_first = jnp.sum(d_first, axis=0)
    d_summed = norm_back(d_first, first_hat, first_inv, norm_gains[0])
    d_branch = d_summed.astype(jnp.bfloat16)
    d_bias_out = jnp.sum(d_branch.astype(jnp.float32), axis=0)
    d_mixed = times_transposed(d_branch, w_out).astype(jnp.bfloat16).reshape(query_rows.shape)
    d_soft = jnp.einsum("nqhd,nkhd->nhqk", d_mixed, value_rows, preferred_element_type=jnp.float32)
    d_value = jnp.einsum(
        "nhqk,nqhd->nkhd",
        soft_weights.astype(jnp.bfloat16),
        d_mixed,
        preferred_element_type=jnp.float32,
    )
    d_scores = (
        soft_weights * (d_soft - jnp.sum(d_soft * soft_weights, axis=-1, keepdims=True))
    ).astype(jnp.bfloat16)
    head_scale = HEAD_DIM ** (-0.5)
    d_query = (
        jnp.einsum("nhqk,nkhd->nqhd", d_scores, key_rows, preferred_element_type=jnp.float32)
        * head_scale
    )
    d_key = (
        jnp.einsum("nhqk,nqhd->nkhd", d_scores, query_rows, preferred_element_type=jnp.float32)
        * head_scale
    )
    d_proj = jnp.concatenate(
        [
            member.astype(jnp.bfloat16).reshape(flat_rows.shape)
            for member in (d_query, d_key, d_value)
        ],
        axis=1,
    )
    model_width = flat_rows.shape[1]
    d_bias_query = jnp.sum(d_proj[:, :model_width].astype(jnp.float32), axis=0)
    d_bias_value = jnp.sum(d_proj[:, 2 * model_width :].astype(jnp.float32), axis=0)
    d_input = d_summed + times_transposed(d_proj, w_qkv)
    pairs = (
        (flat_rows, d_proj),
        (mixed_rows, d_branch),
        (first_low, d_hidden),
        (active, d_branch_ffn),
    )
    vectors = (
        jnp.stack([d_gain_first, d_gain_out]),
        jnp.stack(
            [d_bias_query, d_bias_value, d_bias_out, d_shift_first, d_bias_ffn, d_shift_out]
        ),
        d_bias_up[None],
    )
    return d_input, pairs, vectors


def outer_low(left, right):
    return outer_sum(left, right).astype(jnp.bfloat16)


def seed_grad(cotangent, lengths, cls_grad):
    valid_rows = (jnp.arange(cotangent.shape[1])[None, :] < lengths[:, None]).astype(jnp.float32)
    grad_rows = cotangent.astype(jnp.float32) * valid_rows[:, :, None]
    return grad_rows.at[:, 0, :].add(cls_grad)


def pick(flag, yes, no):
    return jax.tree.map(lambda a, b: jnp.where(flag, a, b), yes, no)


def pick_bit(grid, axis, index):
    return lax.dynamic_index_in_dim(grid, index, axis, keepdims=False)


def own_bit(bit):
    return (lax.axis_index("batch") // bit) % 2


def scatter_sum(grid, bits, left):
    left = list(left)
    for bit in bits:
        axis = left.index(bit)
        mine = own_bit(bit)
        sent = pick_bit(grid, axis, 1 - mine)
        kept = pick_bit(grid, axis, mine)
        arrived = flip_swap(sent, bit)
        total = kept.astype(jnp.float32) + arrived.astype(jnp.float32)
        left.remove(bit)
        grid = total if not left else total.astype(grid.dtype)
    return grid


def all_bits(size):
    bits = [1 << i for i in range(size.bit_length() - 1)]
    return bits[::-1]


def to_grid(array, size):
    bits = all_bits(size)
    return array.reshape((2,) * len(bits) + (array.shape[0] // size,) + array.shape[1:])


def three_orders(size):
    bits = all_bits(size)[::-1]
    if size == 16:
        return [1, 2, 4, 8], [2, 1, 4, 8], [4, 1, 2, 8]
    third = len(bits) // 3
    return [bits[i * third :] + bits[: i * third] for i in range(3)]


def gather_all(block, size):
    if size != 16:
        for bit in all_bits(size)[::-1]:
            block = jnp.concatenate([block, flip_swap(block, bit)], 0)
        return block
    block = jnp.concatenate([block] + [flip_swap(block, k) for k in (1, 2, 3)], 0)
    return jnp.concatenate([block] + [flip_swap(block, k) for k in (4, 8, 12)], 0)


def vector_grid(vectors, size):
    return jnp.concatenate(
        [
            jnp.swapaxes(item.reshape(item.shape[0], size, -1), 0, 1).reshape(size, -1)
            for item in vectors
        ],
        axis=1,
    )


def contrast(own_cls, micro, positive, query_count, batch_index, batch_size):
    width = own_cls.shape[1]
    chip_rows = own_cls.shape[0]
    gathered = gather_all(own_cls, batch_size).reshape(batch_size, chip_rows, width)
    all_q = gathered[:, :query_count].reshape(-1, width)
    all_p = gathered[:, query_count:].reshape(-1, width)
    blocks = jnp.arange(batch_size, dtype=jnp.int32) ^ batch_index
    query_ids = (
        blocks[:, None] * query_count + jnp.arange(query_count, dtype=jnp.int32)[None, :]
    ).reshape(-1)
    passage_ids = (
        3 * query_ids[:, None] + jnp.arange(3, dtype=jnp.int32)[None, :]
    ).reshape(-1)
    labels = jnp.take(micro, query_ids)
    wanted = jnp.take(positive, query_ids)
    logit_scale = LOGIT_GAIN * width ** (-0.5)
    logits = times_transposed(all_q, all_p) * logit_scale
    same_group = labels[:, None] == jnp.repeat(labels, 3)[None, :]
    logits = jnp.where(same_group, logits, MASK_FILL)
    row_top = jnp.max(logits, axis=-1, keepdims=True)
    exponent = jnp.exp(logits - row_top)
    totals = jnp.sum(exponent, axis=-1, keepdims=True)
    target = passage_ids[None, :] == wanted[:, None]
    loss_all = (
        row_top[:, 0] + jnp.log(totals[:, 0]) - jnp.sum(jnp.where(target, logits, 0.0), axis=-1)
    )
    coefficient = (exponent / totals - target.astype(jnp.float32)) * logit_scale
    passage_count = 3 * query_count
    d_cls_q = jnp.dot(coefficient[:query_count], all_p.astype(jnp.float32), precision=PRECISE)
    d_cls_p = lax.dot_general(
        coefficient[:, :passage_count],
        all_q.astype(jnp.float32),
        (((0,), (0,)), ((), ())),
        precision=PRECISE,
    )
    return loss_all[:query_count], d_cls_q, d_cls_p


def shards(
    x_q,
    x_p,
    len_q,
    len_p,
    cot_q,
    cot_p,
    positive,
    micro,
    w_qkv,
    w_out,
    w_up,
    w_down,
    norm_gain,
    biases,
    b_up,
):
    core = lax.axis_index("section")
    is_first = core == 0
    batch_index = lax.axis_index("batch")
    size = lax.axis_size("batch")
    bits = all_bits(size)
    own_sets = (w_qkv, w_out, w_up, w_down, norm_gain, biases, b_up)
    own_q = tuple(member[0, 0] for member in own_sets)
    own_p = tuple(member[0, 1] for member in own_sets)
    other_p = tuple(core_swap(member) for member in own_p)
    layers_p = (pick(is_first, own_p, other_p), pick(is_first, other_p, own_p))
    query_count = x_q.shape[0]
    half_count = x_p.shape[0] // 2

    def own_half(array):
        return lax.dynamic_slice_in_dim(array, core * half_count, half_count, 0)

    rows_p, lens_p, cots_p = own_half(x_p), own_half(len_p), own_half(cot_p)

    early_q, early_kept_q = block_forward(own_q, x_q, len_q)
    mid_q = early_q.astype(jnp.bfloat16)
    late_q, late_kept_q = block_forward(own_q, core_swap(mid_q), len_q)
    mid_p, early_kept_p = block_forward(layers_p[0], rows_p, lens_p)
    mid_p = mid_p.astype(jnp.bfloat16)
    top_p, late_kept_p = block_forward(layers_p[1], mid_p, lens_p)
    top_low_p = top_p.astype(jnp.bfloat16)

    cls_rows = jnp.concatenate([late_q[:, 0, :].astype(jnp.bfloat16), top_low_p[:, 0, :]], 0)
    cls_other = core_swap(cls_rows)
    cls_chip = jnp.concatenate(
        [
            jnp.where(is_first, cls_other[:query_count], cls_rows[:query_count]),
            jnp.where(is_first, cls_rows[query_count:], cls_other[query_count:]),
            jnp.where(is_first, cls_other[query_count:], cls_rows[query_count:]),
        ],
        0,
    )
    loss_own, d_cls_q, d_cls_p = contrast(
        cls_chip, micro, positive, query_count, batch_index, size
    )

    late_grad_q, late_pairs_q, late_vec_q = block_backward(
        own_q, late_kept_q, seed_grad(cot_q, len_q, d_cls_q)
    )
    late_sent_q = late_grad_q.astype(jnp.bfloat16)
    early_grad_q, early_pairs_q, early_vec_q = block_backward(
        own_q, early_kept_q, core_swap(late_sent_q).astype(jnp.float32)
    )
    pairs_q = pick(is_first, early_pairs_q, late_pairs_q)
    vec_q = pick(is_first, early_vec_q, late_vec_q)

    late_grad_p, late_pairs_p, late_vec_p = block_backward(
        layers_p[1], late_kept_p, seed_grad(cots_p, lens_p, own_half(d_cls_p))
    )
    late_sent_p = late_grad_p.astype(jnp.bfloat16).astype(jnp.float32)
    early_grad_p, early_pairs_p, early_vec_p = block_backward(
        layers_p[0], early_kept_p, late_sent_p
    )

    def passage_sums(pairs):
        g_qkv, g_out, g_up, g_down = (outer_low(left, right) for left, right in pairs)

        def halves(array):
            width = array.shape[1] // 2
            keep = lax.dynamic_slice_in_dim(array, core * width, width, 1)
            send = lax.dynamic_slice_in_dim(array, (1 - core) * width, width, 1)
            return keep, send

        results = []
        chunks = ((g_down,), (g_up,), (g_qkv, g_out))
        for chunk, order in zip(chunks, three_orders(size)):
            parts = [halves(array) for array in chunk]
            keep = jnp.concatenate([part[0] for part in parts], 1)
            send = jnp.concatenate([part[1] for part in parts], 1)
            total = (keep.astype(jnp.float32) + core_swap(send).astype(jnp.float32)).astype(
                jnp.bfloat16
            )
            results.append(scatter_sum(to_grid(total, size), order, bits))
        return results

    late_sums = passage_sums(late_pairs_p)
    early_sums = passage_sums(early_pairs_p)

    lefts = [left for left, _ in pairs_q]
    rights = jnp.concatenate([right for _, right in pairs_q], 1)
    rows = rights.shape[0]
    grids = [
        left.reshape((rows,) + (2,) * len(bits) + (left.shape[1] // size,)) for left in lefts
    ]
    left_bits = list(bits)
    for bit in (1, 2):
        axis = 1 + left_bits.index(bit)
        mine = own_bit(bit)
        kept = [pick_bit(grid, axis, mine) for grid in grids]
        sent = [pick_bit(grid, axis, 1 - mine) for grid in grids]
        left_bits.remove(bit)
        packed = jnp.concatenate([item.reshape(rows, -1) for item in sent] + [rights], 1)
        arrived = flip_swap(packed, bit)
        rows = 2 * rows
        grown = []
        offset = 0
        for item in kept:
            flat = item.reshape(rows // 2, -1)
            part = arrived[:, offset : offset + flat.shape[1]]
            offset += flat.shape[1]
            grown.append(jnp.concatenate([flat, part], 0).reshape((rows,) + item.shape[1:]))
        grids = grown
        rights = jnp.concatenate([rights, arrived[:, offset:]], 0)
    query_sums = []
    offset = 0
    for grid, (_, right) in zip(grids, pairs_q):
        width = right.shape[1]
        product = outer_low(grid.reshape(rows, -1), rights[:, offset : offset + width])
        offset += width
        query_sums.append(
            product.reshape((2,) * len(left_bits) + (grid.shape[-1], width))
        )
    wide = jnp.concatenate(query_sums[:3], -1)
    wide = scatter_sum(wide, left_bits[::-1], left_bits)
    down_q = scatter_sum(query_sums[3], left_bits[::-1], left_bits)
    model = down_q.shape[1]
    qkv_q, out_q, up_q = wide[:, : 3 * model], wide[:, 3 * model : 4 * model], wide[:, 4 * model :]

    early_line, late_line = vector_grid(early_vec_p, size), vector_grid(late_vec_p, size)
    line_p = jnp.where(is_first, early_line, late_line) + core_swap(
        jnp.where(is_first, late_line, early_line)
    )
    lines = jnp.concatenate([vector_grid(vec_q, size), line_p], 1)
    lines = scatter_sum(to_grid(lines, size), bits[::-1], bits)[0]
    lines = lines.reshape(2, -1)
    blk = model // size
    g_gain = lines[:, : 2 * blk].reshape(2, 2, blk)
    g_bias = lines[:, 2 * blk : 8 * blk].reshape(2, 6, blk)
    g_bup = lines[:, 8 * blk :]

    def own_layer(early, late):
        other = core_swap(jnp.where(is_first, late, early))
        own = jnp.where(is_first, early, late)
        return jnp.where(is_first, own, other), jnp.where(is_first, other, own)

    def join(early, late, axis):
        return jnp.concatenate(own_layer(early, late), axis)

    down_p = join(early_sums[0], late_sums[0], 1)
    up_p = join(early_sums[1], late_sums[1], 1)
    first, second = own_layer(early_sums[2], late_sums[2])
    cut = 3 * model // 2
    qkv_p = jnp.concatenate([first[:, :cut], second[:, :cut]], 1)
    out_p = jnp.concatenate([first[:, cut:], second[:, cut:]], 1)
    hidden_p = join(mid_p, top_low_p, 0)
    grad_p = join(early_grad_p.reshape(mid_p.shape), late_sent_p.reshape(mid_p.shape), 0)
    hidden_q = jnp.where(is_first, mid_q, late_q.astype(jnp.bfloat16))
    grad_q = jnp.where(is_first, early_grad_q, late_sent_q.astype(jnp.float32))
    return (
        hidden_q[None],
        hidden_p[None],
        grad_q.reshape(x_q.shape)[None],
        grad_p[None],
        loss_own,
        jnp.stack([qkv_q, qkv_p])[None],
        jnp.stack([out_q, out_p])[None],
        jnp.stack([up_q, up_p])[None],
        jnp.stack([down_q, down_p])[None],
        g_gain[None],
        g_bias[None],
        g_bup[None],
        g_bias[None, :, 0, :],
    )


def solution(mesh):
    return jax.shard_map(
        shards,
        mesh=mesh,
        in_specs=(
            P("batch", None, None),
            P("batch", None, None),
            P("batch"),
            P("batch"),
            P("batch", None, None),
            P("batch", None, None),
            P(),
            P(),
            P("section", None, None, None),
            P("section", None, None, None),
            P("section", None, None, None),
            P("section", None, None, None),
            P("section", None, None, None),
            P("section", None, None, None),
            P("section", None, None),
        ),
        out_specs=(
            P("section", "batch", None, None),
            P("section", "batch", None, None),
            P("section", "batch", None, None),
            P("section", "batch", None, None),
            P("batch"),
            P("section", None, "batch", None),
            P("section", None, "batch", None),
            P("section", None, "batch", None),
            P("section", None, "batch", None),
            P("section", None, None, "batch"),
            P("section", None, None, "batch"),
            P("section", None, "batch"),
            P("section", None, "batch"),
        ),
        check_vma=False,
    )
```

time: 2150 us -> 738 us (0.34)
  waiting for transfers between devices: 1440 us -> 204 us
  blocking collectives: 201 us -> 0 us
  other arithmetic: 147 us -> 82.6 us
  matrix products: 140 us -> 195 us
  starting transfers between devices: 4.05 us -> 52.4 us
    reduce_scatter x4 -> x0, waiting for transfers between devices: 949 us -> none  [the longest x1 291 us: shards(): lax.psum_scatter(summed_local[2], 'batch', scatter_dimension=2, tiled=True)]
    unnamed x10 -> x0, waiting for transfers between devices: 281 us -> none
    all_gather x2 -> x0, blocking collectives: 201 us -> none  [the longest x1 136 us: shards(): lax.all_gather(result[1][:, 0, :], ('section', 'batch'), axis=0, tiled=True)]
    add x11 -> x8, other arithmetic: 64.2 us -> 1.25 us  [the longest x1 0.86 us: shards(): jnp.where(is_first, early_line, late_line)]
    ppermute x2 -> x62, starting transfers between devices: 3.77 us -> 52.4 us  [the longest x40 46.3 us: flip_swap(): return lax.ppermute(block, 'batch', [(i, i ^ bit) for i in range(size)])]
    dot_general x9 -> x17, matrix products: 32.2 us -> 66.5 us  [times_transposed(): lax.dot_general(left, right, (((1,), (1,)), ((), ())), preferred_element_...]
    cond x200 -> x0, local copies, waits for them, and re-layouts: 31.7 us -> none  [the longest x2 16 us: shards(): lax.cond(is_first, partial(backward_work, towers, early_rows, early_len,...]
    dynamic_slice x2 -> x30, local copies, waits for them, and re-layouts: 0.26 us -> 31.6 us  [the longest x19 18.6 us: pick_bit(): return lax.dynamic_index_in_dim(grid, index, axis, keepdims=False)]
  transfers between devices with their start and end apart: 9 -> 62, of which waited for: 8 -> 26; matrix products, arithmetic and copies ran while one was open for 5% -> 51% of each run, Pallas kernels for 0% -> 0%
where the time goes in v1:
time: 738 us; the launch traced here: 726 us
  waiting for transfers between devices  204 us (28%)
  matrix products  195 us (26%)
  local copies, waits for them, and re-layouts  187 us (25%)
  other arithmetic  82.6 us (11%)
  starting transfers between devices  52.4 us (7%)
    ppermute x40, waiting for transfers between devices, flip_swap(): return lax.ppermute(block, 'batch', [(i, i ^ bit) for i in range(size)])  203 us
    dot_general x17, matrix products, times_transposed(): lax.dot_general(left, right, (((1,), (1,)), ((), ())), preferred_element_...  66.5 us
    ppermute x40, starting transfers between devices, flip_swap(): return lax.ppermute(block, 'batch', [(i, i ^ bit) for i in range(size)])  46.3 us
    dot_general x12, matrix products, outer_sum(): lax.dot_general(left, right, (((0,), (0,)), ((), ())), preferred_element_...  29.3 us
    unnamed x626, local copies, waits for them, and re-layouts  24.5 us
    dynamic_slice x19, local copies, waits for them, and re-layouts, pick_bit(): return lax.dynamic_index_in_dim(grid, index, axis, keepdims=False)  18.6 us
    dot_general x4, matrix products, block_forward(): hidden = jnp.dot(first_low, w_up, preferred_element_type=jnp.float32) + b_up  18.6 us
    dot_general x4, matrix products, block_forward(): jnp.dot(active, w_down, preferred_element_type=jnp.float32) + biases[4]  15.6 us
  transfers between devices with their start and end apart: 62, of which 26 were waited for; matrix products, arithmetic and copies ran while one was open for 51% of the time, Pallas kernels for 0%

profile of v1, /device:TPU:0, one launch (start us, length us, event | category | flops | bytes accessed | tf_op | source)
XLA Modules:
  0.0 725.8 jit_solution(2092232099719024375)
XLA Ops:
  4.4 2.8 fusion.38
  19.1 3.5 fusion.40
  22.7 4.2 fusion.422
  29.9 2.7 slice_bitcast_fusion.1
  51.7 2.8 fusion.36
  58.9 3.8 broadcast_select_fusion.49
  62.8 3.8 fusion.429
  78.1 3.1 constant_dynamic-slice_fusion.30
  81.2 3.6 fusion.96
  98.5 3.5 fusion.430
  108.2 4.4 multiply_convert_fusion.1
  117.1 3.9 fusion.99
  134.9 3.1 fusion.433
  143.8 6.9 multiply_convert_fusion
  150.8 5.4 fusion.435
  162.6 2.9 collective-permute-start.10
  176.1 5.2 concatenate.151
  189.5 2.7 collective-permute-done.15
  192.2 9.5 %concatenate.152 = bf16[128,768]{1,0:T(8,128)(2,1)} concatenate(bf16[2,768]{1,0:T(2,128)(2,1)} %copy-done.128, bf16[3,768]{1,0:T(4,128)(2,1)} %copy-done.119, bf16[3,768]{1,0:T(4,128)(2,1)S(1)} %get-tuple-element.255, bf16[8,768]{1,0:T(8,128)(2,1)} %collective-permute-done.10, bf16[8,768]{1,0:T(8,128)(2,1)} %collective-permute-done.11, bf16[8,768]{1,0:T(8,128)(2,1)} %collective-permute-done.12, ...), dimensions={0} | concatenate | bytes 393216 | tf_op jit(solution)/shard_map/concatenate | solution.py:262
  221.4 4.8 convert_reduce_fusion.11
  226.2 4.7 multiply_reduce_fusion.16
  238.7 2.8 convert_reduce_fusion.13
  247.4 7.9 %convert_reduce_fusion = (f32[3072]{0:T(1024)}, bf16[384,3072]{1,0:T(8,128)(2,1)S(1)}) fusion(f32[384,3072]{1,0:T(8,128)} %get-tuple-element.291, bf16[3072,768]{1,0:T(8,128)(2,1)} %collective-permute-done.7, pred[]{:T(512)S(6)} %eq.66, bf16[1,2,3072,768]{3,2,1,0:T(8,128)(2,1)} %param.32, f32[384,768]{1,0:T(8,128)S(1)} %get-tuple-element.166), kind=kOutput, calls=%fused_computation.42 | convolution fusion | flops 1828746240 | bytes 17707008 | tf_op jit(solution)/shard_map/dot_general | solution.py:36
  255.7 5.9 multiply_reduce_fusion.3
  263.3 2.8 convolution_convert_fusion.14
  270.2 2.8 multiply_reduce_fusion.1
  280.2 5.8 fusion.123
  287.1 6.4 convert_reduce_fusion.1
  293.6 3.2 multiply_reduce_fusion.4
  303.6 2.8 multiply_reduce_fusion
  317.0 3.9 convolution_convert_fusion.4
  320.9 4.7 convolution_convert_fusion.3
  325.7 4.8 convolution_convert_fusion.2
  330.5 4.3 convolution_convert_fusion.1
  334.9 4.7 convolution_convert_fusion
  342.4 4.0 fusion.203
  351.6 3.2 convert_select_fusion.1
  375.7 2.7 pad_maximum_fusion.3
  391.9 4.9 convert_reduce_fusion.12
  396.9 4.7 multiply_reduce_fusion.17
  420.3 2.7 collective-permute-done.60
  423.2 3.9 fusion.167
  439.3 16.6 %collective-permute-done.18 = bf16[64,9600]{1,0:T(8,128)(2,1)} collective-permute-done((bf16[64,9600]{1,0:T(8,128)(2,1)}, bf16[64,9600]{1,0:T(8,128)(2,1)}, u32[]{:S(2)}, u32[]{:S(2)}) %collective-permute-start.18) | collective-permute-done | bytes 1228832 | tf_op jit(solution)/shard_map/ppermute | solution.py:26
  468.8 2.7 pad_maximum_fusion.4
  471.6 5.7 concatenate.173
  477.2 4.3 copy.656
  482.2 3.3 add_convert_fusion.3
  500.4 2.8 add_convert_fusion.1
  505.9 28.5 %collective-permute-done.19 = bf16[128,8256]{0,1:T(8,128)(2,1)S(1)} collective-permute-done((bf16[128,8256]{0,1:T(8,128)(2,1)S(1)}, bf16[128,8256]{0,1:T(8,128)(2,1)S(1)}, u32[]{:S(2)}, u32[]{:S(2)}) %collective-permute-start.19) | collective-permute-done | bytes 2113568 | tf_op jit(solution)/shard_map/ppermute | solution.py:26
  543.8 15.9 %collective-permute-done.34 = bf16[2,2,2,48,1536]{4,3,0,1,2:T(8,128)(2,1)S(1)} collective-permute-done((bf16[2,2,2,48,1536]{4,3,0,1,2:T(8,128)(2,1)}, bf16[2,2,2,48,1536]{4,3,0,1,2:T(8,128)(2,1)S(1)}, u32[]{:S(2)}, u32[]{:S(2)}) %collective-permute-start.34) | collective-permute-done | bytes 1179680 | tf_op jit(solution)/shard_map/ppermute | solution.py:26
  565.1 18.8 %collective-permute-done.39 = bf16[2,2,2,48,1536]{4,3,0,1,2:T(8,128)(2,1)S(1)} collective-permute-done((bf16[2,2,2,48,1536]{4,3,0,1,2:T(8,128)(2,1)S(1)}, bf16[2,2,2,48,1536]{4,3,0,1,2:T(8,128)(2,1)S(1)}, u32[]{:S(2)}, u32[]{:S(2)}) %collective-permute-start.39) | collective-permute-done | bytes 1179680 | tf_op jit(solution)/shard_map/ppermute | solution.py:26
  585.7 2.9 collective-permute-done.52
  591.4 9.8 %collective-permute-done.24 = bf16[2,2,48,1536]{3,2,0,1:T(8,128)(2,1)S(1)} collective-permute-done((bf16[2,2,48,1536]{3,2,0,1:T(8,128)(2,1)S(1)}, bf16[2,2,48,1536]{3,2,0,1:T(8,128)(2,1)S(1)}, u32[]{:S(2)}, u32[]{:S(2)}) %collective-permute-start.24) | collective-permute-done | bytes 589856 | tf_op jit(solution)/shard_map/ppermute | solution.py:26
  602.9 11.0 %collective-permute-done.29 = bf16[2,2,48,1536]{3,2,0,1:T(8,128)(2,1)S(1)} collective-permute-done((bf16[2,2,48,1536]{3,2,0,1:T(8,128)(2,1)S(1)}, bf16[2,2,48,1536]{3,2,0,1:T(8,128)(2,1)S(1)}, u32[]{:S(2)}, u32[]{:S(2)}) %collective-permute-start.29) | collective-permute-done | bytes 589856 | tf_op jit(solution)/shard_map/ppermute | solution.py:26
  615.5 11.0 %collective-permute-done.35 = bf16[2,2,48,1536]{3,2,0,1:T(8,128)(2,1)S(1)} collective-permute-done((bf16[2,2,48,1536]{3,2,0,1:T(8,128)(2,1)S(1)}, bf16[2,2,48,1536]{3,2,0,1:T(8,128)(2,1)S(1)}, u32[]{:S(2)}, u32[]{:S(2)}) %collective-permute-start.35) | collective-permute-done | bytes 589856 | tf_op jit(solution)/shard_map/ppermute | solution.py:26
  631.2 4.9 collective-permute-done.40
  643.7 5.6 collective-permute-done.36
  650.5 8.3 %collective-permute-done.41 = bf16[2,48,1536]{2,1,0:T(8,128)(2,1)S(1)} collective-permute-done((bf16[2,48,1536]{2,1,0:T(8,128)(2,1)S(1)}, bf16[2,48,1536]{2,1,0:T(8,128)(2,1)S(1)}, u32[]{:S(2)}, u32[]{:S(2)}) %collective-permute-start.41) | collective-permute-done | bytes 294944 | tf_op jit(solution)/shard_map/ppermute | solution.py:26
  659.4 7.9 %collective-permute-done.49 = bf16[2,192,384]{2,1,0:T(8,128)(2,1)S(1)} collective-permute-done((bf16[2,192,384]{2,1,0:T(8,128)(2,1)S(1)}, bf16[2,192,384]{2,1,0:T(8,128)(2,1)S(1)}, u32[]{:S(2)}, u32[]{:S(2)}) %collective-permute-start.49) | collective-permute-done | bytes 294944 | tf_op jit(solution)/shard_map/ppermute | solution.py:26
  667.9 2.7 collective-permute-done.54
  674.4 12.3 %collective-permute-done.37 = bf16[48,1536]{1,0:T(8,128)(2,1)S(1)} collective-permute-done((bf16[48,1536]{1,0:T(8,128)(2,1)S(1)}, bf16[48,1536]{1,0:T(8,128)(2,1)S(1)}, u32[]{:S(2)}, u32[]{:S(2)}) %collective-permute-start.37) | collective-permute-done | bytes 147488 | tf_op jit(solution)/shard_map/ppermute | solution.py:26
  686.7 3.2 collective-permute-done.42
  690.0 2.9 collective-permute-done.50
  697.7 24.6 %collective-permute-done.21 = bf16[48,6144]{1,0:T(8,128)(2,1)S(1)} collective-permute-done((bf16[48,6144]{1,0:T(8,128)(2,1)S(1)}, bf16[48,6144]{1,0:T(8,128)(2,1)S(1)}, u32[]{:S(2)}, u32[]{:S(2)}) %collective-permute-start.21) | collective-permute-done | bytes 589856 | tf_op jit(solution)/shard_map/ppermute | solution.py:26
  (1169 shorter events, 337.9 us)
Async XLA Ops:
  3.0 68.0 %copy-start.122 = (f32[768]{0:T(1024)}, f32[768]{0:T(1024)S(1)}, u32[]{:S(2)}) copy-start(f32[768]{0:T(1024)S(1)} %get-tuple-element.156) | copy-start | bytes 9220
  28.3 23.3 %collective-permute-start = (bf16[2,32,768]{2,1,0:T(8,128)(2,1)}, bf16[2,32,768]{2,1,0:T(8,128)(2,1)}, u32[]{:S(2)}, u32[]{:S(2)}) collective-permute-start(bf16[2,32,768]{2,1,0:T(8,128)(2,1)} %bitcast.7), channel_id=1, source_target_pairs={{0,16},{16,0},{1,17},{17,1},{2,18},{18,2},{3,19},{19,3},{4,20},{20... | collective-permute-start | bytes 294920 | tf_op jit(solution)/shard_map/ppermute | solution.py:21
  29.4 20.7 %collective-permute-start.2 = (f32[6,768]{1,0:T(8,128)}, f32[6,768]{1,0:T(8,128)}, u32[]{:S(2)}, u32[]{:S(2)}) collective-permute-start(f32[6,768]{1,0:T(8,128)} %bitcast.671), channel_id=1, source_target_pairs={{0,16},{16,0},{1,17},{17,1},{2,18},{18,2},{3,19},{19,3},{4,20},{20... | collective-permute-start | bytes 55304 | tf_op jit(solution)/shard_map/ppermute | solution.py:21
  29.5 18.9 %collective-permute-start.6 = (f32[3072]{0:T(1024)}, f32[3072]{0:T(1024)}, u32[]{:S(2)}, u32[]{:S(2)}) collective-permute-start(f32[3072]{0:T(1024)} %bitcast.18), channel_id=1, source_target_pairs={{0,16},{16,0},{1,17},{17,1},{2,18},{18,2},{3,19},{19,3},{4,20},{20... | collective-permute-start | bytes 36872 | tf_op jit(solution)/shard_map/ppermute | solution.py:21
  32.7 73.6 %collective-permute-start.5 = (bf16[768,3072]{1,0:T(8,128)(2,1)}, bf16[768,3072]{1,0:T(8,128)(2,1)}, u32[]{:S(2)}, u32[]{:S(2)}) collective-permute-start(bf16[768,3072]{1,0:T(8,128)(2,1)} %slice_bitcast_fusion.1), channel_id=1, source_target_pairs={{0,16},{16,0},{1,17},{17,1},{2,18},{18,2},{3,19},{19,3},{4,20},{20... | collective-permute-start | bytes 14155784 | tf_op jit(solution)/shard_map/ppermute | solution.py:21
  33.3 13.0 %collective-permute-start.4 = (f32[2,768]{1,0:T(2,128)}, f32[2,768]{1,0:T(2,128)}, u32[]{:S(2)}, u32[]{:S(2)}) collective-permute-start(f32[2,768]{1,0:T(2,128)} %slice_bitcast_fusion.7), channel_id=1, source_target_pairs={{0,16},{16,0},{1,17},{17,1},{2,18},{18,2},{3,19},{19,3},{4,20},{20... | collective-permute-start | bytes 18440 | tf_op jit(solution)/shard_map/ppermute | solution.py:21
  46.4 58.7 %collective-permute-start.3 = (bf16[768,768]{1,0:T(8,128)(2,1)}, bf16[768,768]{1,0:T(8,128)(2,1)}, u32[]{:S(2)}, u32[]{:S(2)}) collective-permute-start(bf16[768,768]{1,0:T(8,128)(2,1)} %slice_bitcast_fusion.3), channel_id=1, source_target_pairs={{0,16},{16,0},{1,17},{17,1},{2,18},{18,2},{3,19},{19,3},{4,20},{20... | collective-permute-start | bytes 3538952 | tf_op jit(solution)/shard_map/ppermute | solution.py:21
  47.7 67.6 %copy-start.130 = (f32[768]{0:T(1024)}, f32[768]{0:T(1024)S(1)}, u32[]{:S(2)}) copy-start(f32[768]{0:T(1024)S(1)} %get-tuple-element.159) | copy-start | bytes 9220
  48.4 32.8 %collective-permute-start.1 = (bf16[768,2304]{1,0:T(8,128)(2,1)}, bf16[768,2304]{1,0:T(8,128)(2,1)}, u32[]{:S(2)}, u32[]{:S(2)}) collective-permute-start(bf16[768,2304]{1,0:T(8,128)(2,1)} %slice_bitcast_fusion.2), channel_id=1, source_target_pairs={{0,16},{16,0},{1,17},{17,1},{2,18},{18,2},{3,19},{19,3},{4,20},{20... | collective-permute-start | bytes 10616840 | tf_op jit(solution)/shard_map/ppermute | solution.py:21
  50.1 62.6 %collective-permute-start.7 = (bf16[3072,768]{1,0:T(8,128)(2,1)}, bf16[3072,768]{1,0:T(8,128)(2,1)}, u32[]{:S(2)}, u32[]{:S(2)}) collective-permute-start(bf16[3072,768]{1,0:T(8,128)(2,1)} %slice_bitcast_fusion), channel_id=1, source_target_pairs={{0,16},{16,0},{1,17},{17,1},{2,18},{18,2},{3,19},{19,3},{4,20},{20... | collective-permute-start | bytes 14155784 | tf_op jit(solution)/shard_map/ppermute | solution.py:21
  157.4 2.5 collective-permute-start.9
  162.6 13.5 %collective-permute-start.10 = (bf16[8,768]{1,0:T(8,128)(2,1)}, bf16[8,768]{1,0:T(8,128)(2,1)}, u32[]{:S(2)}, u32[]{:S(2)}) collective-permute-start(bf16[8,768]{1,0:T(8,128)(2,1)} %pad_maximum_fusion.9), channel_id=1, source_target_pairs={{0,1},{1,0},{2,3},{3,2},{4,5},{5,4},{6,7},{7,6},{8,9},{9,8},{10,11... | collective-permute-start | bytes 36872 | tf_op jit(solution)/shard_map/ppermute | solution.py:26
  165.5 10.6 %collective-permute-start.11 = (bf16[8,768]{1,0:T(8,128)(2,1)}, bf16[8,768]{1,0:T(8,128)(2,1)}, u32[]{:S(2)}, u32[]{:S(2)}) collective-permute-start(bf16[8,768]{1,0:T(8,128)(2,1)} %pad_maximum_fusion.9), channel_id=1, source_target_pairs={{0,2},{1,3},{2,0},{3,1},{4,6},{5,7},{6,4},{7,5},{8,10},{9,11},{10,... | collective-permute-start | bytes 36872 | tf_op jit(solution)/shard_map/ppermute | solution.py:26
  167.0 9.1 %collective-permute-start.12 = (bf16[8,768]{1,0:T(8,128)(2,1)}, bf16[8,768]{1,0:T(8,128)(2,1)}, u32[]{:S(2)}, u32[]{:S(2)}) collective-permute-start(bf16[8,768]{1,0:T(8,128)(2,1)} %pad_maximum_fusion.9), channel_id=1, source_target_pairs={{0,3},{1,2},{2,1},{3,0},{4,7},{5,6},{6,5},{7,4},{8,11},{9,10},{10,... | collective-permute-start | bytes 36872 | tf_op jit(solution)/shard_map/ppermute | solution.py:26
  181.4 5.7 collective-permute-start.13
  183.4 6.1 collective-permute-start.14
  186.0 6.2 collective-permute-start.15
  186.9 246.4 %collective-permute-start.8 = (bf16[3,128,768]{2,1,0:T(8,128)(2,1)}, bf16[3,128,768]{2,1,0:T(8,128)(2,1)}, u32[]{:S(2)}, u32[]{:S(2)}) collective-permute-start(bf16[3,128,768]{2,1,0:T(8,128)(2,1)} %broadcast_select_fusion.42), channel_id=1, source_target_pairs={{0,16},{16,0},{1,17},{17,1},{2,18},{18,2},{3,19},{19,3},{4,20},{20... | collective-permute-start | bytes 1769480 | tf_op jit(solution)/shard_map/ppermute | solution.py:21
  346.4 43.3 %collective-permute-start.16 = (bf16[64,768]{1,0:T(8,128)(2,1)}, bf16[64,768]{1,0:T(8,128)(2,1)S(1)}, u32[]{:S(2)}, u32[]{:S(2)}) collective-permute-start(bf16[64,768]{1,0:T(8,128)(2,1)} %fusion.203), channel_id=1, source_target_pairs={{0,16},{16,0},{1,17},{17,1},{2,18},{18,2},{3,19},{19,3},{4,20},{20... | collective-permute-start | bytes 294920 | tf_op jit(solution)/shard_map/ppermute | solution.py:21
  354.8 80.8 %collective-permute-start.17 = (f32[3,128,768]{2,1,0:T(8,128)}, f32[3,128,768]{2,1,0:T(8,128)}, u32[]{:S(2)}, u32[]{:S(2)}) collective-permute-start(f32[3,128,768]{2,1,0:T(8,128)} %bitcast.46), channel_id=1, source_target_pairs={{0,16},{16,0},{1,17},{17,1},{2,18},{18,2},{3,19},{19,3},{4,20},{20... | collective-permute-start | bytes 3538952 | tf_op jit(solution)/shard_map/ppermute | solution.py:21
  361.2 124.2 %collective-permute-start.22 = (bf16[768,1536]{1,0:T(8,128)(2,1)}, bf16[768,1536]{1,0:T(8,128)(2,1)}, u32[]{:S(2)}, u32[]{:S(2)}) collective-permute-start(bf16[768,1536]{1,0:T(8,128)(2,1)} %pad_maximum_fusion.2), channel_id=1, source_target_pairs={{0,16},{16,0},{1,17},{17,1},{2,18},{18,2},{3,19},{19,3},{4,20},{20... | collective-permute-start | bytes 7077896 | tf_op jit(solution)/shard_map/ppermute | solution.py:21
  375.7 11.4 %collective-permute-start.57 = (f32[16,576]{1,0:T(8,128)}, f32[16,576]{1,0:T(8,128)S(1)}, u32[]{:S(2)}, u32[]{:S(2)}) collective-permute-start(f32[16,576]{1,0:T(8,128)} %fusion.320), channel_id=1, source_target_pairs={{0,16},{16,0},{1,17},{17,1},{2,18},{18,2},{3,19},{19,3},{4,20},{20... | collective-permute-start | bytes 110600 | tf_op jit(solution)/shard_map/ppermute | solution.py:21
  387.7 102.0 %collective-permute-start.27 = (bf16[768,1536]{1,0:T(8,128)(2,1)}, bf16[768,1536]{1,0:T(8,128)(2,1)}, u32[]{:S(2)}, u32[]{:S(2)}) collective-permute-start(bf16[768,1536]{1,0:T(8,128)(2,1)} %pad_maximum_fusion.3), channel_id=1, source_target_pairs={{0,16},{16,0},{1,17},{17,1},{2,18},{18,2},{3,19},{19,3},{4,20},{20... | collective-permute-start | bytes 7077896 | tf_op jit(solution)/shard_map/ppermute | solution.py:21
  410.8 4.4 collective-permute-start.58
  415.3 3.8 collective-permute-start.59
  419.2 3.7 collective-permute-start.60
  422.9 6.0 collective-permute-start.61
  429.0 27.0 %collective-permute-start.18 = (bf16[64,9600]{1,0:T(8,128)(2,1)}, bf16[64,9600]{1,0:T(8,128)(2,1)}, u32[]{:S(2)}, u32[]{:S(2)}) collective-permute-start(bf16[64,9600]{1,0:T(8,128)(2,1)} %get-tuple-element.177), channel_id=1, source_target_pairs={{0,1},{1,0},{2,3},{3,2},{4,5},{5,4},{6,7},{7,6},{8,9},{9,8},{10,11... | collective-permute-start | bytes 3686408 | tf_op jit(solution)/shard_map/ppermute | solution.py:26
  433.3 48.3 %collective-permute-start.33 = (bf16[768,1536]{1,0:T(8,128)(2,1)}, bf16[768,1536]{1,0:T(8,128)(2,1)}, u32[]{:S(2)}, u32[]{:S(2)}) collective-permute-start(bf16[768,1536]{1,0:T(8,128)(2,1)} %constant_dynamic-slice_fusion.17), channel_id=1, source_target_pairs={{0,16},{16,0},{1,17},{17,1},{2,18},{18,2},{3,19},{19,3},{4,20},{20... | collective-permute-start | bytes 7077896 | tf_op jit(solution)/shard_map/ppermute | solution.py:21
  435.6 60.6 %collective-permute-start.38 = (bf16[768,1536]{1,0:T(8,128)(2,1)}, bf16[768,1536]{1,0:T(8,128)(2,1)}, u32[]{:S(2)}, u32[]{:S(2)}) collective-permute-start(bf16[768,1536]{1,0:T(8,128)(2,1)} %constant_dynamic-slice_fusion.14), channel_id=1, source_target_pairs={{0,16},{16,0},{1,17},{17,1},{2,18},{18,2},{3,19},{19,3},{4,20},{20... | collective-permute-start | bytes 7077896 | tf_op jit(solution)/shard_map/ppermute | solution.py:21
  456.0 43.9 %collective-permute-start.46 = (bf16[3072,384]{1,0:T(8,128)(2,1)}, bf16[3072,384]{1,0:T(8,128)(2,1)}, u32[]{:S(2)}, u32[]{:S(2)}) collective-permute-start(bf16[3072,384]{1,0:T(8,128)(2,1)} %constant_dynamic-slice_fusion.11), channel_id=1, source_target_pairs={{0,16},{16,0},{1,17},{17,1},{2,18},{18,2},{3,19},{19,3},{4,20},{20... | collective-permute-start | bytes 7077896 | tf_op jit(solution)/shard_map/ppermute | solution.py:21
  481.6 22.0 %collective-permute-start.51 = (bf16[3072,384]{1,0:T(8,128)(2,1)}, bf16[3072,384]{1,0:T(8,128)(2,1)S(1)}, u32[]{:S(2)}, u32[]{:S(2)}) collective-permute-start(bf16[3072,384]{1,0:T(8,128)(2,1)} %constant_dynamic-slice_fusion.8), channel_id=1, source_target_pairs={{0,16},{16,0},{1,17},{17,1},{2,18},{18,2},{3,19},{19,3},{4,20},{20... | collective-permute-start | bytes 7077896 | tf_op jit(solution)/shard_map/ppermute | solution.py:21
  485.5 48.9 %collective-permute-start.19 = (bf16[128,8256]{0,1:T(8,128)(2,1)S(1)}, bf16[128,8256]{0,1:T(8,128)(2,1)S(1)}, u32[]{:S(2)}, u32[]{:S(2)}) collective-permute-start(bf16[128,8256]{0,1:T(8,128)(2,1)S(1)} %copy-done.54), channel_id=1, source_target_pairs={{0,2},{1,3},{2,0},{3,1},{4,6},{5,7},{6,4},{7,5},{8,10},{9,11},{10,... | collective-permute-start | bytes 6340616 | tf_op jit(solution)/shard_map/ppermute | solution.py:26
  489.7 52.0 %collective-permute-start.23 = (bf16[2,2,2,48,1536]{4,3,0,1,2:T(8,128)(2,1)S(1)}, bf16[2,2,2,48,1536]{4,3,0,1,2:T(8,128)(2,1)S(1)}, u32[]{:S(2)}, u32[]{:S(2)}) collective-permute-start(bf16[2,2,2,48,1536]{4,3,0,1,2:T(8,128)(2,1)S(1)} %bitcast.740), channel_id=1, source_target_pairs={{0,4},{1,5},{2,6},{3,7},{4,0},{5,1},{6,2},{7,3},{8,12},{9,13},{10,... | collective-permute-start | bytes 3538952 | tf_op jit(solution)/shard_map/ppermute | solution.py:26
  496.2 46.4 %collective-permute-start.28 = (bf16[2,2,2,48,1536]{4,3,0,1,2:T(8,128)(2,1)}, bf16[2,2,2,48,1536]{4,3,0,1,2:T(8,128)(2,1)S(1)}, u32[]{:S(2)}, u32[]{:S(2)}) collective-permute-start(bf16[2,2,2,48,1536]{4,3,0,1,2:T(8,128)(2,1)} %bitcast.669), channel_id=1, source_target_pairs={{0,4},{1,5},{2,6},{3,7},{4,0},{5,1},{6,2},{7,3},{8,12},{9,13},{10,... | collective-permute-start | bytes 3538952 | tf_op jit(solution)/shard_map/ppermute | solution.py:26
  499.8 59.9 %collective-permute-start.34 = (bf16[2,2,2,48,1536]{4,3,0,1,2:T(8,128)(2,1)}, bf16[2,2,2,48,1536]{4,3,0,1,2:T(8,128)(2,1)S(1)}, u32[]{:S(2)}, u32[]{:S(2)}) collective-permute-start(bf16[2,2,2,48,1536]{4,3,0,1,2:T(8,128)(2,1)} %bitcast.668), channel_id=1, source_target_pairs={{0,2},{1,3},{2,0},{3,1},{4,6},{5,7},{6,4},{7,5},{8,10},{9,11},{10,... | collective-permute-start | bytes 3538952 | tf_op jit(solution)/shard_map/ppermute | solution.py:26
  503.6 80.2 %collective-permute-start.39 = (bf16[2,2,2,48,1536]{4,3,0,1,2:T(8,128)(2,1)S(1)}, bf16[2,2,2,48,1536]{4,3,0,1,2:T(8,128)(2,1)S(1)}, u32[]{:S(2)}, u32[]{:S(2)}) collective-permute-start(bf16[2,2,2,48,1536]{4,3,0,1,2:T(8,128)(2,1)S(1)} %bitcast.739), channel_id=1, source_target_pairs={{0,2},{1,3},{2,0},{3,1},{4,6},{5,7},{6,4},{7,5},{8,10},{9,11},{10,... | collective-permute-start | bytes 3538952 | tf_op jit(solution)/shard_map/ppermute | solution.py:26
  534.4 28.9 %collective-permute-start.47 = (bf16[2,2,2,192,384]{4,3,0,1,2:T(8,128)(2,1)S(1)}, bf16[2,2,2,192,384]{4,3,0,1,2:T(8,128)(2,1)S(1)}, u32[]{:S(2)}, u32[]{:S(2)}) collective-permute-start(bf16[2,2,2,192,384]{4,3,0,1,2:T(8,128)(2,1)S(1)} %bitcast.742), channel_id=1, source_target_pairs={{0,1},{1,0},{2,3},{3,2},{4,5},{5,4},{6,7},{7,6},{8,9},{9,8},{10,11... | collective-permute-start | bytes 3538952 | tf_op jit(solution)/shard_map/ppermute | solution.py:26
  541.7 46.9 %collective-permute-start.52 = (bf16[2,2,2,192,384]{4,3,0,1,2:T(8,128)(2,1)S(1)}, bf16[2,2,2,192,384]{4,3,0,1,2:T(8,128)(2,1)S(1)}, u32[]{:S(2)}, u32[]{:S(2)}) collective-permute-start(bf16[2,2,2,192,384]{4,3,0,1,2:T(8,128)(2,1)S(1)} %bitcast.741), channel_id=1, source_target_pairs={{0,1},{1,0},{2,3},{3,2},{4,5},{5,4},{6,7},{7,6},{8,9},{9,8},{10,11... | collective-permute-start | bytes 3538952 | tf_op jit(solution)/shard_map/ppermute | solution.py:26
  542.6 152.1 %collective-permute-start.20 = (bf16[2,48,6144]{2,1,0:T(8,128)(2,1)S(1)}, bf16[2,48,6144]{2,1,0:T(8,128)(2,1)S(1)}, u32[]{:S(2)}, u32[]{:S(2)}) collective-permute-start(bf16[2,48,6144]{2,1,0:T(8,128)(2,1)S(1)} %dynamic-slice_bitcast_fusion), channel_id=1, source_target_pairs={{0,4},{1,5},{2,6},{3,7},{4,0},{5,1},{6,2},{7,3},{8,12},{9,13},{10,... | collective-permute-start | bytes 3538952 | tf_op jit(solution)/shard_map/ppermute | solution.py:26
  559.7 30.9 %collective-permute-start.44 = (bf16[2,192,768]{2,1,0:T(8,128)(2,1)S(1)}, bf16[2,192,768]{2,1,0:T(8,128)(2,1)S(1)}, u32[]{:S(2)}, u32[]{:S(2)}) collective-permute-start(bf16[2,192,768]{2,1,0:T(8,128)(2,1)S(1)} %dynamic-slice_bitcast_fusion.3), channel_id=1, source_target_pairs={{0,4},{1,5},{2,6},{3,7},{4,0},{5,1},{6,2},{7,3},{8,12},{9,13},{10,... | collective-permute-start | bytes 1769480 | tf_op jit(solution)/shard_map/ppermute | solution.py:26
  563.3 37.9 %collective-permute-start.24 = (bf16[2,2,48,1536]{3,2,0,1:T(8,128)(2,1)S(1)}, bf16[2,2,48,1536]{3,2,0,1:T(8,128)(2,1)S(1)}, u32[]{:S(2)}, u32[]{:S(2)}) collective-permute-start(bf16[2,2,48,1536]{3,2,0,1:T(8,128)(2,1)S(1)} %dynamic-slice_bitcast_fusion.7), channel_id=1, source_target_pairs={{0,1},{1,0},{2,3},{3,2},{4,5},{5,4},{6,7},{7,6},{8,9},{9,8},{10,11... | collective-permute-start | bytes 1769480 | tf_op jit(solution)/shard_map/ppermute | solution.py:26
  583.9 30.0 %collective-permute-start.29 = (bf16[2,2,48,1536]{3,2,0,1:T(8,128)(2,1)S(1)}, bf16[2,2,48,1536]{3,2,0,1:T(8,128)(2,1)S(1)}, u32[]{:S(2)}, u32[]{:S(2)}) collective-permute-start(bf16[2,2,48,1536]{3,2,0,1:T(8,128)(2,1)S(1)} %dynamic-slice_bitcast_fusion.6), channel_id=1, source_target_pairs={{0,1},{1,0},{2,3},{3,2},{4,5},{5,4},{6,7},{7,6},{8,9},{9,8},{10,11... | collective-permute-start | bytes 1769480 | tf_op jit(solution)/shard_map/ppermute | solution.py:26
  588.6 37.9 %collective-permute-start.35 = (bf16[2,2,48,1536]{3,2,0,1:T(8,128)(2,1)S(1)}, bf16[2,2,48,1536]{3,2,0,1:T(8,128)(2,1)S(1)}, u32[]{:S(2)}, u32[]{:S(2)}) collective-permute-start(bf16[2,2,48,1536]{3,2,0,1:T(8,128)(2,1)S(1)} %dynamic-slice_bitcast_fusion.5), channel_id=1, source_target_pairs={{0,1},{1,0},{2,3},{3,2},{4,5},{5,4},{6,7},{7,6},{8,9},{9,8},{10,11... | collective-permute-start | bytes 1769480 | tf_op jit(solution)/shard_map/ppermute | solution.py:26
  590.6 45.5 %collective-permute-start.40 = (bf16[2,2,48,1536]{3,2,0,1:T(8,128)(2,1)S(1)}, bf16[2,2,48,1536]{3,2,0,1:T(8,128)(2,1)S(1)}, u32[]{:S(2)}, u32[]{:S(2)}) collective-permute-start(bf16[2,2,48,1536]{3,2,0,1:T(8,128)(2,1)S(1)} %dynamic-slice_bitcast_fusion.4), channel_id=1, source_target_pairs={{0,1},{1,0},{2,3},{3,2},{4,5},{5,4},{6,7},{7,6},{8,9},{9,8},{10,11... | collective-permute-start | bytes 1769480 | tf_op jit(solution)/shard_map/ppermute | solution.py:26
  601.2 28.1 %collective-permute-start.48 = (bf16[2,2,192,384]{3,2,0,1:T(8,128)(2,1)S(1)}, bf16[2,2,192,384]{3,2,0,1:T(8,128)(2,1)S(1)}, u32[]{:S(2)}, u32[]{:S(2)}) collective-permute-start(bf16[2,2,192,384]{3,2,0,1:T(8,128)(2,1)S(1)} %dynamic-slice_bitcast_fusion.2), channel_id=1, source_target_pairs={{0,2},{1,3},{2,0},{3,1},{4,6},{5,7},{6,4},{7,5},{8,10},{9,11},{10,... | collective-permute-start | bytes 1769480 | tf_op jit(solution)/shard_map/ppermute | solution.py:26
  613.9 23.9 %collective-permute-start.53 = (bf16[2,2,192,384]{3,2,0,1:T(8,128)(2,1)S(1)}, bf16[2,2,192,384]{3,2,0,1:T(8,128)(2,1)S(1)}, u32[]{:S(2)}, u32[]{:S(2)}) collective-permute-start(bf16[2,2,192,384]{3,2,0,1:T(8,128)(2,1)S(1)} %dynamic-slice_bitcast_fusion.1), channel_id=1, source_target_pairs={{0,2},{1,3},{2,0},{3,1},{4,6},{5,7},{6,4},{7,5},{8,10},{9,11},{10,... | collective-permute-start | bytes 1769480 | tf_op jit(solution)/shard_map/ppermute | solution.py:26
  626.5 12.4 %collective-permute-start.45 = (bf16[192,768]{1,0:T(8,128)(2,1)S(1)}, bf16[192,768]{1,0:T(8,128)(2,1)S(1)}, u32[]{:S(2)}, u32[]{:S(2)}) collective-permute-start(bf16[192,768]{1,0:T(8,128)(2,1)S(1)} %dynamic-slice_bitcast_fusion.11), channel_id=1, source_target_pairs={{0,8},{1,9},{2,10},{3,11},{4,12},{5,13},{6,14},{7,15},{8,0},{9,1},... | collective-permute-start | bytes 884744 | tf_op jit(solution)/shard_map/ppermute | solution.py:26
  629.4 10.9 %collective-permute-start.25 = (bf16[2,48,1536]{2,1,0:T(8,128)(2,1)S(1)}, bf16[2,48,1536]{2,1,0:T(8,128)(2,1)S(1)}, u32[]{:S(2)}, u32[]{:S(2)}) collective-permute-start(bf16[2,48,1536]{2,1,0:T(8,128)(2,1)S(1)} %dynamic-slice_bitcast_fusion.15), channel_id=1, source_target_pairs={{0,2},{1,3},{2,0},{3,1},{4,6},{5,7},{6,4},{7,5},{8,10},{9,11},{10,... | collective-permute-start | bytes 884744 | tf_op jit(solution)/shard_map/ppermute | solution.py:26
  636.1 6.7 collective-permute-start.30
  637.7 11.6 %collective-permute-start.36 = (bf16[2,48,1536]{2,1,0:T(8,128)(2,1)S(1)}, bf16[2,48,1536]{2,1,0:T(8,128)(2,1)S(1)}, u32[]{:S(2)}, u32[]{:S(2)}) collective-permute-start(bf16[2,48,1536]{2,1,0:T(8,128)(2,1)S(1)} %dynamic-slice_bitcast_fusion.13), channel_id=1, source_target_pairs={{0,4},{1,5},{2,6},{3,7},{4,0},{5,1},{6,2},{7,3},{8,12},{9,13},{10,... | collective-permute-start | bytes 884744 | tf_op jit(solution)/shard_map/ppermute | solution.py:26
  638.9 19.9 %collective-permute-start.41 = (bf16[2,48,1536]{2,1,0:T(8,128)(2,1)S(1)}, bf16[2,48,1536]{2,1,0:T(8,128)(2,1)S(1)}, u32[]{:S(2)}, u32[]{:S(2)}) collective-permute-start(bf16[2,48,1536]{2,1,0:T(8,128)(2,1)S(1)} %dynamic-slice_bitcast_fusion.12), channel_id=1, source_target_pairs={{0,4},{1,5},{2,6},{3,7},{4,0},{5,1},{6,2},{7,3},{8,12},{9,13},{10,... | collective-permute-start | bytes 884744 | tf_op jit(solution)/shard_map/ppermute | solution.py:26
  640.3 27.0 %collective-permute-start.49 = (bf16[2,192,384]{2,1,0:T(8,128)(2,1)S(1)}, bf16[2,192,384]{2,1,0:T(8,128)(2,1)S(1)}, u32[]{:S(2)}, u32[]{:S(2)}) collective-permute-start(bf16[2,192,384]{2,1,0:T(8,128)(2,1)S(1)} %dynamic-slice_bitcast_fusion.10), channel_id=1, source_target_pairs={{0,4},{1,5},{2,6},{3,7},{4,0},{5,1},{6,2},{7,3},{8,12},{9,13},{10,... | collective-permute-start | bytes 884744 | tf_op jit(solution)/shard_map/ppermute | solution.py:26
  642.8 27.8 %collective-permute-start.54 = (bf16[2,192,384]{2,1,0:T(8,128)(2,1)S(1)}, bf16[2,192,384]{2,1,0:T(8,128)(2,1)S(1)}, u32[]{:S(2)}, u32[]{:S(2)}) collective-permute-start(bf16[2,192,384]{2,1,0:T(8,128)(2,1)S(1)} %dynamic-slice_bitcast_fusion.9), channel_id=1, source_target_pairs={{0,4},{1,5},{2,6},{3,7},{4,0},{5,1},{6,2},{7,3},{8,12},{9,13},{10,... | collective-permute-start | bytes 884744 | tf_op jit(solution)/shard_map/ppermute | solution.py:26
  649.3 21.8 %collective-permute-start.26 = (bf16[48,1536]{1,0:T(8,128)(2,1)S(1)}, bf16[48,1536]{1,0:T(8,128)(2,1)S(1)}, u32[]{:S(2)}, u32[]{:S(2)}) collective-permute-start(bf16[48,1536]{1,0:T(8,128)(2,1)S(1)} %dynamic-slice_bitcast_fusion.21), channel_id=1, source_target_pairs={{0,8},{1,9},{2,10},{3,11},{4,12},{5,13},{6,14},{7,15},{8,0},{9,1},... | collective-permute-start | bytes 442376 | tf_op jit(solution)/shard_map/ppermute | solution.py:26
  658.8 14.9 %collective-permute-start.31 = (bf16[48,1536]{1,0:T(8,128)(2,1)S(1)}, bf16[48,1536]{1,0:T(8,128)(2,1)S(1)}, u32[]{:S(2)}, u32[]{:S(2)}) collective-permute-start(bf16[48,1536]{1,0:T(8,128)(2,1)S(1)} %dynamic-slice_bitcast_fusion.20), channel_id=1, source_target_pairs={{0,8},{1,9},{2,10},{3,11},{4,12},{5,13},{6,14},{7,15},{8,0},{9,1},... | collective-permute-start | bytes 442376 | tf_op jit(solution)/shard_map/ppermute | solution.py:26
  667.3 19.4 %collective-permute-start.37 = (bf16[48,1536]{1,0:T(8,128)(2,1)S(1)}, bf16[48,1536]{1,0:T(8,128)(2,1)S(1)}, u32[]{:S(2)}, u32[]{:S(2)}) collective-permute-start(bf16[48,1536]{1,0:T(8,128)(2,1)S(1)} %dynamic-slice_bitcast_fusion.19), channel_id=1, source_target_pairs={{0,8},{1,9},{2,10},{3,11},{4,12},{5,13},{6,14},{7,15},{8,0},{9,1},... | collective-permute-start | bytes 442376 | tf_op jit(solution)/shard_map/ppermute | solution.py:26
  670.6 19.3 %collective-permute-start.42 = (bf16[48,1536]{1,0:T(8,128)(2,1)S(1)}, bf16[48,1536]{1,0:T(8,128)(2,1)S(1)}, u32[]{:S(2)}, u32[]{:S(2)}) collective-permute-start(bf16[48,1536]{1,0:T(8,128)(2,1)S(1)} %dynamic-slice_bitcast_fusion.18), channel_id=1, source_target_pairs={{0,8},{1,9},{2,10},{3,11},{4,12},{5,13},{6,14},{7,15},{8,0},{9,1},... | collective-permute-start | bytes 442376 | tf_op jit(solution)/shard_map/ppermute | solution.py:26
  671.2 21.7 %collective-permute-start.50 = (bf16[192,384]{1,0:T(8,128)(2,1)S(1)}, bf16[192,384]{1,0:T(8,128)(2,1)S(1)}, u32[]{:S(2)}, u32[]{:S(2)}) collective-permute-start(bf16[192,384]{1,0:T(8,128)(2,1)S(1)} %dynamic-slice_bitcast_fusion.17), channel_id=1, source_target_pairs={{0,8},{1,9},{2,10},{3,11},{4,12},{5,13},{6,14},{7,15},{8,0},{9,1},... | collective-permute-start | bytes 442376 | tf_op jit(solution)/shard_map/ppermute | solution.py:26
  673.7 20.8 %collective-permute-start.55 = (bf16[192,384]{1,0:T(8,128)(2,1)S(1)}, bf16[192,384]{1,0:T(8,128)(2,1)S(1)}, u32[]{:S(2)}, u32[]{:S(2)}) collective-permute-start(bf16[192,384]{1,0:T(8,128)(2,1)S(1)} %dynamic-slice_bitcast_fusion.16), channel_id=1, source_target_pairs={{0,8},{1,9},{2,10},{3,11},{4,12},{5,13},{6,14},{7,15},{8,0},{9,1},... | collective-permute-start | bytes 442376 | tf_op jit(solution)/shard_map/ppermute | solution.py:26
  686.7 8.4 %collective-permute-start.32 = (f32[48,1536]{1,0:T(8,128)S(1)}, f32[48,1536]{1,0:T(8,128)S(1)}, u32[]{:S(2)}, u32[]{:S(2)}) collective-permute-start(f32[48,1536]{1,0:T(8,128)S(1)} %fusion.255), channel_id=1, source_target_pairs={{0,16},{16,0},{1,17},{17,1},{2,18},{18,2},{3,19},{19,3},{4,20},{20... | collective-permute-start | bytes 884744 | tf_op jit(solution)/shard_map/ppermute | solution.py:21
  689.9 6.5 collective-permute-start.43
  694.6 1.6 collective-permute-start.56
  695.0 27.2 %collective-permute-start.21 = (bf16[48,6144]{1,0:T(8,128)(2,1)S(1)}, bf16[48,6144]{1,0:T(8,128)(2,1)S(1)}, u32[]{:S(2)}, u32[]{:S(2)}) collective-permute-start(bf16[48,6144]{1,0:T(8,128)(2,1)S(1)} %dynamic-slice_bitcast_fusion.8), channel_id=1, source_target_pairs={{0,8},{1,9},{2,10},{3,11},{4,12},{5,13},{6,14},{7,15},{8,0},{9,1},... | collective-permute-start | bytes 1769480 | tf_op jit(solution)/shard_map/ppermute | solution.py:26
  (302 other events, 1385.7 us)

commit v2 on v1

v2 whole, which is shorter than its diff:
```python
import jax
import jax.numpy as jnp
from jax import lax
from jax.experimental import pallas as pl
from jax.experimental.pallas import tpu as pltpu
from jax.sharding import PartitionSpec as P

HEADS = 12
HEAD_DIM = 64


NORM_EPS = 1e-05
SQRT_HALF = 0.7071067811865476
ROOT_TAU_INV = 0.3989422804014327
MASK_FILL = -1e30
LOGIT_GAIN = 2.5
PRECISE = lax.Precision.HIGHEST


def core_swap(block):
    return lax.ppermute(block, "section", [(0, 1), (1, 0)])


def flip_swap(block, bit):
    size = lax.axis_size("batch")
    return lax.ppermute(block, "batch", [(i, i ^ bit) for i in range(size)])


F32 = jnp.float32
LOW = jnp.bfloat16
VMEM_LIMIT = 58 * 1024 * 1024
BLOCKS = 16
IS_FIRST, CORE, PLACES, Z_PLACES, X_BIT, Y_BIT, LENGTHS = 0, 1, 2, 50, 54, 55, 56
ORDERS = ((1, 2, 4, 8), (2, 1, 4, 8), (4, 1, 2, 8))


def mm(left, right):
    return lax.dot_general(left, right, (((1,), (0,)), ((), ())), preferred_element_type=F32)


def mm_nt(left, right):
    return lax.dot_general(left, right, (((1,), (1,)), ((), ())), preferred_element_type=F32)


def mm_tn(left, right):
    return lax.dot_general(left, right, (((0,), (0,)), ((), ())), preferred_element_type=F32)


def row_mean(values):
    return jnp.sum(values, axis=-1, keepdims=True) * (1.0 / values.shape[-1])


def normed_rows(values):
    center = values - row_mean(values)
    inverse = lax.rsqrt(row_mean(center * center) + NORM_EPS)
    return center * inverse, inverse


def norm_pull(upstream, normed, inverse, gain):
    scaled = upstream * gain
    return inverse * (scaled - row_mean(scaled) - normed * row_mean(scaled * normed))


def col_sum(values):
    return jnp.sum(values, axis=0, keepdims=True)


class Moves:
    def __init__(self, sems):
        self.sems = sems
        self.used = 0
        self.open = []

    def slot(self):
        self.used += 1
        return self.sems.at[self.used - 1]

    def fetch(self, source, target):
        copy = pltpu.make_async_copy(source, target, self.slot())
        copy.start()
        return copy

    def fetch_either(self, flag, first, second, target):
        sem = self.slot()
        copy = pltpu.make_async_copy(first, target, sem)
        if second is None:
            copy.start()
            return copy
        other = pltpu.make_async_copy(second, target, sem)

        @pl.when(flag)
        def _():
            copy.start()

        @pl.when(jnp.logical_not(flag))
        def _():
            other.start()

        return copy

    def store(self, source, target):
        self.open.append(self.fetch(source, target))

    def drain(self):
        for copy in self.open:
            copy.wait()


class Tower:
    def __init__(self, index, info, weights, others, small, small_other, seqs, slots, first_len):
        self.index = index
        self.info = info
        self.weights = weights
        self.others = others
        self.small = small
        self.small_other = small_other
        self.seqs = seqs
        self.slots = slots
        self.first_len = first_len
        self.count = seqs * slots
        self.width = weights[1].shape[-1]
        self.wide = weights[2].shape[-1]
        self.group = self.count if self.count <= 128 else slots
        self.shared = others is not None

    def given(self, which):
        own = [self.weights[at] for at in which]
        return own + ([self.others[at] for at in which] if self.shared else [])

    def given_small(self):
        return list(self.small) + ([self.small_other] if self.shared else [])

    def use_own(self, info, layer):
        return info[IS_FIRST] == (1 if layer == 0 else 0)

    def lengths_at(self, info):
        return self.first_len + (info[CORE] * self.seqs if self.shared else 0)

    def row_start(self, info):
        return pl.multiple_of(info[CORE] * self.count, self.count) if self.shared else 0

    def small_rows(self, refs, flag):
        own = [refs[0][0, self.index], refs[1][0, self.index]]
        if self.shared:
            other = refs[3]
            own = [
                jnp.where(flag, own[0], other[0:2, :]),
                jnp.where(flag, own[1], other[2:8, :]),
            ]
        return own

    def hidden_bias(self, refs, flag, step, tile):
        own = refs[2][0, self.index : self.index + 1, step * tile : (step + 1) * tile]
        if self.shared:
            own = jnp.where(flag, own, refs[3][8 + step : 9 + step, :])
        return own


ANYWHERE = pl.BlockSpec(memory_space=pl.ANY)
SCALARS = pl.BlockSpec(memory_space=pltpu.SMEM)
INSIDE = pl.BlockSpec(memory_space=pltpu.VMEM)


def call_kernel(kernel, name, inputs, outs, scratch, copies, flops, after):
    count = len(inputs)
    extra = len(after)

    def body(*refs):
        refs = list(refs)
        kernel(
            refs[:count],
            refs[count + extra : count + extra + len(outs)],
            refs[count + extra + len(outs) : -1],
            Moves(refs[-1]),
        )

    return pl.pallas_call(
        body,
        out_shape=[jax.ShapeDtypeStruct(shape, kind) for shape, kind in outs],
        in_specs=[spec for spec, _ in inputs] + [ANYWHERE] * extra,
        out_specs=[ANYWHERE] * len(outs),
        scratch_shapes=[pltpu.VMEM(shape, kind) for shape, kind in scratch]
        + [pltpu.SemaphoreType.DMA((copies,))],
        compiler_params=pltpu.CompilerParams(vmem_limit_bytes=VMEM_LIMIT),
        cost_estimate=pl.CostEstimate(
            flops=flops, bytes_accessed=flops // 64, transcendentals=0
        ),
        name=name,
    )(*[array for _, array in inputs], *after)


def pair_masks(dtype):
    lanes = lax.broadcasted_iota(jnp.int32, (1, 128), 1)
    low = jnp.where(lanes < HEAD_DIM, 1.0, 0.0)
    return low.astype(dtype), (1.0 - low).astype(dtype)


def stacked_pair(block, low, high):
    return jnp.concatenate([block * low, block * high], axis=0)


def joined_pair(stacked, group):
    lanes = lax.broadcasted_iota(jnp.int32, (1, 128), 1)
    return jnp.where(lanes < HEAD_DIM, stacked[:group], stacked[group:])


def pair_softmax(query_stack, key_block, valid):
    scores = mm_nt(query_stack, key_block) * HEAD_DIM ** (-0.5)
    scores = jnp.where(valid, scores, MASK_FILL)
    exponent = jnp.exp(scores - jnp.max(scores, axis=-1, keepdims=True))
    return exponent * (1.0 / jnp.sum(exponent, axis=-1, keepdims=True))


def valid_keys(info, first_len, group, slots):
    rows = lax.broadcasted_iota(jnp.int32, (2 * group, group), 0)
    keys = lax.broadcasted_iota(jnp.int32, (2 * group, group), 1)
    seqs = group // slots
    if seqs == 1:
        return keys < info[first_len]
    rows = jnp.where(rows >= group, rows - group, rows)
    valid = None
    for j in range(seqs):
        low = j * slots
        inside = (
            (rows >= low)
            & (rows < low + slots)
            & (keys >= low)
            & (keys < low + info[first_len + j])
        )
        valid = inside if valid is None else valid | inside
    return valid


def forward_layer(tower, layer, rows, whole_rows, after=()):
    count, width, wide, group = tower.count, tower.width, tower.wide, tower.group
    tile = width

    def kernel(ins, outs, scratch, moves):
        info, x_any = ins[0], ins[1]
        weights = ins[2:6]
        others = ins[6:10] if tower.shared else [None] * 4
        smalls = ins[10:] if tower.shared else ins[6:]
        out_any, qkv_any, mix_any, low_any, act_any, slope_any, hat1_any, hat2_any, inv_any = outs
        x_v, w_qkv, w_out, w_up, w_down, acc_v = scratch[:6]
        out_v, qkv_v, mix_v, low_v, act_v, slope_v, hat1_v, hat2_v, inv_v = scratch[6:]
        use_own = tower.use_own(info, layer)
        if whole_rows:
            x_any = x_any.at[pl.ds(tower.row_start(info), count)]
        arrived = [moves.fetch(x_any, x_v)]
        for own, other, target in zip(weights, others, (w_qkv, w_out, w_up, w_down)):
            arrived.append(
                moves.fetch_either(use_own, own.at[0, tower.index], other, target)
            )
        gains, bias = tower.small_rows(smalls, use_own)
        arrived[0].wait()
        arrived[1].wait()
        x = x_v[...]
        for part in range(3):
            block = mm(x, w_qkv[:, part * width : (part + 1) * width])
            if part == 0:
                block = block + bias[0:1, :]
            if part == 2:
                block = block + bias[1:2, :]
            qkv_v[:, part * width : (part + 1) * width] = block.astype(LOW)
        moves.store(qkv_v, qkv_any)

        def one_group(g, carry):
            at = pl.ds(pl.multiple_of(g * group, group), group)
            valid = valid_keys(
                info, tower.lengths_at(info) + g * (group // tower.slots), group, tower.slots
            )
            low, high = pair_masks(LOW)
            for pair in range(width // 128):
                lane = pair * 128
                q2 = qkv_v[at, lane : lane + 128]
                k2 = qkv_v[at, width + lane : width + lane + 128]
                v2 = qkv_v[at, 2 * width + lane : 2 * width + lane + 128]
                soft = pair_softmax(stacked_pair(q2, low, high), k2, valid)
                mixed = joined_pair(mm(soft.astype(LOW), v2), group)
                mix_v[at, lane : lane + 128] = mixed.astype(LOW)
            return carry

        lax.fori_loop(0, count // group, one_group, 0)
        moves.store(mix_v, mix_any)
        arrived[2].wait()
        summed = x.astype(F32) + (mm(mix_v[...], w_out[...]) + bias[2:3, :])
        hat, inverse = normed_rows(summed)
        hat1_v[...] = hat
        inv_v[0] = jnp.broadcast_to(inverse, (count, 128))
        moves.store(hat1_v, hat1_any)
        first = hat * gains[0:1, :] + bias[3:4, :]
        low_v[...] = first.astype(LOW)
        moves.store(low_v, low_any)
        acc_v[...] = first + bias[4:5, :]
        arrived[3].wait()
        arrived[4].wait()
        for step in range(wide // tile):
            cols = slice(step * tile, (step + 1) * tile)
            hidden = mm(low_v[...], w_up[:, cols]) + tower.hidden_bias(
                smalls, use_own, step, tile
            )
            cdf = 0.5 * (1.0 + lax.erf(hidden * SQRT_HALF))
            act_v[:, cols] = (hidden * cdf).astype(LOW)
            slope_v[:, cols] = (
                cdf + hidden * (jnp.exp(-0.5 * hidden * hidden) * ROOT_TAU_INV)
            ).astype(LOW)
            acc_v[...] += mm(act_v[:, cols], w_down[cols, :])
        moves.store(act_v, act_any)
        moves.store(slope_v, slope_any)
        hat, inverse = normed_rows(acc_v[...])
        hat2_v[...] = hat
        moves.store(hat2_v, hat2_any)
        inv_v[1] = jnp.broadcast_to(inverse, (count, 128))
        moves.store(inv_v, inv_any)
        out_v[...] = (hat * gains[1:2, :] + bias[5:6, :]).astype(LOW)
        moves.store(out_v, out_any)
        moves.drain()

    outs = [
        ((count, width), LOW),
        ((count, 3 * width), LOW),
        ((count, width), LOW),
        ((count, width), LOW),
        ((count, wide), LOW),
        ((count, wide), LOW),
        ((count, width), F32),
        ((count, width), F32),
        ((2, count, 128), F32),
    ]
    scratch = [
        ((count, width), LOW),
        ((width, 3 * width), LOW),
        ((width, width), LOW),
        ((width, wide), LOW),
        ((wide, width), LOW),
        ((count, width), F32),
    ]
    inputs = [(SCALARS, tower.info), (ANYWHERE, rows)]
    inputs += [(ANYWHERE, array) for array in tower.given((0, 1, 2, 3))]
    inputs += [(INSIDE, array) for array in tower.given_small()]
    return call_kernel(
        kernel,
        "layer_forward",
        inputs,
        outs,
        scratch + outs,
        5 + len(outs),
        2 * max(count, 256) * (4 * width * width + 2 * width * wide),
        list(after),
    )


def place_rows(target, block, info, first, size, column=None):
    for piece in range(block.shape[0] // size):
        at = pl.multiple_of(info[first + piece] * size, size)
        rows = block[piece * size : (piece + 1) * size].astype(LOW)
        if column is None:
            target[pl.ds(at, size), :] = rows
        else:
            target[pl.ds(at, size), pl.ds(column[0], column[1])] = rows


def backward_wide(tower, layer, upstream, first_rows, kept, with_sums, after=()):
    act, slope, low, hat2, inverse = kept
    count, width, wide = tower.count, tower.width, tower.wide
    tile = width
    steps = wide // tile
    half = width // 2
    seeded = first_rows is not None

    def kernel(ins, outs, scratch, moves):
        ins = list(ins)
        info, up_any = ins.pop(0), ins.pop(0)
        first_ref = ins.pop(0) if seeded else None
        own_w = [ins.pop(0) for _ in range(2)]
        other_w = [ins.pop(0) for _ in range(2)] if tower.shared else [None] * 2
        act_any, slope_any, low_any, hat_any, inv_any = (ins.pop(0) for _ in range(5))
        smalls = ins
        w_up, w_down, up_v, act_v, slope_v, low_v, hat_v, inv_v = scratch[:8]
        da_any, df_any, dh_any, vec_any = outs[:4]
        da_v, df_v, dh_v, vec_v = scratch[8:12]
        if with_sums:
            down_send, down_keep, up_send, up_keep = scratch[12:]
        use_own = tower.use_own(info, layer)
        core_at = info[CORE]
        if seeded:
            up_any = up_any.at[pl.ds(tower.row_start(info), count)]
        got = [
            moves.fetch(up_any, up_v),
            moves.fetch(hat_any, hat_v),
            moves.fetch(inv_any.at[1], inv_v),
            moves.fetch_either(use_own, own_w[1].at[0, tower.index], other_w[1], w_down),
            moves.fetch(slope_any, slope_v),
            moves.fetch_either(use_own, own_w[0].at[0, tower.index], other_w[0], w_up),
            moves.fetch(low_any, low_v),
            moves.fetch(act_any, act_v),
        ]
        gains, _ = tower.small_rows(smalls, use_own)
        for copy in got[:3]:
            copy.wait()
        upward = up_v[...].astype(F32)
        if seeded:
            row_at = lax.broadcasted_iota(jnp.int32, (count, 1), 0)
            lengths = tower.lengths_at(info)
            seen = jnp.zeros((count, 1), F32)
            for seq in range(tower.seqs):
                start = seq * tower.slots
                inside_seq = (row_at >= start) & (row_at < start + info[lengths + seq])
                seen = jnp.where(inside_seq, 1.0, seen)
            upward = upward * seen
            for seq in range(tower.seqs):
                upward = upward + jnp.where(
                    row_at == seq * tower.slots, first_ref[seq : seq + 1, :], 0.0
                )
        hat = hat_v[...]
        vec_v[0:1, :] = col_sum(upward * hat)
        vec_v[1:2, :] = col_sum(upward)
        d_second = norm_pull(upward, hat, inv_v[:, 0:1], gains[1:2, :])
        d_low = d_second.astype(LOW)
        df_v[...] = d_low
        vec_v[2:3, :] = col_sum(d_low.astype(F32))
        vec_v[7:8, :] = jnp.zeros((1, width), F32)
        moves.store(df_v, df_any)
        da_v[...] = d_second
        for copy in got[3:]:
            copy.wait()
        if with_sums:
            df_send = df_v[:, pl.ds(pl.multiple_of((1 - core_at) * half, 128), half)]
            df_keep = df_v[:, pl.ds(pl.multiple_of(core_at * half, 128), half)]
        for step in range(steps):
            at = lax.rem(step + (1 - core_at) * (steps // 2), steps)
            cols = pl.ds(pl.multiple_of(at * tile, tile), tile)
            w_rows = w_down[cols, :]
            d_hidden = (mm_nt(df_v[...], w_rows) * slope_v[:, cols].astype(F32)).astype(LOW)
            dh_v[:, cols] = d_hidden
            vec_v[pl.ds(3 + at, 1), :] = col_sum(d_hidden.astype(F32))
            da_v[...] += mm_nt(d_hidden, w_up[:, cols])
            if with_sums:
                product = mm_tn(low_v[...], d_hidden)
                target = up_send if step < steps // 2 else up_keep
                place_rows(
                    target,
                    product,
                    info,
                    PLACES + BLOCKS,
                    width // BLOCKS,
                    ((step % (steps // 2)) * tile, tile),
                )
                if step == steps // 2 - 1:
                    moves.store(up_send, outs[6])
                left = act_v[:, cols]
                piece = wide // BLOCKS
                per = tile // piece
                place_rows(down_send, mm_tn(left, df_send), info, PLACES + at * per, piece)
                place_rows(down_keep, mm_tn(left, df_keep), info, PLACES + at * per, piece)
        if with_sums:
            moves.store(down_send, outs[4])
            moves.store(down_keep, outs[5])
            moves.store(up_keep, outs[7])
        moves.store(da_v, da_any)
        moves.store(dh_v, dh_any)
        moves.store(vec_v, vec_any)
        moves.drain()

    outs = [
        ((count, width), F32),
        ((count, width), LOW),
        ((count, wide), LOW),
        ((8, width), F32),
    ]
    if with_sums:
        outs += [((wide, half), LOW)] * 2 + [((width, wide // 2), LOW)] * 2
    scratch = [
        ((width, wide), LOW),
        ((wide, width), LOW),
        ((count, width), upstream.dtype),
        ((count, wide), LOW),
        ((count, wide), LOW),
        ((count, width), LOW),
        ((count, width), F32),
        ((count, 128), F32),
    ]
    inputs = [(SCALARS, tower.info), (ANYWHERE, upstream)]
    if seeded:
        inputs.append((INSIDE, first_rows))
    inputs += [(ANYWHERE, array) for array in tower.given((2, 3))]
    inputs += [(ANYWHERE, array) for array in (act, slope, low, hat2, inverse)]
    inputs += [(INSIDE, array) for array in tower.given_small()]
    return call_kernel(
        kernel,
        "backward_wide",
        inputs,
        outs,
        scratch + outs,
        8 + len(outs),
        2 * max(count, 256) * width * wide * (4 if with_sums else 2),
        list(after),
    )


def backward_attention(tower, layer, rows, whole_rows, d_first, kept, with_sums, low_out, after=()):
    qkv, mixed, hat1, inverse = kept
    count, width, group = tower.count, tower.width, tower.group
    half = width // 2
    out_type = LOW if low_out else F32

    def kernel(ins, outs, scratch, moves):
        ins = list(ins)
        info, da_any = ins.pop(0), ins.pop(0)
        own_w = [ins.pop(0) for _ in range(2)]
        other_w = [ins.pop(0) for _ in range(2)] if tower.shared else [None] * 2
        x_any, qkv_any, mix_any, hat_any, inv_any = (ins.pop(0) for _ in range(5))
        smalls = ins
        dx_any, dz_any, dp_any, vec_any = outs[:4]
        w_qkv, w_out, da_v, x_v, qkv_v, mix_v, hat_v, inv_v, dmix_v, du_v = scratch[:10]
        dx_v, dz_v, dp_v, vec_v = scratch[10:14]
        use_own = tower.use_own(info, layer)
        core_at = info[CORE]
        if whole_rows:
            x_any = x_any.at[pl.ds(tower.row_start(info), count)]
        got = [
            moves.fetch(da_any, da_v),
            moves.fetch(hat_any, hat_v),
            moves.fetch(inv_any.at[0], inv_v),
            moves.fetch_either(use_own, own_w[1].at[0, tower.index], other_w[1], w_out),
            moves.fetch(qkv_any, qkv_v),
            moves.fetch(mix_any, mix_v),
            moves.fetch(x_any, x_v),
            moves.fetch_either(use_own, own_w[0].at[0, tower.index], other_w[0], w_qkv),
        ]
        gains, _ = tower.small_rows(smalls, use_own)
        for copy in got[:3]:
            copy.wait()
        upward = da_v[...]
        hat = hat_v[...]
        vec_v[0:1, :] = col_sum(upward * hat)
        vec_v[1:2, :] = col_sum(upward)
        d_summed = norm_pull(upward, hat, inv_v[:, 0:1], gains[0:1, :])
        du_v[...] = d_summed
        d_low = d_summed.astype(LOW)
        dz_v[...] = d_low
        vec_v[2:3, :] = col_sum(d_low.astype(F32))
        vec_v[5:8, :] = jnp.zeros((3, width), F32)
        moves.store(dz_v, dz_any)
        got[3].wait()
        dmix_v[...] = mm_nt(d_low, w_out[...]).astype(LOW)
        got[4].wait()

        def one_group(g, carry):
            at = pl.ds(pl.multiple_of(g * group, group), group)
            valid = valid_keys(
                info, tower.lengths_at(info) + g * (group // tower.slots), group, tower.slots
            )
            low, high = pair_masks(LOW)
            scale = HEAD_DIM ** (-0.5)
            for pair in range(width // 128):
                lane = pair * 128
                q2 = qkv_v[at, lane : lane + 128]
                k2 = qkv_v[at, width + lane : width + lane + 128]
                v2 = qkv_v[at, 2 * width + lane : 2 * width + lane + 128]
                query_stack = stacked_pair(q2, low, high)
                soft = pair_softmax(query_stack, k2, valid)
                d_stack = stacked_pair(dmix_v[at, lane : lane + 128], low, high)
                d_soft = mm_nt(d_stack, v2)
                total = jnp.sum(d_soft * soft, axis=-1, keepdims=True)
                d_scores = (soft * (d_soft - total)).astype(LOW)
                dp_v[at, lane : lane + 128] = (
                    joined_pair(mm(d_scores, k2), group) * scale
                ).astype(LOW)
                dp_v[at, width + lane : width + lane + 128] = (
                    mm_tn(d_scores, query_stack) * scale
                ).astype(LOW)
                dp_v[at, 2 * width + lane : 2 * width + lane + 128] = mm_tn(
                    soft.astype(LOW), d_stack
                ).astype(LOW)
            return carry

        lax.fori_loop(0, count // group, one_group, 0)
        vec_v[3:4, :] = col_sum(dp_v[:, :width].astype(F32))
        vec_v[4:5, :] = col_sum(dp_v[:, 2 * width :].astype(F32))
        moves.store(dp_v, dp_any)
        for copy in got[5:]:
            copy.wait()
        if with_sums:
            send, keep = scratch[14:]
            wide_half = 3 * half
            piece = width // BLOCKS
            first = PLACES + 2 * BLOCKS
            for target, side, to in ((send, 1 - core_at, outs[4]), (keep, core_at, outs[5])):
                for third in range(3):
                    cols = pl.ds(pl.multiple_of(side * wide_half + third * half, 128), half)
                    product = mm_tn(x_v[...], dp_v[:, cols])
                    place_rows(target, product, info, first, piece, (third * half, half))
                cols = pl.ds(pl.multiple_of(side * half, 128), half)
                product = mm_tn(mix_v[...], dz_v[:, cols])
                place_rows(target, product, info, first, piece, (wide_half, half))
                moves.store(target, to)
        d_input = du_v[...]
        for part in range(3):
            cols = slice(part * width, (part + 1) * width)
            d_input = d_input + mm_nt(dp_v[:, cols], w_qkv[:, cols])
        dx_v[...] = d_input.astype(out_type)
        moves.store(dx_v, dx_any)
        moves.store(vec_v, vec_any)
        moves.drain()

    outs = [
        ((count, width), out_type),
        ((count, width), LOW),
        ((count, 3 * width), LOW),
        ((8, width), F32),
    ]
    if with_sums:
        outs += [((width, 4 * half), LOW)] * 2
    scratch = [
        ((width, 3 * width), LOW),
        ((width, width), LOW),
        ((count, width), F32),
        ((count, width), LOW),
        ((count, 3 * width), LOW),
        ((count, width), LOW),
        ((count, width), F32),
        ((count, 128), F32),
        ((count, width), LOW),
        ((count, width), F32),
    ]
    inputs = [(SCALARS, tower.info), (ANYWHERE, d_first)]
    inputs += [(ANYWHERE, array) for array in tower.given((0, 1))]
    inputs += [(ANYWHERE, array) for array in (rows, qkv, mixed, hat1, inverse)]
    inputs += [(INSIDE, array) for array in tower.given_small()]
    return call_kernel(
        kernel,
        "backward_attention",
        inputs,
        outs,
        scratch + outs,
        8 + len(outs),
        2 * max(count, 256) * 4 * width * width * (2 if with_sums else 1),
        list(after),
    )


def block_chooser(rows, columns, valid, size, bit):
    at = lax.broadcasted_iota(jnp.int32, (1, columns), 1)
    piece = jnp.floor((at.astype(F32) + 0.5) * (1.0 / size)).astype(jnp.int32)
    wanted = jnp.where(at < valid, at + (piece + bit) * size, -1)
    row_at = lax.broadcasted_iota(jnp.int32, (rows, columns), 0)
    return jnp.where(row_at == wanted, 1.0, 0.0).astype(LOW)


def pack_first(info, early, late, width, after=()):
    count = early[0].shape[0]
    wide = early[3].shape[1]
    half = width // 2
    lefts = 3 * half + wide // 2
    rights = sum(array.shape[1] for array in early[4:])

    def kernel(ins, outs, scratch, moves):
        info_ref = ins[0]
        first, second = ins[1:9], ins[9:17]
        held, keep, send = scratch[:8], scratch[8], scratch[9]
        flag = info_ref[IS_FIRST] == 1
        got = [moves.fetch_either(flag, a, b, to) for a, b, to in zip(first, second, held)]
        mine = info_ref[X_BIT]
        choose = []
        for size in (width // BLOCKS, wide // BLOCKS):
            choose.append(
                [block_chooser(width, half, half, size, bit) for bit in (mine, 1 - mine)]
            )
        for copy in got:
            copy.wait()
        for target, which in ((keep, 0), (send, 1)):
            for part in range(3):
                target[:, part * half : (part + 1) * half] = mm(
                    held[part][...], choose[0][which]
                ).astype(LOW)
            for part in range(wide // width):
                at = (3 + part) * half
                target[:, at : at + half] = mm(
                    held[3][:, part * width : (part + 1) * width], choose[1][which]
                ).astype(LOW)
        at = lefts
        for part in held[4:]:
            send[:, at : at + part.shape[1]] = part[...]
            at += part.shape[1]
        moves.store(keep, outs[0])
        moves.store(send, outs[1])
        moves.drain()

    outs = [((count, lefts), LOW), ((count, lefts + rights), LOW)]
    inputs = [(SCALARS, info)] + [(ANYWHERE, array) for array in tuple(early) + tuple(late)]
    scratch = [(array.shape, LOW) for array in early]
    return call_kernel(
        kernel, "pack_first", inputs, outs, scratch + outs, 10, 1 << 28, list(after)
    )


def pack_second(info, keep, send, arrived, width, after=()):
    count, lefts = keep.shape
    rights = send.shape[1] - lefts
    half, quarter = width // 2, width // 4
    third = 256
    groups = lefts // half - 3
    packed = 3 * third + groups * quarter

    def kernel(ins, outs, scratch, moves):
        info_ref, keep_any, send_any, arrived_any = ins
        keep_v, send_v, arrived_v, keep2, send2 = scratch
        got = [
            moves.fetch(keep_any, keep_v),
            moves.fetch(send_any, send_v),
            moves.fetch(arrived_any, arrived_v),
        ]
        mine = info_ref[Y_BIT]
        narrow = [
            block_chooser(half, third, quarter, width // BLOCKS, bit) for bit in (mine, 1 - mine)
        ]
        broad = [
            block_chooser(2 * half, 2 * quarter, 2 * quarter, quarter, bit)
            for bit in (mine, 1 - mine)
        ]
        for copy in got:
            copy.wait()
        for target, which in ((keep2, 0), (send2, 1)):
            for source, row in ((keep_v, 0), (arrived_v, count)):
                rows = slice(row, row + count)
                for part in range(3):
                    target[rows, part * third : (part + 1) * third] = mm(
                        source[:, part * half : (part + 1) * half], narrow[which]
                    ).astype(LOW)
                for part in range(groups // 2):
                    at = 3 * third + 2 * part * quarter
                    begin = (3 + 2 * part) * half
                    target[rows, at : at + 2 * quarter] = mm(
                        source[:, begin : begin + 2 * half], broad[which]
                    ).astype(LOW)
        send2[:count, packed:] = send_v[:, lefts:]
        send2[count:, packed:] = arrived_v[:, lefts:]
        moves.store(keep2, outs[0])
        moves.store(send2, outs[1])
        moves.drain()

    outs = [((2 * count, packed), LOW), ((2 * count, packed + rights), LOW)]
    inputs = [(SCALARS, info)] + [(ANYWHERE, array) for array in (keep, send, arrived)]
    scratch = [(array.shape, LOW) for array in (keep, send, arrived)]
    return call_kernel(
        kernel, "pack_second", inputs, outs, scratch + outs, 5, 1 << 28, list(after)
    )


def query_products(info, keep, send, arrived, width, wide, after=()):
    count, packed = keep.shape
    third = 256
    piece = width // BLOCKS
    columns = 3 * width + width + wide + (wide // width) * width

    def kernel(ins, outs, scratch, moves):
        info_ref, keep_any, send_any, arrived_any = ins
        left_v, right_v, result = scratch
        total = right_v.shape[1]
        got = [
            moves.fetch(keep_any, left_v.at[:count]),
            moves.fetch(arrived_any.at[:, :packed], left_v.at[pl.ds(count, count)]),
            moves.fetch(send_any.at[:, packed:], right_v.at[:count]),
            moves.fetch(arrived_any.at[:, packed:], right_v.at[pl.ds(count, count)]),
        ]
        for copy in got:
            copy.wait()
        at = 0
        for part, cols in enumerate((3 * width, width, wide)):
            left = left_v[:, part * third : (part + 1) * third]
            for begin in range(0, cols, width):
                product = mm_tn(left, right_v[:, at + begin : at + begin + width])
                for z in range(4):
                    row = pl.multiple_of(info_ref[Z_PLACES + z] * piece, piece)
                    result[pl.ds(row, piece), at + begin : at + begin + width] = product[
                        z * piece : (z + 1) * piece
                    ].astype(LOW)
            at += cols
        product = mm_tn(left_v[:, 3 * third :], right_v[:, at:])
        per = wide // width
        for z in range(4):
            row = pl.multiple_of(info_ref[Z_PLACES + z] * piece, piece)
            for part in range(per):
                begin = (z * per + part) * piece
                result[pl.ds(row, piece), at + part * width : at + (part + 1) * width] = product[
                    begin : begin + piece
                ].astype(LOW)
        moves.store(result.at[pl.ds(2 * piece, 2 * piece)], outs[0])
        moves.store(result.at[pl.ds(0, 2 * piece)], outs[1])
        moves.drain()

    outs = [((2 * piece, columns), LOW)] * 2
    inputs = [(SCALARS, info)] + [(ANYWHERE, array) for array in (keep, send, arrived)]
    scratch = [
        ((2 * count, packed), LOW),
        ((2 * count, send.shape[1] - packed), LOW),
        ((4 * piece, columns), LOW),
    ]
    return call_kernel(
        kernel, "query_products", inputs, outs, scratch, 6, 1 << 30, list(after)
    )


def pick_bit(grid, axis, index):
    return lax.dynamic_index_in_dim(grid, index, axis, keepdims=False)


def own_bit(bit):
    return (lax.axis_index("batch") // bit) % 2


def scatter_sum(grid, bits, left):
    left = list(left)
    for bit in bits:
        axis = left.index(bit)
        mine = own_bit(bit)
        sent = pick_bit(grid, axis, 1 - mine)
        kept = pick_bit(grid, axis, mine)
        arrived = flip_swap(sent, bit)
        total = kept.astype(jnp.float32) + arrived.astype(jnp.float32)
        left.remove(bit)
        grid = total if not left else total.astype(grid.dtype)
    return grid


def all_bits(size):
    bits = [1 << i for i in range(size.bit_length() - 1)]
    return bits[::-1]


def to_grid(array, size):
    bits = all_bits(size)
    return array.reshape((2,) * len(bits) + (array.shape[0] // size,) + array.shape[1:])


def gather_all(block, size):
    if size != 16:
        for bit in all_bits(size)[::-1]:
            block = jnp.concatenate([block, flip_swap(block, bit)], 0)
        return block
    block = jnp.concatenate([block] + [flip_swap(block, k) for k in (1, 2, 3)], 0)
    return jnp.concatenate([block] + [flip_swap(block, k) for k in (4, 8, 12)], 0)


def contrast(own_cls, micro, positive, query_count, batch_index, batch_size):
    width = own_cls.shape[1]
    chip_rows = own_cls.shape[0]
    gathered = gather_all(own_cls, batch_size).reshape(batch_size, chip_rows, width)
    all_q = gathered[:, :query_count].reshape(-1, width)
    all_p = gathered[:, query_count:].reshape(-1, width)
    blocks = jnp.arange(batch_size, dtype=jnp.int32) ^ batch_index
    query_ids = (
        blocks[:, None] * query_count + jnp.arange(query_count, dtype=jnp.int32)[None, :]
    ).reshape(-1)
    passage_ids = (
        3 * query_ids[:, None] + jnp.arange(3, dtype=jnp.int32)[None, :]
    ).reshape(-1)
    labels = jnp.take(micro, query_ids)
    wanted = jnp.take(positive, query_ids)
    logit_scale = LOGIT_GAIN * width ** (-0.5)
    logits = mm_nt(all_q, all_p) * logit_scale
    same_group = labels[:, None] == jnp.repeat(labels, 3)[None, :]
    logits = jnp.where(same_group, logits, MASK_FILL)
    row_top = jnp.max(logits, axis=-1, keepdims=True)
    exponent = jnp.exp(logits - row_top)
    totals = jnp.sum(exponent, axis=-1, keepdims=True)
    target = passage_ids[None, :] == wanted[:, None]
    loss_all = (
        row_top[:, 0] + jnp.log(totals[:, 0]) - jnp.sum(jnp.where(target, logits, 0.0), axis=-1)
    )
    coefficient = (exponent / totals - target.astype(jnp.float32)) * logit_scale
    passage_count = 3 * query_count
    d_cls_q = jnp.dot(coefficient[:query_count], all_p.astype(jnp.float32), precision=PRECISE)
    d_cls_p = lax.dot_general(
        coefficient[:, :passage_count],
        all_q.astype(jnp.float32),
        (((0,), (0,)), ((), ())),
        precision=PRECISE,
    )
    return loss_all[:query_count], d_cls_q, d_cls_p


def integers(core, index, size, len_q, len_p):
    blocks = jnp.arange(BLOCKS, dtype=jnp.int32)
    own = index // (size // BLOCKS)
    relative = blocks ^ own
    places = [
        sum(((relative // bit) % 2) * (8 >> at) for at, bit in enumerate(order))
        for order in ORDERS
    ]
    depth = jnp.arange(4, dtype=jnp.int32) ^ (own // 4)
    z_places = (depth % 2) * 2 + depth // 2
    few = jnp.stack([1 - core, core])
    ends = jnp.stack([own % 2, (own // 2) % 2])
    return jnp.concatenate([few, *places, z_places, ends, len_q, len_p]).astype(jnp.int32)


def two_halves(first, second):
    cut = first.shape[0] // 2

    def added(low, high):
        return (first[low:high].astype(F32) + second[low:high].astype(F32)).astype(LOW)

    return added(cut, 2 * cut), added(0, cut)


class Chain:
    def __init__(self, send, keep, order, size, over_core=True):
        self.order = list(order)
        self.size = size
        self.scale = size // BLOCKS
        self.keep = keep
        self.sent = send
        if over_core:
            self.arrived = core_swap(send)
        else:
            self.arrived = self.swap(send)

    def swap(self, block):
        return flip_swap(block, self.order.pop(0) * self.scale)

    def step(self):
        self.sent, self.keep = two_halves(self.keep, self.arrived)
        self.arrived = self.swap(self.sent)
        return self.sent

    def result(self):
        while self.order:
            self.step()
        total = self.keep.astype(F32) + self.arrived.astype(F32)
        return total

    def rest(self, total):
        if self.scale == 1:
            return total
        left = all_bits(self.scale)
        return scatter_sum(to_grid(total.astype(LOW), self.scale), left, left)


def shards(
    x_q,
    x_p,
    len_q,
    len_p,
    cot_q,
    cot_p,
    positive,
    micro,
    w_qkv,
    w_out,
    w_up,
    w_down,
    norm_gain,
    biases,
    b_up,
):
    core = lax.axis_index("section")
    is_first = core == 0
    batch_index = lax.axis_index("batch")
    size = lax.axis_size("batch")
    bits = all_bits(size)
    query_count, slots_q, model = x_q.shape
    half_count = x_p.shape[0] // 2
    slots_p = x_p.shape[1]
    wide = w_up.shape[-1]
    info = integers(core, batch_index, size, len_q, len_p)
    weights = (w_qkv, w_out, w_up, w_down)
    smalls = (norm_gain, biases, b_up)
    other_p = tuple(core_swap(member[0, 1]) for member in weights)
    small_other = core_swap(
        jnp.concatenate([norm_gain[0, 1], biases[0, 1], b_up[0, 1].reshape(-1, model)], 0)
    )
    tower_q = Tower(0, info, weights, None, smalls, None, query_count, slots_q, LENGTHS)
    tower_p = Tower(
        1, info, weights, other_p, smalls, small_other, half_count, slots_p, LENGTHS + query_count
    )
    flat_q = x_q.reshape(-1, model)
    flat_p = x_p.reshape(-1, model)
    cots_q = cot_q.reshape(-1, model)
    cots_p = cot_p.reshape(-1, model)

    early_q = forward_layer(tower_q, 0, flat_q, True)
    mid_q = early_q[0]
    arrived_q = core_swap(mid_q)
    late_q = forward_layer(tower_q, 1, arrived_q, True)
    early_p = forward_layer(tower_p, 0, flat_p, True, (late_q[0],))
    mid_p = early_p[0]
    late_p = forward_layer(tower_p, 1, mid_p, False)
    top_q, top_p = late_q[0], late_p[0]

    cls_rows = jnp.concatenate([top_q[::slots_q], top_p[::slots_p]], 0)
    cls_other = core_swap(cls_rows)
    cls_chip = jnp.concatenate(
        [
            jnp.where(is_first, cls_other[:query_count], cls_rows[:query_count]),
            jnp.where(is_first, cls_rows[query_count:], cls_other[query_count:]),
            jnp.where(is_first, cls_other[query_count:], cls_rows[query_count:]),
        ],
        0,
    )
    loss_own, d_cls_q, d_cls_p = contrast(
        cls_chip, micro, positive, query_count, batch_index, size
    )
    d_own_p = lax.dynamic_slice_in_dim(d_cls_p, core * half_count, half_count, 0)

    def wide_kept(kept):
        return kept[4], kept[5], kept[3], kept[7], kept[8]

    def narrow_kept(kept):
        return kept[1], kept[2], kept[6], kept[8]

    def factors(rows, kept, wide_back, narrow_back):
        return (
            rows,
            kept[2],
            kept[3],
            kept[4],
            narrow_back[2],
            narrow_back[1],
            wide_back[2],
            wide_back[1],
        )

    late_wide_p = backward_wide(tower_p, 1, cots_p, d_own_p, wide_kept(late_p), True)
    down1 = Chain(late_wide_p[4], late_wide_p[5], ORDERS[0], size)
    up1 = Chain(late_wide_p[6], late_wide_p[7], ORDERS[1], size)

    late_wide_q = backward_wide(
        tower_q, 1, cots_q, d_cls_q, wide_kept(late_q), False, (late_wide_p[0],)
    )
    after = (down1.step(), up1.step())
    late_back_q = backward_attention(
        tower_q, 1, arrived_q, True, late_wide_q[0], narrow_kept(late_q), False, True, after
    )
    late_sent_q = late_back_q[0]
    grad_mid_q = core_swap(late_sent_q)
    late_back_p = backward_attention(
        tower_p, 1, mid_p, False, late_wide_p[0], narrow_kept(late_p), True, True, (late_sent_q,)
    )
    late_sent_p = late_back_p[0]
    rest1 = Chain(late_back_p[4], late_back_p[5], ORDERS[2], size)
    after = (down1.step(), up1.step(), late_sent_p)
    early_wide_q = backward_wide(
        tower_q, 0, grad_mid_q, None, wide_kept(early_q), False, after
    )
    after = (rest1.step(),)
    early_back_q = backward_attention(
        tower_q, 0, flat_q, True, early_wide_q[0], narrow_kept(early_q), False, False, after
    )
    keep, send = pack_first(
        info,
        factors(flat_q, early_q, early_wide_q, early_back_q),
        factors(arrived_q, late_q, late_wide_q, late_back_q),
        model,
    )
    gather_bits = [bit * (size // BLOCKS) for bit in (1, 2)]
    arrived = flip_swap(send, gather_bits[0])
    after = (down1.step(), up1.step(), send)
    early_wide_p = backward_wide(
        tower_p, 0, late_sent_p, None, wide_kept(early_p), True, after
    )
    down0 = Chain(early_wide_p[4], early_wide_p[5], ORDERS[0], size)
    up0 = Chain(early_wide_p[6], early_wide_p[7], ORDERS[1], size)
    after = (rest1.step(), down1.step(), up1.step())
    keep, send = pack_second(info, keep, send, arrived, model)
    arrived = flip_swap(send, gather_bits[1])
    early_back_p = backward_attention(
        tower_p,
        0,
        flat_p,
        True,
        early_wide_p[0],
        narrow_kept(early_p),
        True,
        False,
        after + (send,),
    )
    early_grad_p = early_back_p[0]
    rest0 = Chain(early_back_p[4], early_back_p[5], ORDERS[2], size)
    send, keep = query_products(info, keep, send, arrived, model, wide)
    query = Chain(send, keep, (4, 8), size, False)

    late_sums = [chain.rest(chain.result()) for chain in (down1, up1, rest1)]
    early_sums = [chain.rest(chain.result()) for chain in (down0, up0, rest0)]
    total_q = query.result()
    at = 4 * model + wide
    down_q = jnp.concatenate(
        [total_q[:, at + part * model : at + (part + 1) * model] for part in range(wide // model)],
        0,
    )
    down_q = query.rest(down_q)
    narrow_q = query.rest(total_q[:, :at])
    qkv_q = narrow_q[:, : 3 * model]
    out_q = narrow_q[:, 3 * model : 4 * model]
    up_q = narrow_q[:, 4 * model :]

    early_vec_p = jnp.concatenate([early_wide_p[3], early_back_p[3]], 0)
    late_vec_p = jnp.concatenate([late_wide_p[3], late_back_p[3]], 0)
    vec_p = jnp.where(is_first, early_vec_p, late_vec_p) + core_swap(
        jnp.where(is_first, late_vec_p, early_vec_p)
    )
    vec_q = jnp.where(
        is_first,
        jnp.concatenate([early_wide_q[3], early_back_q[3]], 0),
        jnp.concatenate([late_wide_q[3], late_back_q[3]], 0),
    )
    vecs = jnp.stack([vec_q, vec_p])
    narrow = jnp.concatenate([vecs[:, 0:3], vecs[:, 8:13]], 1)
    narrow = jnp.moveaxis(narrow.reshape(2, 8, size, -1), 2, 0)
    blk = narrow.shape[-1]
    wide_v = jnp.moveaxis(vecs[:, 3:7].reshape(2, size, 1, -1), 1, 0)
    lines = jnp.concatenate(
        [narrow.reshape(size, 2, 8 * blk), wide_v.reshape(size, 2, -1)], 2
    ).reshape(size, -1)
    lines = scatter_sum(to_grid(lines, size), bits[::-1], bits)[0].reshape(2, -1)
    eight = lines[:, : 8 * blk].reshape(2, 8, blk)
    g_gain = jnp.stack([eight[:, 3], eight[:, 0]], 1)
    g_bias = jnp.stack([eight[:, at] for at in (6, 7, 5, 4, 2, 1)], 1)
    g_bup = lines[:, 8 * blk :]

    def own_layer(early, late):
        other = core_swap(jnp.where(is_first, late, early))
        own = jnp.where(is_first, early, late)
        return jnp.where(is_first, own, other), jnp.where(is_first, other, own)

    def join(early, late, axis):
        return jnp.concatenate(own_layer(early, late), axis)

    down_p = join(early_sums[0], late_sums[0], 1)
    up_p = join(early_sums[1], late_sums[1], 1)
    first, second = own_layer(early_sums[2], late_sums[2])
    cut = 3 * model // 2
    qkv_p = jnp.concatenate([first[:, :cut], second[:, :cut]], 1)
    out_p = jnp.concatenate([first[:, cut:], second[:, cut:]], 1)
    hidden_p = join(mid_p, top_p, 0).reshape(x_p.shape)
    grad_p = join(early_grad_p, late_sent_p.astype(F32), 0).reshape(x_p.shape)
    hidden_q = jnp.where(is_first, mid_q, top_q).reshape(x_q.shape)
    grad_q = jnp.where(is_first, early_back_q[0], late_sent_q.astype(F32)).reshape(x_q.shape)
    return (
        hidden_q[None],
        hidden_p[None],
        grad_q[None],
        grad_p[None],
        loss_own,
        jnp.stack([qkv_q, qkv_p])[None],
        jnp.stack([out_q, out_p])[None],
        jnp.stack([up_q, up_p])[None],
        jnp.stack([down_q, down_p])[None],
        g_gain[None],
        g_bias[None],
        g_bup[None],
        g_bias[None, :, 0, :],
    )


def solution(mesh):
    return jax.shard_map(
        shards,
        mesh=mesh,
        in_specs=(
            P("batch", None, None),
            P("batch", None, None),
            P("batch"),
            P("batch"),
            P("batch", None, None),
            P("batch", None, None),
            P(),
            P(),
            P("section", None, None, None),
            P("section", None, None, None),
            P("section", None, None, None),
            P("section", None, None, None),
            P("section", None, None, None),
            P("section", None, None, None),
            P("section", None, None),
        ),
        out_specs=(
            P("section", "batch", None, None),
            P("section", "batch", None, None),
            P("section", "batch", None, None),
            P("section", "batch", None, None),
            P("batch"),
            P("section", None, "batch", None),
            P("section", None, "batch", None),
            P("section", None, "batch", None),
            P("section", None, "batch", None),
            P("section", None, None, "batch"),
            P("section", None, None, "batch"),
            P("section", None, "batch"),
            P("section", None, "batch"),
        ),
        check_vma=False,
    )
```

time: 738 us -> 540 us (0.73)
  matrix products: 195 us -> 1.25 us
  Pallas kernels: 0 us -> 181 us
  local copies, waits for them, and re-layouts: 187 us -> 27.1 us
  other arithmetic: 82.6 us -> 44.2 us
  waiting for transfers between devices: 204 us -> 221 us
    dot_general x65 -> x1, matrix products: 183 us -> 0.28 us  [mm_nt(): lax.dot_general(left, right, (((1,), (1,)), ((), ())), preferred_element_...]
    pallas_call x0 -> x15, Pallas kernels: none -> 181 us  [call_kernel(): pl.pallas_call(body, out_shape=[jax.ShapeDtypeStruct(shape, kind) for sha...]
    reshape x45 -> x5, local copies, waits for them, and re-layouts: 45.8 us -> 0.41 us  [the longest x2 0.15 us: shards(): narrow = jnp.moveaxis(narrow.reshape(2, 8, size, -1), 2, 0)]
    dynamic_slice x30 -> x1, local copies, waits for them, and re-layouts: 31.6 us -> 0.61 us  [shards(): lax.dynamic_slice_in_dim(d_cls_p, core * half_count, half_count, 0)]
    reduce_sum x21 -> x0, other arithmetic: 17.8 us -> none  [the longest x4 5.79 us: block_backward(): d_bias_ffn = jnp.sum(d_branch_ffn.astype(jnp.float32), axis=0)]
    ppermute x40 -> x38, waiting for transfers between devices: 203 us -> 219 us  [flip_swap(): return lax.ppermute(block, 'batch', [(i, i ^ bit) for i in range(size)])]
    unnamed x626 -> x133, local copies, waits for them, and re-layouts: 24.5 us -> 8.91 us
    concatenate x16 -> x4, local copies, waits for them, and re-layouts: 14.7 us -> 1.39 us  [the longest x1 0.74 us: shards(): early_vec_p = jnp.concatenate([early_wide_p[3], early_back_p[3]], 0)]
  transfers between devices with their start and end apart: 62 -> 58, of which waited for: 26 -> 25; matrix products, arithmetic and copies ran while one was open for 51% -> 10% of each run, Pallas kernels for 0% -> 24%
where the time goes in v2:
time: 540 us; the launch traced here: 533 us
  waiting for transfers between devices  221 us (41%)
  Pallas kernels  181 us (34%)
  starting transfers between devices  55.7 us (10%)
  other arithmetic  44.2 us (8%)
  local copies, waits for them, and re-layouts  27.1 us (5%)
    ppermute x38, waiting for transfers between devices, flip_swap(): return lax.ppermute(block, 'batch', [(i, i ^ bit) for i in range(size)])  219 us
    pallas_call x15, Pallas kernels, call_kernel(): pl.pallas_call(body, out_shape=[jax.ShapeDtypeStruct(shape, kind) for sha...  181 us
    ppermute x38, starting transfers between devices, flip_swap(): return lax.ppermute(block, 'batch', [(i, i ^ bit) for i in range(size)])  51.4 us
    convert_element_type x25, other arithmetic, added(): (first[low:high].astype(F32) + second[low:high].astype(F32)).astype(LOW)  29.7 us
  transfers between devices with their start and end apart: 58, of which 25 were waited for; matrix products, arithmetic and copies ran while one was open for 10% of the time, Pallas kernels for 24%

profile of v2, /device:TPU:0, one launch (start us, length us, event | category | flops | bytes accessed | tf_op | source)
XLA Modules:
  0.0 532.5 jit_solution(9618717898313599074)
XLA Ops:
  0.7 5.2 slice_bitcast_fusion.1
  7.5 2.7 slice_bitcast_fusion
  10.6 1.5 copy-done.4
  12.2 2.1 slice_bitcast_fusion.2
  16.1 9.4 %layer_forward.4 = (bf16[64,768]{1,0:T(8,128)(2,1)}, bf16[64,2304]{1,0:T(8,128)(2,1)}, bf16[64,768]{1,0:T(8,128)(2,1)}, bf16[64,768]{1,0:T(8,128)(2,1)}, bf16[64...) custom-call(s32[64]{0:T(128)} %concatenate.81.refs_0_, ...), custom_call_target="tpu_custom_call" | custom-call | flops 3623878656 | bytes 56623104 | tf_op jit(solution)/shard_map/layer_forward/pallas_call | solution.py:177
  27.8 9.3 %layer_forward.5 = (bf16[64,768]{1,0:T(8,128)(2,1)}, bf16[64,2304]{1,0:T(8,128)(2,1)}, bf16[64,768]{1,0:T(8,128)(2,1)}, bf16[64,768]{1,0:T(8,128)(2,1)}, bf16[64...) custom-call(s32[64]{0:T(128)} %concatenate.81.refs_0_, ...), custom_call_target="tpu_custom_call" | custom-call | flops 3623878656 | bytes 56623104 | tf_op jit(solution)/shard_map/layer_forward/pallas_call | solution.py:177
  39.0 16.1 %layer_forward.6 = (bf16[384,768]{1,0:T(8,128)(2,1)}, bf16[384,2304]{1,0:T(8,128)(2,1)}, bf16[384,768]{1,0:T(8,128)(2,1)}, bf16[384,768]{1,0:T(8,128)(2,1)}, bf1...) custom-call(s32[64]{0:T(128)} %concatenate.81.refs_0_, ...), custom_call_target="tpu_custom_call" | custom-call | flops 5435817984 | bytes 84934656 | tf_op jit(solution)/shard_map/layer_forward/pallas_call | solution.py:177
  55.1 16.3 %layer_forward.7 = (bf16[384,768]{1,0:T(8,128)(2,1)}, bf16[384,2304]{1,0:T(8,128)(2,1)}, bf16[384,768]{1,0:T(8,128)(2,1)}, bf16[384,768]{1,0:T(8,128)(2,1)}, bf1...) custom-call(s32[64]{0:T(128)} %concatenate.81.refs_0_, ...), custom_call_target="tpu_custom_call" | custom-call | flops 5435817984 | bytes 84934656 | tf_op jit(solution)/shard_map/layer_forward/pallas_call | solution.py:177
  74.2 3.9 collective-permute-start.10
  79.8 2.0 collective-permute-done.8
  82.3 1.6 collective-permute-start.11
  84.0 2.6 collective-permute-start.12
  87.2 2.9 collective-permute-done.12
  90.0 2.4 collective-permute-done.13
  94.1 20.6 %backward_wide.4 = (f32[384,768]{1,0:T(8,128)}, bf16[384,768]{1,0:T(8,128)(2,1)}, bf16[384,3072]{1,0:T(8,128)(2,1)}, f32[8,768]{1,0:T(8,128)}, bf16[3072,384]{1,...) custom-call(s32[64]{0:T(128)} %concatenate.81.refs_0_, ...), custom_call_target="tpu_custom_call" | custom-call | flops 7247757312 | bytes 113246208 | tf_op jit(solution)/shard_map/backward_wide/pallas_call | solution.py:177
  116.7 8.9 %backward_wide.5 = (f32[64,768]{1,0:T(8,128)}, bf16[64,768]{1,0:T(8,128)(2,1)}, bf16[64,3072]{1,0:T(8,128)(2,1)}, f32[8,768]{1,0:T(8,128)}) custom-call(s32[64]{0:T(128)} %concatenate.81.refs_0_, bf16[64,768]{1,0:T(8,128)(2,1)} %bitcast.111, f32[2,768]{1,0:T(2,128)} %fusion.18.refs_2_, bf16[1,2,768,3072]{3,2,1,0:T(8,128)(2,1)} %refs_2_.18, ...), custom_call_target="tpu_custom_call" | custom-call | flops 2415919104 | bytes 37748736 | tf_op jit(solution)/shard_map/backward_wide/pallas_call | solution.py:177
  125.6 1.5 copy-done.24
  127.1 2.5 add_convert_fusion.8
  130.2 2.3 add_convert_fusion.9
  132.6 1.5 collective-permute-start.17
  134.1 7.9 %backward_attention.4 = (bf16[64,768]{1,0:T(8,128)(2,1)}, bf16[64,768]{1,0:T(8,128)(2,1)}, bf16[64,2304]{1,0:T(8,128)(2,1)}, f32[8,768]{1,0:T(8,128)}) custom-call(s32[64]{0:T(128)} %concatenate.81.refs_0_, f32[64,768]{1,0:T(8,128)} %get-tuple-element.107.refs_1_, bf16[1,2,768,2304]{3,2,1,0:T(8,128)(2,1)} %refs_2_.19, bf16[1,2,768,768]{3,2,1,0:T(8,128)(2,1)} %refs_3_.23, ...), custom_call_target="tpu_custom_call" | custom-call | flops 1207959552 | bytes 18874368 | tf_op jit(solution)/shard_map/backward_attention/pallas_call | solution.py:177
  142.0 19.6 %backward_attention.5 = (bf16[384,768]{1,0:T(8,128)(2,1)}, bf16[384,768]{1,0:T(8,128)(2,1)}, bf16[384,2304]{1,0:T(8,128)(2,1)}, f32[8,768]{1,0:T(8,128)}, bf16[7...) custom-call(s32[64]{0:T(128)} %concatenate.81.refs_0_, f32[384,768]{1,0:T(8,128)} %get-tuple-element.106.refs_13_.refs_1_, ...), custom_call_target="tpu_custom_call" | custom-call | flops 3623878656 | bytes 56623104 | tf_op jit(solution)/shard_map/backward_attention/pallas_call | solution.py:177
  163.6 1.6 add_convert_fusion.22
  166.3 1.6 add_convert_fusion.23
  167.9 1.6 collective-permute-start.20
  170.2 8.7 %backward_wide.6 = (f32[64,768]{1,0:T(8,128)}, bf16[64,768]{1,0:T(8,128)(2,1)}, bf16[64,3072]{1,0:T(8,128)(2,1)}, f32[8,768]{1,0:T(8,128)}) custom-call(s32[64]{0:T(128)} %concatenate.81.refs_0_, bf16[64,768]{1,0:T(8,128)(2,1)} %copy-done.50, bf16[1,2,768,3072]{3,2,1,0:T(8,128)(2,1)} %refs_2_.18, bf16[1,2,3072,768]{3,2,1,0:T(8,128)(2,1)} %refs_3_.22, ...), custom_call_target="tpu_custom_call" | custom-call | flops 2415919104 | bytes 37748736 | tf_op jit(solution)/shard_map/backward_wide/pallas_call | solution.py:177
  178.9 2.3 collective-permute-done.21
  181.1 1.4 add_convert_fusion.34
  184.9 2.4 add_convert_fusion.6
  188.2 4.3 collective-permute-done.24
  193.3 5.5 %collective-permute-done.23 = bf16[384,384]{1,0:T(8,128)(2,1)S(1)} collective-permute-done((bf16[384,384]{1,0:T(8,128)(2,1)S(1)}, bf16[384,384]{1,0:T(8,128)(2,1)S(1)}, u32[]{:S(2)}, u32[]{:S(2)}) %collective-permute-start.23) | collective-permute-done | bytes 294944 | tf_op jit(solution)/shard_map/ppermute | solution.py:26
  199.6 7.9 %backward_attention.6 = (f32[64,768]{1,0:T(8,128)}, bf16[64,768]{1,0:T(8,128)(2,1)}, bf16[64,2304]{1,0:T(8,128)(2,1)}, f32[8,768]{1,0:T(8,128)}) custom-call(s32[64]{0:T(128)} %concatenate.81.refs_0_, f32[64,768]{1,0:T(8,128)} %get-tuple-element.125.refs_1_, bf16[1,2,768,2304]{3,2,1,0:T(8,128)(2,1)} %refs_2_.19, bf16[1,2,768,768]{3,2,1,0:T(8,128)(2,1)} %refs_3_.23, ...), custom_call_target="tpu_custom_call" | custom-call | flops 1207959552 | bytes 18874368 | tf_op jit(solution)/shard_map/backward_attention/pallas_call | solution.py:177
  207.6 4.7 pack_first.1
  213.3 20.7 %backward_wide.7 = (f32[384,768]{1,0:T(8,128)}, bf16[384,768]{1,0:T(8,128)(2,1)}, bf16[384,3072]{1,0:T(8,128)(2,1)}, f32[8,768]{1,0:T(8,128)}, bf16[3072,384]{1,...) custom-call(s32[64]{0:T(128)} %concatenate.81.refs_0_, ...), custom_call_target="tpu_custom_call" | custom-call | flops 7247757312 | bytes 113246208 | tf_op jit(solution)/shard_map/backward_wide/pallas_call | solution.py:177
  234.8 2.4 add_convert_fusion.18
  237.2 1.8 collective-permute-done.25.refs_3_
  240.1 5.3 %pack_second.1 = (bf16[128,1536]{1,0:T(8,128)(2,1)}, bf16[128,8448]{1,0:T(8,128)(2,1)}) custom-call(s32[64]{0:T(128)} %concatenate.81.refs_0_, bf16[64,2688]{1,0:T(8,128)(2,1)} %get-tuple-element.150.refs_1_, bf16[64,9600]{1,0:T(8,128)(2,1)} %get-tuple-element.145.refs_17_.refs_2_, bf16[64,9600]{1,0:T(8,128)(2,1)} %copy-done.33), custom_call_target="tpu_custom_call" | custom-call | flops 268435456 | bytes 4194304 | tf_op jit(solution)/shard_map/pack_second/pallas_call | solution.py:177
  245.5 19.3 %backward_attention.7 = (f32[384,768]{1,0:T(8,128)}, bf16[384,768]{1,0:T(8,128)(2,1)}, bf16[384,2304]{1,0:T(8,128)(2,1)}, f32[8,768]{1,0:T(8,128)}, bf16[768,153...) custom-call(s32[64]{0:T(128)} %concatenate.81.refs_0_, f32[384,768]{1,0:T(8,128)} %get-tuple-element.146.refs_1_, ...), custom_call_target="tpu_custom_call" | custom-call | flops 3623878656 | bytes 56623104 | tf_op jit(solution)/shard_map/backward_attention/pallas_call | solution.py:177
  269.8 1.7 collective-permute-done.54
  271.6 1.6 collective-permute-start.55
  277.8 1.5 collective-permute-start.27
  281.0 2.8 collective-permute-done.57
  285.3 3.1 add_convert_fusion.1
  289.5 2.4 add_convert_fusion.3
  295.9 61.2 %collective-permute-done.36 = bf16[96,1536]{1,0:T(8,128)(2,1)S(1)} collective-permute-done((bf16[96,1536]{1,0:T(8,128)(2,1)S(1)}, bf16[96,1536]{1,0:T(8,128)(2,1)S(1)}, u32[]{:S(2)}, u32[]{:S(2)}) %collective-permute-start.36) | collective-permute-done | bytes 294944 | tf_op jit(solution)/shard_map/ppermute | solution.py:26
  361.9 1.6 pad_maximum_fusion
  363.5 2.4 collective-permute-start.44
  365.9 6.1 %query_products.1 = (bf16[96,9216]{1,0:T(8,128)(2,1)}, bf16[96,9216]{1,0:T(8,128)(2,1)}) custom-call(s32[64]{0:T(128)} %concatenate.81.refs_0_, bf16[128,1536]{1,0:T(8,128)(2,1)} %get-tuple-element.153.refs_1_, bf16[128,8448]{1,0:T(8,128)(2,1)} %get-tuple-element.151.refs_18_.refs_2_, bf16[128,8448]{1,0:T(8,128)(2,1)} %collective-permute-done.27.refs_3_), custom_call_target="tpu_custom_call" | custom-call | flops 1073741824 | bytes 16777216 | tf_op jit(solution)/shard_map/query_products/pallas_call | solution.py:177
  372.0 2.7 collective-permute-done.48
  374.7 2.4 collective-permute-start.37
  377.1 1.4 add_convert_fusion.27
  378.5 1.5 collective-permute-start.49
  380.8 2.5 add_convert_fusion.5
  383.3 6.5 %collective-permute-done.49 = bf16[384,384]{1,0:T(8,128)(2,1)S(1)} collective-permute-done((bf16[384,384]{1,0:T(8,128)(2,1)S(1)}, bf16[384,384]{1,0:T(8,128)(2,1)S(1)}, u32[]{:S(2)}, u32[]{:S(2)}) %collective-permute-start.49) | collective-permute-done | bytes 294944 | tf_op jit(solution)/shard_map/ppermute | solution.py:26
  390.0 6.2 %collective-permute-done.42 = bf16[96,1536]{1,0:T(8,128)(2,1)S(1)} collective-permute-done((bf16[96,1536]{1,0:T(8,128)(2,1)S(1)}, bf16[96,1536]{1,0:T(8,128)(2,1)S(1)}, u32[]{:S(2)}, u32[]{:S(2)}) %collective-permute-start.42) | collective-permute-done | bytes 294944 | tf_op jit(solution)/shard_map/ppermute | solution.py:26
  397.4 2.5 collective-permute-start.28
  399.9 22.3 %collective-permute-done.50 = bf16[192,384]{1,0:T(8,128)(2,1)S(1)} collective-permute-done((bf16[192,384]{1,0:T(8,128)(2,1)S(1)}, bf16[192,384]{1,0:T(8,128)(2,1)S(1)}, u32[]{:S(2)}, u32[]{:S(2)}) %collective-permute-start.50) | collective-permute-done | bytes 147488 | tf_op jit(solution)/shard_map/ppermute | solution.py:26
  422.2 3.4 collective-permute-start.43
  425.8 36.2 %collective-permute-done.43 = bf16[48,1536]{1,0:T(8,128)(2,1)S(1)} collective-permute-done((bf16[48,1536]{1,0:T(8,128)(2,1)S(1)}, bf16[48,1536]{1,0:T(8,128)(2,1)S(1)}, u32[]{:S(2)}, u32[]{:S(2)}) %collective-permute-start.43) | collective-permute-done | bytes 147488 | tf_op jit(solution)/shard_map/ppermute | solution.py:26
  463.9 14.3 %collective-permute-done.32 = bf16[192,1536]{1,0:T(8,128)(2,1)S(1)} collective-permute-done((bf16[192,1536]{1,0:T(8,128)(2,1)S(1)}, bf16[192,1536]{1,0:T(8,128)(2,1)S(1)}, u32[]{:S(2)}, u32[]{:S(2)}) %collective-permute-start.32) | collective-permute-done | bytes 589856 | tf_op jit(solution)/shard_map/ppermute | solution.py:26
  479.2 3.4 collective-permute-start.29
  482.6 4.4 collective-permute-done.33
  487.1 3.4 collective-permute-start.34
  490.8 36.4 %collective-permute-done.34 = bf16[48,1536]{1,0:T(8,128)(2,1)S(1)} collective-permute-done((bf16[48,1536]{1,0:T(8,128)(2,1)S(1)}, bf16[48,1536]{1,0:T(8,128)(2,1)S(1)}, u32[]{:S(2)}, u32[]{:S(2)}) %collective-permute-start.34) | collective-permute-done | bytes 147488 | tf_op jit(solution)/shard_map/ppermute | solution.py:26
  (331 shorter events, 61.7 us)
Async XLA Ops:
  0.6 72.1 %copy-start = (s32[32]{0:T(128)S(1)}, s32[32]{0:T(128)}, u32[]{:S(2)}) copy-start(s32[32]{0:T(128)} %param.24) | copy-start | bytes 388
  5.9 32.1 %collective-permute-start.3 = (bf16[768,3072]{1,0:T(8,128)(2,1)}, bf16[768,3072]{1,0:T(8,128)(2,1)}, u32[]{:S(2)}, u32[]{:S(2)}) collective-permute-start(bf16[768,3072]{1,0:T(8,128)(2,1)} %slice_bitcast_fusion.1), channel_id=1, source_target_pairs={{0,16},{16,0},{1,17},{17,1},{2,18},{18,2},{3,19},{19,3},{4,20},{20... | collective-permute-start | bytes 14155784 | tf_op jit(solution)/shard_map/ppermute | solution.py:21
  10.2 27.8 %collective-permute-start.4 = (bf16[3072,768]{1,0:T(8,128)(2,1)}, bf16[3072,768]{1,0:T(8,128)(2,1)}, u32[]{:S(2)}, u32[]{:S(2)}) collective-permute-start(bf16[3072,768]{1,0:T(8,128)(2,1)} %slice_bitcast_fusion), channel_id=1, source_target_pairs={{0,16},{16,0},{1,17},{17,1},{2,18},{18,2},{3,19},{19,3},{4,20},{20... | collective-permute-start | bytes 14155784 | tf_op jit(solution)/shard_map/ppermute | solution.py:21
  14.3 23.7 %collective-permute-start.1 = (bf16[768,2304]{1,0:T(8,128)(2,1)}, bf16[768,2304]{1,0:T(8,128)(2,1)}, u32[]{:S(2)}, u32[]{:S(2)}) collective-permute-start(bf16[768,2304]{1,0:T(8,128)(2,1)} %slice_bitcast_fusion.2), channel_id=1, source_target_pairs={{0,16},{16,0},{1,17},{17,1},{2,18},{18,2},{3,19},{19,3},{4,20},{20... | collective-permute-start | bytes 10616840 | tf_op jit(solution)/shard_map/ppermute | solution.py:21
  25.5 1.6 collective-permute-start
  25.7 12.2 %collective-permute-start.2 = (bf16[768,768]{1,0:T(8,128)(2,1)S(1)}, bf16[768,768]{1,0:T(8,128)(2,1)S(1)}, u32[]{:S(2)}, u32[]{:S(2)}) collective-permute-start(bf16[768,768]{1,0:T(8,128)(2,1)S(1)} %slice_bitcast_fusion.3), channel_id=1, source_target_pairs={{0,16},{16,0},{1,17},{17,1},{2,18},{18,2},{3,19},{19,3},{4,20},{20... | collective-permute-start | bytes 3538952 | tf_op jit(solution)/shard_map/ppermute | solution.py:21
  27.1 10.8 %collective-permute-start.5 = (f32[12,768]{1,0:T(8,128)S(1)}, f32[12,768]{1,0:T(8,128)S(1)}, u32[]{:S(2)}, u32[]{:S(2)}) collective-permute-start(f32[12,768]{1,0:T(8,128)S(1)} %pad_maximum_fusion.3), channel_id=1, source_target_pairs={{0,16},{16,0},{1,17},{17,1},{2,18},{18,2},{3,19},{19,3},{4,20},{20... | collective-permute-start | bytes 110600 | tf_op jit(solution)/shard_map/ppermute | solution.py:21
  72.5 1.6 collective-permute-start.7
  74.2 5.5 %collective-permute-start.10 = (bf16[8,768]{1,0:T(8,128)(2,1)S(1)}, bf16[8,768]{1,0:T(8,128)(2,1)S(1)}, u32[]{:S(2)}, u32[]{:S(2)}) collective-permute-start(bf16[8,768]{1,0:T(8,128)(2,1)S(1)} %pad_maximum_fusion.6), channel_id=1, source_target_pairs={{0,3},{1,2},{2,1},{3,0},{4,7},{5,6},{6,5},{7,4},{8,11},{9,10},{10,... | collective-permute-start | bytes 36872 | tf_op jit(solution)/shard_map/ppermute | solution.py:26
  78.1 3.7 collective-permute-start.8
  78.6 3.7 collective-permute-start.9
  82.3 4.8 collective-permute-start.11
  84.0 6.0 %collective-permute-start.12 = (bf16[32,768]{1,0:T(8,128)(2,1)S(1)}, bf16[32,768]{1,0:T(8,128)(2,1)S(1)}, u32[]{:S(2)}, u32[]{:S(2)}) collective-permute-start(bf16[32,768]{1,0:T(8,128)(2,1)S(1)} %concatenate.86), channel_id=1, source_target_pairs={{0,8},{1,9},{2,10},{3,11},{4,12},{5,13},{6,14},{7,15},{8,0},{9,1},... | collective-permute-start | bytes 147464 | tf_op jit(solution)/shard_map/ppermute | solution.py:26
  86.6 5.9 %collective-permute-start.13 = (bf16[32,768]{1,0:T(8,128)(2,1)S(1)}, bf16[32,768]{1,0:T(8,128)(2,1)S(1)}, u32[]{:S(2)}, u32[]{:S(2)}) collective-permute-start(bf16[32,768]{1,0:T(8,128)(2,1)S(1)} %concatenate.86), channel_id=1, source_target_pairs={{0,12},{1,13},{2,14},{3,15},{4,8},{5,9},{6,10},{7,11},{8,4},{9,5},... | collective-permute-start | bytes 147464 | tf_op jit(solution)/shard_map/ppermute | solution.py:26
  114.7 10.9 %collective-permute-start.15 = (bf16[768,1536]{1,0:T(8,128)(2,1)}, bf16[768,1536]{1,0:T(8,128)(2,1)S(1)}, u32[]{:S(2)}, u32[]{:S(2)}) collective-permute-start(bf16[768,1536]{1,0:T(8,128)(2,1)} %get-tuple-element.114), channel_id=1, source_target_pairs={{0,16},{16,0},{1,17},{17,1},{2,18},{18,2},{3,19},{19,3},{4,20},{20... | collective-permute-start | bytes 7077896 | tf_op jit(solution)/shard_map/ppermute | solution.py:21
  114.8 15.4 %collective-permute-start.14 = (bf16[3072,384]{1,0:T(8,128)(2,1)}, bf16[3072,384]{1,0:T(8,128)(2,1)}, u32[]{:S(2)}, u32[]{:S(2)}) collective-permute-start(bf16[3072,384]{1,0:T(8,128)(2,1)} %get-tuple-element.112), channel_id=1, source_target_pairs={{0,16},{16,0},{1,17},{17,1},{2,18},{18,2},{3,19},{19,3},{4,20},{20... | collective-permute-start | bytes 7077896 | tf_op jit(solution)/shard_map/ppermute | solution.py:21
  129.6 34.0 %collective-permute-start.18 = (bf16[384,1536]{1,0:T(8,128)(2,1)S(1)}, bf16[384,1536]{1,0:T(8,128)(2,1)}, u32[]{:S(2)}, u32[]{:S(2)}) collective-permute-start(bf16[384,1536]{1,0:T(8,128)(2,1)S(1)} %get-tuple-element.181.refs_13_), channel_id=1, source_target_pairs={{0,2},{1,3},{2,0},{3,1},{4,6},{5,7},{6,4},{7,5},{8,10},{9,11},{10,... | collective-permute-start | bytes 3538952 | tf_op jit(solution)/shard_map/ppermute | solution.py:26
  132.6 33.7 %collective-permute-start.17 = (bf16[1536,384]{1,0:T(8,128)(2,1)S(1)}, bf16[1536,384]{1,0:T(8,128)(2,1)}, u32[]{:S(2)}, u32[]{:S(2)}) collective-permute-start(bf16[1536,384]{1,0:T(8,128)(2,1)S(1)} %get-tuple-element.183.refs_12_), channel_id=1, source_target_pairs={{0,1},{1,0},{2,3},{3,2},{4,5},{5,4},{6,7},{7,6},{8,9},{9,8},{10,11... | collective-permute-start | bytes 3538952 | tf_op jit(solution)/shard_map/ppermute | solution.py:26
  161.6 23.3 %collective-permute-start.19 = (bf16[768,1536]{1,0:T(8,128)(2,1)}, bf16[768,1536]{1,0:T(8,128)(2,1)}, u32[]{:S(2)}, u32[]{:S(2)}) collective-permute-start(bf16[768,1536]{1,0:T(8,128)(2,1)} %get-tuple-element.130), channel_id=1, source_target_pairs={{0,16},{16,0},{1,17},{17,1},{2,18},{18,2},{3,19},{19,3},{4,20},{20... | collective-permute-start | bytes 7077896 | tf_op jit(solution)/shard_map/ppermute | solution.py:21
  162.6 105.9 %collective-permute-start.6 = (bf16[384,768]{1,0:T(8,128)(2,1)}, bf16[384,768]{1,0:T(8,128)(2,1)}, u32[]{:S(2)}, u32[]{:S(2)}) collective-permute-start(bf16[384,768]{1,0:T(8,128)(2,1)} %broadcast_select_fusion.2), channel_id=1, source_target_pairs={{0,16},{16,0},{1,17},{17,1},{2,18},{18,2},{3,19},{19,3},{4,20},{20... | collective-permute-start | bytes 1769480 | tf_op jit(solution)/shard_map/ppermute | solution.py:21
  163.6 5.9 %collective-permute-start.16 = (bf16[64,768]{1,0:T(8,128)(2,1)S(1)}, bf16[64,768]{1,0:T(8,128)(2,1)S(1)}, u32[]{:S(2)}, u32[]{:S(2)}) collective-permute-start(bf16[64,768]{1,0:T(8,128)(2,1)S(1)} %copy-done.45), channel_id=1, source_target_pairs={{0,16},{16,0},{1,17},{17,1},{2,18},{18,2},{3,19},{19,3},{4,20},{20... | collective-permute-start | bytes 294920 | tf_op jit(solution)/shard_map/ppermute | solution.py:21
  165.3 15.9 %collective-permute-start.21 = (bf16[192,1536]{1,0:T(8,128)(2,1)S(1)}, bf16[192,1536]{1,0:T(8,128)(2,1)}, u32[]{:S(2)}, u32[]{:S(2)}) collective-permute-start(bf16[192,1536]{1,0:T(8,128)(2,1)S(1)} %get-tuple-element.195.refs_13_), channel_id=1, source_target_pairs={{0,1},{1,0},{2,3},{3,2},{4,5},{5,4},{6,7},{7,6},{8,9},{9,8},{10,11... | collective-permute-start | bytes 1769480 | tf_op jit(solution)/shard_map/ppermute | solution.py:26
  167.9 15.5 %collective-permute-start.20 = (bf16[768,384]{1,0:T(8,128)(2,1)S(1)}, bf16[768,384]{1,0:T(8,128)(2,1)S(1)}, u32[]{:S(2)}, u32[]{:S(2)}) collective-permute-start(bf16[768,384]{1,0:T(8,128)(2,1)S(1)} %get-tuple-element.197.refs_12_), channel_id=1, source_target_pairs={{0,2},{1,3},{2,0},{3,1},{4,6},{5,7},{6,4},{7,5},{8,10},{9,11},{10,... | collective-permute-start | bytes 1769480 | tf_op jit(solution)/shard_map/ppermute | solution.py:26
  182.5 10.0 %collective-permute-start.24 = (bf16[96,1536]{1,0:T(8,128)(2,1)S(1)}, bf16[96,1536]{1,0:T(8,128)(2,1)S(1)}, u32[]{:S(2)}, u32[]{:S(2)}) collective-permute-start(bf16[96,1536]{1,0:T(8,128)(2,1)S(1)} %get-tuple-element.220.refs_16_), channel_id=1, source_target_pairs={{0,4},{1,5},{2,6},{3,7},{4,0},{5,1},{6,2},{7,3},{8,12},{9,13},{10,... | collective-permute-start | bytes 884744 | tf_op jit(solution)/shard_map/ppermute | solution.py:26
  183.6 15.2 %collective-permute-start.23 = (bf16[384,384]{1,0:T(8,128)(2,1)S(1)}, bf16[384,384]{1,0:T(8,128)(2,1)S(1)}, u32[]{:S(2)}, u32[]{:S(2)}) collective-permute-start(bf16[384,384]{1,0:T(8,128)(2,1)S(1)} %get-tuple-element.222.refs_15_), channel_id=1, source_target_pairs={{0,4},{1,5},{2,6},{3,7},{4,0},{5,1},{6,2},{7,3},{8,12},{9,13},{10,... | collective-permute-start | bytes 884744 | tf_op jit(solution)/shard_map/ppermute | solution.py:26
  187.3 47.5 %collective-permute-start.22 = (bf16[384,1536]{1,0:T(8,128)(2,1)S(1)}, bf16[384,1536]{1,0:T(8,128)(2,1)}, u32[]{:S(2)}, u32[]{:S(2)}) collective-permute-start(bf16[384,1536]{1,0:T(8,128)(2,1)S(1)} %get-tuple-element.179.refs_12_), channel_id=1, source_target_pairs={{0,4},{1,5},{2,6},{3,7},{4,0},{5,1},{6,2},{7,3},{8,12},{9,13},{10,... | collective-permute-start | bytes 3538952 | tf_op jit(solution)/shard_map/ppermute | solution.py:26
  212.3 26.7 %collective-permute-start.25 = (bf16[64,9600]{1,0:T(8,128)(2,1)}, bf16[64,9600]{1,0:T(8,128)(2,1)S(1)}, u32[]{:S(2)}, u32[]{:S(2)}) collective-permute-start(bf16[64,9600]{1,0:T(8,128)(2,1)} %get-tuple-element.145.refs_17_.refs_2_), channel_id=1, source_target_pairs={{0,1},{1,0},{2,3},{3,2},{4,5},{5,4},{6,7},{7,6},{8,9},{9,8},{10,11... | collective-permute-start | bytes 3686408 | tf_op jit(solution)/shard_map/ppermute | solution.py:26
  265.5 1.3 collective-permute-start.53
  267.5 4.0 collective-permute-start.54
  271.6 3.8 collective-permute-start.55
  274.3 11.0 %collective-permute-start.46 = (bf16[3072,384]{1,0:T(8,128)(2,1)}, bf16[3072,384]{1,0:T(8,128)(2,1)}, u32[]{:S(2)}, u32[]{:S(2)}) collective-permute-start(bf16[3072,384]{1,0:T(8,128)(2,1)} %get-tuple-element.161), channel_id=1, source_target_pairs={{0,16},{16,0},{1,17},{17,1},{2,18},{18,2},{3,19},{19,3},{4,20},{20... | collective-permute-start | bytes 7077896 | tf_op jit(solution)/shard_map/ppermute | solution.py:21
  274.3 15.3 %collective-permute-start.39 = (bf16[768,1536]{1,0:T(8,128)(2,1)}, bf16[768,1536]{1,0:T(8,128)(2,1)}, u32[]{:S(2)}, u32[]{:S(2)}) collective-permute-start(bf16[768,1536]{1,0:T(8,128)(2,1)} %get-tuple-element.159), channel_id=1, source_target_pairs={{0,16},{16,0},{1,17},{17,1},{2,18},{18,2},{3,19},{19,3},{4,20},{20... | collective-permute-start | bytes 7077896 | tf_op jit(solution)/shard_map/ppermute | solution.py:21
  275.4 3.8 collective-permute-start.56
  276.8 16.4 %collective-permute-start.35 = (bf16[192,1536]{1,0:T(8,128)(2,1)}, bf16[192,1536]{1,0:T(8,128)(2,1)}, u32[]{:S(2)}, u32[]{:S(2)}) collective-permute-start(bf16[192,1536]{1,0:T(8,128)(2,1)} %get-tuple-element.191.refs_15_), channel_id=1, source_target_pairs={{0,1},{1,0},{2,3},{3,2},{4,5},{5,4},{6,7},{7,6},{8,9},{9,8},{10,11... | collective-permute-start | bytes 1769480 | tf_op jit(solution)/shard_map/ppermute | solution.py:26
  277.8 85.7 %collective-permute-start.27 = (bf16[128,8448]{1,0:T(8,128)(2,1)S(1)}, bf16[128,8448]{1,0:T(8,128)(2,1)}, u32[]{:S(2)}, u32[]{:S(2)}) collective-permute-start(bf16[128,8448]{1,0:T(8,128)(2,1)S(1)} %copy-done.10), channel_id=1, source_target_pairs={{0,2},{1,3},{2,0},{3,1},{4,6},{5,7},{6,4},{7,5},{8,10},{9,11},{10,... | collective-permute-start | bytes 6488072 | tf_op jit(solution)/shard_map/ppermute | solution.py:26
  279.3 4.6 collective-permute-start.57
  283.9 96.2 %collective-permute-start.30 = (bf16[768,1536]{1,0:T(8,128)(2,1)}, bf16[768,1536]{1,0:T(8,128)(2,1)}, u32[]{:S(2)}, u32[]{:S(2)}) collective-permute-start(bf16[768,1536]{1,0:T(8,128)(2,1)} %get-tuple-element.157), channel_id=1, source_target_pairs={{0,16},{16,0},{1,17},{17,1},{2,18},{18,2},{3,19},{19,3},{4,20},{20... | collective-permute-start | bytes 7077896 | tf_op jit(solution)/shard_map/ppermute | solution.py:21
  288.4 68.8 %collective-permute-start.47 = (bf16[1536,384]{1,0:T(8,128)(2,1)S(1)}, bf16[1536,384]{1,0:T(8,128)(2,1)S(1)}, u32[]{:S(2)}, u32[]{:S(2)}) collective-permute-start(bf16[1536,384]{1,0:T(8,128)(2,1)S(1)} %get-tuple-element.173), channel_id=1, source_target_pairs={{0,1},{1,0},{2,3},{3,2},{4,5},{5,4},{6,7},{7,6},{8,9},{9,8},{10,11... | collective-permute-start | bytes 3538952 | tf_op jit(solution)/shard_map/ppermute | solution.py:26
  291.9 65.2 %copy-start.34 = (f32[384,768]{1,0:T(8,128)S(1)}, f32[384,768]{1,0:T(8,128)}, u32[]{:S(2)}) copy-start(f32[384,768]{1,0:T(8,128)} %convert_select_fusion) | copy-start | bytes 3538948
  291.9 65.3 %copy-start.43 = (bf16[192,384]{1,0:T(8,128)(2,1)S(1)}, bf16[192,384]{1,0:T(8,128)(2,1)}, u32[]{:S(2)}) copy-start(bf16[192,384]{1,0:T(8,128)(2,1)} %add_convert_fusion.49.refs_16_) | copy-start | bytes 442372
  291.9 67.0 %collective-permute-start.40 = (bf16[384,1536]{1,0:T(8,128)(2,1)S(1)}, bf16[384,1536]{1,0:T(8,128)(2,1)S(1)}, u32[]{:S(2)}, u32[]{:S(2)}) collective-permute-start(bf16[384,1536]{1,0:T(8,128)(2,1)S(1)} %get-tuple-element.175), channel_id=1, source_target_pairs={{0,2},{1,3},{2,0},{3,1},{4,6},{5,7},{6,4},{7,5},{8,10},{9,11},{10,... | collective-permute-start | bytes 3538952 | tf_op jit(solution)/shard_map/ppermute | solution.py:26
  294.5 62.6 %collective-permute-start.36 = (bf16[96,1536]{1,0:T(8,128)(2,1)S(1)}, bf16[96,1536]{1,0:T(8,128)(2,1)S(1)}, u32[]{:S(2)}, u32[]{:S(2)}) collective-permute-start(bf16[96,1536]{1,0:T(8,128)(2,1)S(1)} %get-tuple-element.216), channel_id=1, source_target_pairs={{0,2},{1,3},{2,0},{3,1},{4,6},{5,7},{6,4},{7,5},{8,10},{9,11},{10,... | collective-permute-start | bytes 884744 | tf_op jit(solution)/shard_map/ppermute | solution.py:26
  295.3 63.6 %copy-start.59 = (f32[2,6,48]{2,0,1:T(2,128)}, f32[2,6,48]{2,0,1:T(2,128)S(1)}, u32[]{:S(2)}) copy-start(f32[2,6,48]{2,0,1:T(2,128)S(1)} %constant_dynamic-update-slice_fusion.4) | copy-start | bytes 6916
  357.1 3.4 collective-permute-start.26
  357.2 40.2 %collective-permute-start.51 = (bf16[192,384]{1,0:T(8,128)(2,1)S(1)}, bf16[192,384]{1,0:T(8,128)(2,1)S(1)}, u32[]{:S(2)}, u32[]{:S(2)}) collective-permute-start(bf16[192,384]{1,0:T(8,128)(2,1)S(1)} %copy-done.43), channel_id=1, source_target_pairs={{0,8},{1,9},{2,10},{3,11},{4,12},{5,13},{6,14},{7,15},{8,0},{9,1},... | collective-permute-start | bytes 442376 | tf_op jit(solution)/shard_map/ppermute | solution.py:26
  358.9 15.8 %collective-permute-start.48 = (bf16[768,384]{1,0:T(8,128)(2,1)}, bf16[768,384]{1,0:T(8,128)(2,1)}, u32[]{:S(2)}, u32[]{:S(2)}) collective-permute-start(bf16[768,384]{1,0:T(8,128)(2,1)} %get-tuple-element.187), channel_id=1, source_target_pairs={{0,2},{1,3},{2,0},{3,1},{4,6},{5,7},{6,4},{7,5},{8,10},{9,11},{10,... | collective-permute-start | bytes 1769480 | tf_op jit(solution)/shard_map/ppermute | solution.py:26
  360.5 17.9 %collective-permute-start.41 = (bf16[192,1536]{1,0:T(8,128)(2,1)}, bf16[192,1536]{1,0:T(8,128)(2,1)S(1)}, u32[]{:S(2)}, u32[]{:S(2)}) collective-permute-start(bf16[192,1536]{1,0:T(8,128)(2,1)} %get-tuple-element.189), channel_id=1, source_target_pairs={{0,1},{1,0},{2,3},{3,2},{4,5},{5,4},{6,7},{7,6},{8,9},{9,8},{10,11... | collective-permute-start | bytes 1769480 | tf_op jit(solution)/shard_map/ppermute | solution.py:26
  363.5 62.2 %collective-permute-start.44 = (bf16[48,1536]{1,0:T(8,128)(2,1)S(1)}, bf16[48,1536]{1,0:T(8,128)(2,1)S(1)}, u32[]{:S(2)}, u32[]{:S(2)}) collective-permute-start(bf16[48,1536]{1,0:T(8,128)(2,1)S(1)} %copy-done.42), channel_id=1, source_target_pairs={{0,8},{1,9},{2,10},{3,11},{4,12},{5,13},{6,14},{7,15},{8,0},{9,1},... | collective-permute-start | bytes 442376 | tf_op jit(solution)/shard_map/ppermute | solution.py:26
  374.7 116.1 %collective-permute-start.37 = (bf16[48,1536]{1,0:T(8,128)(2,1)S(1)}, bf16[48,1536]{1,0:T(8,128)(2,1)S(1)}, u32[]{:S(2)}, u32[]{:S(2)}) collective-permute-start(bf16[48,1536]{1,0:T(8,128)(2,1)S(1)} %add_convert_fusion.44), channel_id=1, source_target_pairs={{0,8},{1,9},{2,10},{3,11},{4,12},{5,13},{6,14},{7,15},{8,0},{9,1},... | collective-permute-start | bytes 442376 | tf_op jit(solution)/shard_map/ppermute | solution.py:26
  378.5 11.4 %collective-permute-start.49 = (bf16[384,384]{1,0:T(8,128)(2,1)S(1)}, bf16[384,384]{1,0:T(8,128)(2,1)S(1)}, u32[]{:S(2)}, u32[]{:S(2)}) collective-permute-start(bf16[384,384]{1,0:T(8,128)(2,1)S(1)} %get-tuple-element.212), channel_id=1, source_target_pairs={{0,4},{1,5},{2,6},{3,7},{4,0},{5,1},{6,2},{7,3},{8,12},{9,13},{10,... | collective-permute-start | bytes 884744 | tf_op jit(solution)/shard_map/ppermute | solution.py:26
  380.1 16.1 %collective-permute-start.42 = (bf16[96,1536]{1,0:T(8,128)(2,1)S(1)}, bf16[96,1536]{1,0:T(8,128)(2,1)S(1)}, u32[]{:S(2)}, u32[]{:S(2)}) collective-permute-start(bf16[96,1536]{1,0:T(8,128)(2,1)S(1)} %get-tuple-element.214), channel_id=1, source_target_pairs={{0,4},{1,5},{2,6},{3,7},{4,0},{5,1},{6,2},{7,3},{8,12},{9,13},{10,... | collective-permute-start | bytes 884744 | tf_op jit(solution)/shard_map/ppermute | solution.py:26
  383.3 78.6 %copy-start.30 = (bf16[96,1536]{1,0:T(8,128)(2,1)S(1)}, bf16[96,1536]{1,0:T(8,128)(2,1)}, u32[]{:S(2)}) copy-start(bf16[96,1536]{1,0:T(8,128)(2,1)} %copy-done.29) | copy-start | bytes 884740
  383.3 78.6 %copy-start.41 = (bf16[96,1536]{1,0:T(8,128)(2,1)S(1)}, bf16[96,1536]{1,0:T(8,128)(2,1)}, u32[]{:S(2)}) copy-start(bf16[96,1536]{1,0:T(8,128)(2,1)} %copy-done.40) | copy-start | bytes 884740
  389.9 72.3 %collective-permute-start.31 = (bf16[384,1536]{1,0:T(8,128)(2,1)S(1)}, bf16[384,1536]{1,0:T(8,128)(2,1)S(1)}, u32[]{:S(2)}, u32[]{:S(2)}) collective-permute-start(bf16[384,1536]{1,0:T(8,128)(2,1)S(1)} %get-tuple-element.177), channel_id=1, source_target_pairs={{0,4},{1,5},{2,6},{3,7},{4,0},{5,1},{6,2},{7,3},{8,12},{9,13},{10,... | collective-permute-start | bytes 3538952 | tf_op jit(solution)/shard_map/ppermute | solution.py:26
  396.2 26.0 %collective-permute-start.50 = (bf16[192,384]{1,0:T(8,128)(2,1)S(1)}, bf16[192,384]{1,0:T(8,128)(2,1)S(1)}, u32[]{:S(2)}, u32[]{:S(2)}) collective-permute-start(bf16[192,384]{1,0:T(8,128)(2,1)S(1)} %add_convert_fusion.39), channel_id=1, source_target_pairs={{0,8},{1,9},{2,10},{3,11},{4,12},{5,13},{6,14},{7,15},{8,0},{9,1},... | collective-permute-start | bytes 442376 | tf_op jit(solution)/shard_map/ppermute | solution.py:26
  397.4 81.6 %collective-permute-start.28 = (bf16[96,9216]{1,0:T(8,128)(2,1)S(1)}, bf16[96,9216]{1,0:T(8,128)(2,1)S(1)}, u32[]{:S(2)}, u32[]{:S(2)}) collective-permute-start(bf16[96,9216]{1,0:T(8,128)(2,1)S(1)} %copy-done.62), channel_id=1, source_target_pairs={{0,4},{1,5},{2,6},{3,7},{4,0},{5,1},{6,2},{7,3},{8,12},{9,13},{10,... | collective-permute-start | bytes 5308424 | tf_op jit(solution)/shard_map/ppermute | solution.py:26
  422.2 39.8 %collective-permute-start.43 = (bf16[48,1536]{1,0:T(8,128)(2,1)S(1)}, bf16[48,1536]{1,0:T(8,128)(2,1)S(1)}, u32[]{:S(2)}, u32[]{:S(2)}) collective-permute-start(bf16[48,1536]{1,0:T(8,128)(2,1)S(1)} %add_convert_fusion.42), channel_id=1, source_target_pairs={{0,8},{1,9},{2,10},{3,11},{4,12},{5,13},{6,14},{7,15},{8,0},{9,1},... | collective-permute-start | bytes 442376 | tf_op jit(solution)/shard_map/ppermute | solution.py:26
  425.7 64.9 %collective-permute-start.52 = (f32[192,384]{1,0:T(8,128)S(1)}, f32[192,384]{1,0:T(8,128)S(1)}, u32[]{:S(2)}, u32[]{:S(2)}) collective-permute-start(f32[192,384]{1,0:T(8,128)S(1)} %fusion.7), channel_id=1, source_target_pairs={{0,16},{16,0},{1,17},{17,1},{2,18},{18,2},{3,19},{19,3},{4,20},{20... | collective-permute-start | bytes 884744 | tf_op jit(solution)/shard_map/ppermute | solution.py:21
  462.1 1.6 collective-permute-start.45
  462.5 15.8 %collective-permute-start.32 = (bf16[192,1536]{1,0:T(8,128)(2,1)S(1)}, bf16[192,1536]{1,0:T(8,128)(2,1)S(1)}, u32[]{:S(2)}, u32[]{:S(2)}) collective-permute-start(bf16[192,1536]{1,0:T(8,128)(2,1)S(1)} %get-tuple-element.193), channel_id=1, source_target_pairs={{0,1},{1,0},{2,3},{3,2},{4,5},{5,4},{6,7},{7,6},{8,9},{9,8},{10,11... | collective-permute-start | bytes 1769480 | tf_op jit(solution)/shard_map/ppermute | solution.py:26
  478.4 8.7 %collective-permute-start.33 = (bf16[96,1536]{1,0:T(8,128)(2,1)S(1)}, bf16[96,1536]{1,0:T(8,128)(2,1)S(1)}, u32[]{:S(2)}, u32[]{:S(2)}) collective-permute-start(bf16[96,1536]{1,0:T(8,128)(2,1)S(1)} %get-tuple-element.218), channel_id=1, source_target_pairs={{0,2},{1,3},{2,0},{3,1},{4,6},{5,7},{6,4},{7,5},{8,10},{9,11},{10,... | collective-permute-start | bytes 884744 | tf_op jit(solution)/shard_map/ppermute | solution.py:26
  479.2 48.2 %collective-permute-start.29 = (bf16[48,9216]{1,0:T(8,128)(2,1)S(1)}, bf16[48,9216]{1,0:T(8,128)(2,1)S(1)}, u32[]{:S(2)}, u32[]{:S(2)}) collective-permute-start(bf16[48,9216]{1,0:T(8,128)(2,1)S(1)} %add_convert_fusion.12), channel_id=1, source_target_pairs={{0,8},{1,9},{2,10},{3,11},{4,12},{5,13},{6,14},{7,15},{8,0},{9,1},... | collective-permute-start | bytes 2654216 | tf_op jit(solution)/shard_map/ppermute | solution.py:26
  487.1 40.0 %collective-permute-start.34 = (bf16[48,1536]{1,0:T(8,128)(2,1)S(1)}, bf16[48,1536]{1,0:T(8,128)(2,1)S(1)}, u32[]{:S(2)}, u32[]{:S(2)}) collective-permute-start(bf16[48,1536]{1,0:T(8,128)(2,1)S(1)} %add_convert_fusion.46), channel_id=1, source_target_pairs={{0,8},{1,9},{2,10},{3,11},{4,12},{5,13},{6,14},{7,15},{8,0},{9,1},... | collective-permute-start | bytes 442376 | tf_op jit(solution)/shard_map/ppermute | solution.py:26
  527.3 2.8 collective-permute-start.38
  (57 other events, 513.6 us)
